TPU v7x, 32 devices: a whole 2x2x4 slice. The times are simulated.
32 devices in a mesh: lat: 8 (over y, x, core), lev: 4 (over z).
Axes of the slice: x: 2, y: 2, z: 4, core: 2. Of those that a mesh axis runs over, the one named last changes fastest.
Arguments:
- fourier: bfloat16 [2560, 48, 256], P('lat', 'lev'), may hold values from -6 to 6
- table: int32 [128], replicated, may hold values from 0 to 127, each once
- legendre: bfloat16 [128, 2, 129, 1280], P(('lat', 'lev')), may hold values from -0.15625 to 0.15625
Outputs:
- spectral: bfloat16 [128, 2, 48, 129], P(('lat', 'lev'))
Inputs may be any that keep to these rules, and one draw needn't show every extreme that they name: `table`: every pair index appears exactly once.
All inputs are finite; a program needn't handle non-finite values.
Results may differ from a plain program's by a relative error of at most 0.0051.
Values may be sent and summed in bfloat16 or wider, within the bound.
No kernel may reach another device: no remote copies, remote signals or barrier semaphores. Data moves between devices by JAX's collectives and lax.ppermute only.
A program may use at most 128 MiB of HBM per device.

v0:
```python
import jax
import jax.numpy as jnp
from jax import lax
from jax.sharding import PartitionSpec as P


def partner_2(array, axis, apart):
    return lax.ppermute(array, axis, [(i, i ^ 1 << apart) for i in range(lax.axis_size(axis))])


def regroup(outgoing, lat_count, lev_count):
    lat_rows, channels, width = outgoing.shape
    devices = lat_count * lev_count
    shaped = outgoing.reshape((1, lat_rows, channels, devices, width // devices))
    arrived = lax.all_to_all(shaped, ("lat", "lev"), split_axis=3, concat_axis=0, tiled=True)
    return arrived.reshape((devices, lat_rows, channels, width // devices))


def on_device(fourier, table, legendre):
    lat_count = lax.axis_size("lat")
    lev_count = lax.axis_size("lev")
    half_lat = lat_count // 2
    lat_rows, channels, wavenumbers = fourier.shape
    slot_count = legendre.shape[0]
    degree_rows = legendre.shape[2]
    columns = jnp.stack([table, wavenumbers - 1 - table], axis=1).reshape(-1)
    picked = jnp.take(fourier, columns, axis=2)
    top_bit = lat_count.bit_length() - 2
    partner = partner_2(picked, "lat", top_bit)
    mirror_sign = jnp.where(lax.axis_index("lat") < half_lat, 1.0, -1.0).astype(jnp.float32)
    merged = (partner.astype(jnp.float32) + mirror_sign * picked.astype(jnp.float32)).astype(
        jnp.bfloat16
    )
    arrived = regroup(merged, lat_count, lev_count)
    halves = arrived.reshape(2, half_lat, lev_count, lat_rows, channels, slot_count, 2)
    tables = legendre.reshape(slot_count, 2, degree_rows, half_lat, lat_rows)
    products = jnp.einsum(
        "ealbcsw,serab->selcwr", halves, tables, preferred_element_type=jnp.float32
    )
    products = products.reshape(slot_count, 2, lev_count * channels, 2, degree_rows)
    position = lax.axis_index(("lat", "lev")) * slot_count
    owned = lax.dynamic_slice_in_dim(table, position, slot_count)
    parity = jnp.arange(2, dtype=jnp.int32)
    row_counts = (wavenumbers - owned[:, None] - parity[None, :] + 1) // 2
    first_member = jnp.arange(degree_rows, dtype=jnp.int32)[None, None, :] < row_counts[:, :, None]
    spectral = jnp.where(first_member[:, :, None, :], products[:, :, :, 0], products[:, :, :, 1])
    return spectral.astype(jnp.bfloat16)


def solution(mesh):
    in_specs = (P("lat", "lev", None), P(), P(("lat", "lev"), None, None, None))
    out_specs = P(("lat", "lev"), None, None, None)
    return jax.shard_map(
        on_device, mesh=mesh, in_specs=in_specs, out_specs=out_specs, check_vma=False
    )
```

profile of v0, /device:TPU:0, one launch (start us, length us, event | category | flops | bytes accessed | tf_op | source)
XLA Modules:
  0.0 135.2 jit_solution(17563981866949817294)
XLA Ops:
  0.0 0.7 subtract_bitcast_fusion
  0.7 0.7 pad_add_fusion
  1.3 0.1 copy.25
  1.4 0.1 reshape.91
  1.6 0.1 reshape.90
  1.8 3.7 %copy.27 = bf16[320,12,256]{0,1,2:T(8,128)(2,1)S(1)} copy(bf16[320,12,256]{2,0,1:T(8,128)(2,1)} %param.3) | data formatting | bytes 3932160 | tf_op args[0]
  5.5 2.7 %gather_fusion = bf16[256,320,12]{1,2,0:T(8,128)(2,1)} fusion(bf16[320,12,256]{0,1,2:T(8,128)(2,1)S(1)} %copy.27, s32[1024]{0:T(1024)S(1)} %pad_clamp_fusion), kind=kCustom, calls=%fused_computation | custom fusion | bytes 3933184 | tf_op jit(solution)/shard_map/jit(_take)/gather | solution.py:27
  8.2 4.1 %copy.28 = bf16[256,320,12]{0,1,2:T(8,128)(2,1)S(1)} copy(bf16[256,320,12]{1,2,0:T(8,128)(2,1)} %gather_fusion) | data formatting | bytes 3932160 | tf_op jit(solution)/shard_map/jit(_take)/gather | solution.py:27
  12.3 1.4 %select_bitcast_fusion = bf16[320,12,256]{2,0,1:T(8,128)(2,1)} fusion(bf16[256,320,12]{0,1,2:T(8,128)(2,1)S(1)} %copy.28, pred[256]{0:T(512)(128)(4,1)S(1)} %compare_and_fusion), kind=kLoop, calls=%fused_computation.5 | loop fusion | flops 983040 | bytes 3932416 | tf_op jit(solution)/shard_map/jit(_take)/select_n | solution.py:27
  13.7 3.0 %collective-permute-start = (bf16[320,12,256]{2,0,1:T(8,128)(2,1)}, bf16[320,12,256]{2,0,1:T(8,128)(2,1)}, u32[]{:S(2)}, u32[]{:S(2)}) collective-permute-start(bf16[320,12,256]{2,0,1:T(8,128)(2,1)} %select_bitcast_fusion), channel_id=1, source_target_pairs={{0,16},{4,20},{8,24},{12,28},{16,0},{20,4},{24,8},{28,12},{1,17},{... | collective-permute-start | bytes 5898248 | tf_op jit(solution)/shard_map/ppermute | solution.py:8
  16.7 43.1 %collective-permute-done = bf16[320,12,256]{2,0,1:T(8,128)(2,1)} collective-permute-done((bf16[320,12,256]{2,0,1:T(8,128)(2,1)}, bf16[320,12,256]{2,0,1:T(8,128)(2,1)}, u32[]{:S(2)}, u32[]{:S(2)}) %collective-permute-start) | collective-permute-done | bytes 1966112 | tf_op jit(solution)/shard_map/ppermute | solution.py:8
  59.8 3.5 %add_convert_fusion = bf16[320,12,256]{2,0,1:T(8,128)(2,1)} fusion(bf16[320,12,256]{2,0,1:T(8,128)(2,1)} %collective-permute-done, f32[]{:T(128)S(6)} %select_n.45, bf16[256,320,12]{0,1,2:T(8,128)(2,1)S(1)} %copy.28, pred[256]{0:T(512)(128)(4,1)S(1)} %compare_and_fusion), kind=kLoop, calls=%fused_computation.1 | loop fusion | flops 5898240 | bytes 5898500 | tf_op jit(solution)/shard_map/convert_element_type | solution.py:31
  63.3 2.9 %copy.29 = bf16[320,12,256]{0,2,1:T(8,128)(2,1)S(1)} copy(bf16[320,12,256]{2,0,1:T(8,128)(2,1)} %add_convert_fusion) | data formatting | bytes 3932160 | tf_op jit(solution)/shard_map/convert_element_type | solution.py:31
  66.2 1.7 %copy.30 = bf16[1,320,12,32,8]{1,4,2,0,3:T(8,128)(2,1)} copy(bf16[1,320,12,32,8]{1,4,3,2,0:T(8,128)(2,1)S(1)} %bitcast.32) | data formatting | bytes 3932160 | tf_op jit(solution)/shard_map/reshape | solution.py:14
  67.9 6.1 %all-to-all-start = ((bf16[1,320,12,32,8]{1,4,2,0,3:T(8,128)(2,1)}), bf16[1,320,12,32,8]{1,4,2,0,3:T(8,128)(2,1)S(1)}, u32[]{:S(2)}, u32[]{:S(2)}) async-start(bf16[1,320,12,32,8]{1,4,2,0,3:T(8,128)(2,1)} %copy.30), calls=%async_computation | async-start | bytes 4718592 | tf_op jit(solution)/shard_map/all_to_all | solution.py:15
  74.0 0.0 copy-start
  74.0 9.1 %reshape.93 = bf16[4,2,129,4,320]{4,3,1,2,0:T(4,128)(2,1)} reshape(bf16[4,2,129,1280]{3,1,2,0:T(2,128)(2,1)} %param.5) | data formatting | bytes 5283840 | tf_op jit(solution)/shard_map/reshape | solution.py:36
  83.1 0.0 copy-done
  83.1 0.1 dynamic-slice_subtract_fusion
  83.2 0.1 add_select_fusion
  83.2 0.1 iota_compare_fusion
  83.3 44.0 %all-to-all-done = bf16[1,320,12,32,8]{1,4,2,0,3:T(8,128)(2,1)S(1)} async-done(((bf16[1,320,12,32,8]{1,4,2,0,3:T(8,128)(2,1)}), bf16[1,320,12,32,8]{1,4,2,0,3:T(8,128)(2,1)S(1)}, u32[]{:S(2)}, u32[]{:S(2)}) %all-to-all-start) | async-done | bytes 1966112 | tf_op jit(solution)/shard_map/all_to_all | solution.py:15
  127.3 2.4 %reshape_reshape.3 = bf16[2,4,4,320,12,4,2]{3,6,5,4,2,1,0:T(2,128)(2,1)} reshape(bf16[32,1,320,12,1,8]{2,5,3,0,4,1:T(8,128)(2,1)S(1)} %bitcast.31) | data formatting | bytes 3932160 | tf_op jit(solution)/shard_map/reshape;reshape | solution.py:35
  129.7 3.6 %fusion.3 = bf16[4,2,4,12,2,129]{5,3,4,2,1,0:T(8,128)(2,1)S(1)} fusion(bf16[4,2,129,4,320,1,1]{4,3,1,2,0,6,5:T(4,128)(2,1)} %bitcast.34, bf16[2,4,4,320,12,4,2]{3,6,5,4,2,1,0:T(2,128)(2,1)} %reshape_reshape.3), kind=kOutput, calls=%fused_computation.6 | convolution fusion | flops 253624320 | bytes 4806144 | tf_op jit(solution)/shard_map/ealbcsw,serab->selcwr/dot_general | solution.py:37
  133.4 0.3 copy.33
  133.7 0.7 fusion.13
  134.4 0.7 fusion.9
  (3 shorter events, 0.0 us)
Async XLA Ops:
  13.7 46.1 %collective-permute-start = (bf16[320,12,256]{2,0,1:T(8,128)(2,1)}, bf16[320,12,256]{2,0,1:T(8,128)(2,1)}, u32[]{:S(2)}, u32[]{:S(2)}) collective-permute-start(bf16[320,12,256]{2,0,1:T(8,128)(2,1)} %select_bitcast_fusion), channel_id=1, source_target_pairs={{0,16},{4,20},{8,24},{12,28},{16,0},{20,4},{24,8},{28,12},{1,17},{... | collective-permute-start | bytes 5898248 | tf_op jit(solution)/shard_map/ppermute | solution.py:8
  67.9 59.4 %all-to-all-start = ((bf16[1,320,12,32,8]{1,4,2,0,3:T(8,128)(2,1)}), bf16[1,320,12,32,8]{1,4,2,0,3:T(8,128)(2,1)S(1)}, u32[]{:S(2)}, u32[]{:S(2)}) async-start(bf16[1,320,12,32,8]{1,4,2,0,3:T(8,128)(2,1)} %copy.30), calls=%async_computation | async-start | bytes 4718592 | tf_op jit(solution)/shard_map/all_to_all | solution.py:15
  74.0 9.1 %copy-start = (s32[128]{0:T(128)S(1)}, s32[128]{0:T(128)}, u32[]{:S(2)}) copy-start(s32[128]{0:T(128)} %param.4) | copy-start | bytes 1540
where the time goes:
time: 136 us; the launch traced here: 135 us
  waiting for transfers between devices  87.1 us (64%)
  local copies, waits for them, and re-layouts  28 us (21%)
  starting transfers between devices  9.04 us (7%)
  other arithmetic  7.24 us (5%)
  matrix products  3.64 us (3%)
    all_to_all x1, waiting for transfers between devices, regroup(): lax.all_to_all(shaped, ('lat', 'lev'), split_axis=3, concat_axis=0, tiled...  44 us
    ppermute x1, waiting for transfers between devices, partner_2(): lax.ppermute(array, axis, [(i, i ^ 1 << apart) for i in range(lax.axis_si...  43.1 us
    reshape x1, local copies, waits for them, and re-layouts, on_device(): tables = legendre.reshape(slot_count, 2, degree_rows, half_lat, lat_rows)  9.07 us
    gather x2, local copies, waits for them, and re-layouts, on_device(): picked = jnp.take(fourier, columns, axis=2)  6.75 us
    all_to_all x1, starting transfers between devices, regroup(): lax.all_to_all(shaped, ('lat', 'lev'), split_axis=3, concat_axis=0, tiled...  6.07 us
    unnamed x3, local copies, waits for them, and re-layouts  3.75 us
    dot_general x1, matrix products, on_device(): jnp.einsum('ealbcsw,serab->selcwr', halves, tables, preferred_element_typ...  3.64 us
    convert_element_type x1, other arithmetic, on_device(): (partner.astype(jnp.float32) + mirror_sign * picked.astype(jnp.float32))....  3.5 us
  transfers between devices with their start and end apart: 2, of which 2 were waited for; matrix products, arithmetic and copies ran while one was open for 7% of the time, Pallas kernels for 0%

commit v1 on v0

v1 whole, which is shorter than its diff:
```python
import functools

import jax
import jax.numpy as jnp
from jax import lax
from jax.experimental import pallas as pl
from jax.experimental.pallas import tpu as pltpu
from jax.sharding import PartitionSpec as P

NT = (((1,), (1,)), ((), ()))


def pick_kernel(table_ref, x_ref, out_ref, onehot):
    rows, width = onehot.shape

    @pl.when(pl.program_id(0) == 0)
    def _():
        pairs = table_ref.shape[1]
        row = lax.broadcasted_iota(jnp.int32, (rows, pairs), 0)
        lane = lax.broadcasted_iota(jnp.int32, (rows, pairs), 1)
        mine = jnp.where(lane == row // 2, table_ref[...], 0)
        pair = jnp.sum(mine, axis=1, keepdims=True)
        second = lax.broadcasted_iota(jnp.int32, (rows, 1), 0) % 2 == 1
        column = jnp.where(second, width - 1 - pair, pair)
        at = lax.broadcasted_iota(jnp.int32, (rows, width), 1)
        onehot[...] = jnp.where(at == column, 1.0, 0.0).astype(jnp.bfloat16)

    picked = lax.dot_general(onehot[...], x_ref[...], NT, preferred_element_type=jnp.float32)
    out_ref[...] = picked.astype(jnp.bfloat16).reshape(out_ref.shape)


def pick(table, x, devices, steps):
    length, width = x.shape
    block = length // steps
    per = width // devices
    return pl.pallas_call(
        pick_kernel,
        grid=(steps,),
        in_specs=[
            pl.BlockSpec((1, table.shape[0]), lambda i: (0, 0)),
            pl.BlockSpec((block, width), lambda i: (i, 0)),
        ],
        out_specs=pl.BlockSpec((devices, per, block), lambda i: (0, 0, i)),
        out_shape=jax.ShapeDtypeStruct((devices, per, length), jnp.bfloat16),
        scratch_shapes=[pltpu.VMEM((width, width), jnp.bfloat16)],
        compiler_params=pltpu.CompilerParams(vmem_limit_bytes=40 * 2**20),
    )(table.reshape(1, -1), x)


def transform_kernel(first_ref, arrived_ref, tables_ref, out_ref, held, total, *, lat_rows):
    channels = arrived_ref.shape[3] // lat_rows
    both = 2 * lat_rows
    for x in range(2):
        for lev in range(4):
            for c in range(0, channels, 2):
                at = (lev * channels + c) * 8
                for core in range(2):
                    sym, anti = [], []
                    for k in (c, c + 1):
                        lanes = pl.ds(k * lat_rows, lat_rows)
                        north = arrived_ref[2 * x + core, lev, :, lanes].astype(jnp.float32)
                        south = arrived_ref[4 + 2 * x + core, lev, :, lanes].astype(jnp.float32)
                        sym.append(north + south)
                        anti.append(north - south)
                    lanes = pl.ds(x * both + core * lat_rows, lat_rows)
                    held[0, at : at + 16, lanes] = jnp.concatenate(sym, 0).astype(jnp.bfloat16)
                    held[1, at : at + 16, lanes] = jnp.concatenate(anti, 0).astype(jnp.bfloat16)
    for s in range(4):
        for e in range(2):
            products = lax.dot_general(
                held[e], tables_ref[s, e], NT, preferred_element_type=jnp.float32
            )
            for at in range(0, products.shape[1], 128):
                width = min(128, products.shape[1] - at)
                total[at // 128, :, :width] = products[:, at : at + width]
                one = total[at // 128, pl.ds(2 * s, 4 * channels, stride=8), :]
                two = total[at // 128, pl.ds(2 * s + 1, 4 * channels, stride=8), :]
                degree = lax.broadcasted_iota(jnp.int32, one.shape, 1) + at
                chosen = jnp.where(degree < first_ref[s, e], one, two).astype(jnp.bfloat16)
                out_ref[s, e, :, at : at + width] = chosen[:, :width]


def transform(first, arrived, tables):
    _, levs, _, length = arrived.shape
    slots, _, degrees, lats = tables.shape
    lat_rows = lats // 4
    channels = length // lat_rows * levs
    vmem = pl.BlockSpec(memory_space=pltpu.VMEM)
    return pl.pallas_call(
        functools.partial(transform_kernel, lat_rows=lat_rows),
        in_specs=[pl.BlockSpec(memory_space=pltpu.SMEM), vmem, vmem],
        out_specs=vmem,
        out_shape=jax.ShapeDtypeStruct((slots, 2, channels, degrees), jnp.bfloat16),
        scratch_shapes=[
            pltpu.VMEM((2, channels * 8, lats), jnp.bfloat16),
            pltpu.VMEM((pl.cdiv(degrees, 128), channels * 8, 128), jnp.float32),
        ],
        compiler_params=pltpu.CompilerParams(vmem_limit_bytes=40 * 2**20),
    )(first, arrived, tables)


def row_counts(table, slot_count, wavenumbers):
    position = lax.axis_index(("lat", "lev")) * slot_count
    owned = lax.dynamic_slice_in_dim(table, position, slot_count)
    parity = jnp.arange(2, dtype=jnp.int32)
    return (wavenumbers - owned[:, None] - parity[None, :] + 1) // 2


def on_block(fourier, table, legendre):
    lat_count, lev_count = lax.axis_size("lat"), lax.axis_size("lev")
    lat_rows, channels, wavenumbers = fourier.shape
    x = fourier.transpose(1, 0, 2).reshape(channels * lat_rows, wavenumbers)
    outgoing = pick(table, x, lat_count * lev_count, 3)
    arrived = lax.all_to_all(outgoing, ("lat", "lev"), split_axis=0, concat_axis=0, tiled=True)
    arrived = arrived.reshape((lat_count, lev_count) + arrived.shape[1:])
    first = row_counts(table, legendre.shape[0], wavenumbers)
    return transform(first, arrived, legendre)


def on_any(fourier, table, legendre):
    lat_count, lev_count = lax.axis_size("lat"), lax.axis_size("lev")
    devices, half_lat = lat_count * lev_count, lat_count // 2
    lat_rows, channels, wavenumbers = fourier.shape
    slot_count, _, degree_rows, _ = legendre.shape
    columns = jnp.stack([table, wavenumbers - 1 - table], axis=1).reshape(-1)
    picked = jnp.take(fourier, columns, axis=2)
    shaped = picked.reshape((1, lat_rows, channels, devices, wavenumbers // devices))
    arrived = lax.all_to_all(shaped, ("lat", "lev"), split_axis=3, concat_axis=0, tiled=True)
    halves = arrived.reshape(2, half_lat, lev_count, lat_rows, channels, slot_count, 2)
    north, south = halves[0].astype(jnp.float32), halves[1].astype(jnp.float32)
    merged = jnp.stack([north + south, north - south]).astype(jnp.bfloat16)
    tables = legendre.reshape(slot_count, 2, degree_rows, half_lat, lat_rows)
    products = jnp.einsum(
        "ealbcsw,serab->selcwr", merged, tables, preferred_element_type=jnp.float32
    )
    products = products.reshape(slot_count, 2, lev_count * channels, 2, degree_rows)
    first = row_counts(table, slot_count, wavenumbers)
    in_first = jnp.arange(degree_rows, dtype=jnp.int32)[None, None, :] < first[:, :, None]
    spectral = jnp.where(in_first[:, :, None, :], products[:, :, :, 0], products[:, :, :, 1])
    return spectral.astype(jnp.bfloat16)


def solution(mesh):
    in_specs = (P("lat", "lev", None), P(), P(("lat", "lev"), None, None, None))
    out_specs = P(("lat", "lev"), None, None, None)
    on_device = on_block if dict(mesh.shape) == {"lat": 8, "lev": 4} else on_any
    return jax.shard_map(
        on_device, mesh=mesh, in_specs=in_specs, out_specs=out_specs, check_vma=False
    )
```

time: 136 us -> 63 us (0.46)
  waiting for transfers between devices: 87.1 us -> 42.2 us
  local copies, waits for them, and re-layouts: 28 us -> 4.3 us
  Pallas kernels: 0 us -> 7.76 us
  other arithmetic: 7.24 us -> 0.16 us
  matrix products: 3.64 us -> 0 us
  starting transfers between devices: 9.04 us -> 7.41 us
    ppermute x1 -> x0, waiting for transfers between devices: 43.1 us -> none  [partner_2(): lax.ppermute(array, axis, [(i, i ^ 1 << apart) for i in range(lax.axis_si...]
    reshape x4 -> x0, local copies, waits for them, and re-layouts: 11 us -> none  [the longest x1 9.07 us: on_device(): tables = legendre.reshape(slot_count, 2, degree_rows, half_lat, lat_rows)]
    pallas_call x0 -> x2, Pallas kernels: none -> 7.76 us  [the longest x1 5.09 us: transform(): pl.pallas_call(functools.partial(transform_kernel, lat_rows=lat_rows), in...]
    gather x2 -> x0, local copies, waits for them, and re-layouts: 6.75 us -> none  [on_device(): picked = jnp.take(fourier, columns, axis=2)]
    convert_element_type x2 -> x0, other arithmetic: 4.23 us -> none  [the longest x1 3.5 us: on_device(): (partner.astype(jnp.float32) + mirror_sign * picked.astype(jnp.float32))....]
    dot_general x1 -> x0, matrix products: 3.64 us -> none  [on_device(): jnp.einsum('ealbcsw,serab->selcwr', halves, tables, preferred_element_typ...]
    ppermute x1 -> x0, starting transfers between devices: 2.97 us -> none  [partner_2(): lax.ppermute(array, axis, [(i, i ^ 1 << apart) for i in range(lax.axis_si...]
    convert_element_type x1 -> x0, local copies, waits for them, and re-layouts: 2.91 us -> none  [on_device(): (partner.astype(jnp.float32) + mirror_sign * picked.astype(jnp.float32))....]
  transfers between devices with their start and end apart: 2 -> 1, of which waited for: 2 -> 1; matrix products, arithmetic and copies ran while one was open for 7% -> 4% of each run, Pallas kernels for 0% -> 0%
where the time goes in v1:
time: 63 us; the launch traced here: 61.9 us
  waiting for transfers between devices  42.2 us (67%)
  Pallas kernels  7.76 us (12%)
  starting transfers between devices  7.41 us (12%)
  local copies, waits for them, and re-layouts  4.3 us (7%)
    all_to_all x1, waiting for transfers between devices, on_block(): lax.all_to_all(outgoing, ('lat', 'lev'), split_axis=0, concat_axis=0, til...  42.2 us
    all_to_all x1, starting transfers between devices, on_block(): lax.all_to_all(outgoing, ('lat', 'lev'), split_axis=0, concat_axis=0, til...  7.41 us
    pallas_call x1, Pallas kernels, transform(): pl.pallas_call(functools.partial(transform_kernel, lat_rows=lat_rows), in...  5.09 us
    unnamed x7, local copies, waits for them, and re-layouts  4.3 us
    pallas_call x1, Pallas kernels, pick(): pl.pallas_call(pick_kernel, grid=(steps,), in_specs=[pl.BlockSpec((1, tab...  2.68 us
  transfers between devices with their start and end apart: 1, of which 1 were waited for; matrix products, arithmetic and copies ran while one was open for 4% of the time, Pallas kernels for 0%

profile of v1, /device:TPU:0, one launch (start us, length us, event | category | flops | bytes accessed | tf_op | source)
XLA Modules:
  0.0 61.9 jit_solution(5048303883169236524)
XLA Ops:
  0.0 0.0 copy-start
  0.0 1.5 %copy-done = bf16[320,12,256]{2,0,1:T(8,128)(2,1)S(1)} copy-done((bf16[320,12,256]{2,0,1:T(8,128)(2,1)S(1)}, bf16[320,12,256]{2,0,1:T(8,128)(2,1)}, u32[]{:S(2)}) %copy-start) | copy-done | bytes 1966104
  1.5 0.0 copy-start.1
  1.5 0.7 %copy-done.1 = s32[128]{0:T(128)S(1)} copy-done((s32[128]{0:T(128)S(1)}, s32[128]{0:T(128)}, u32[]{:S(2)}) %copy-start.1) | copy-done | bytes 536
  2.2 2.7 %shard_map.37 = bf16[32,8,3840]{2,1,0:T(8,128)(2,1)} custom-call(s32[1,128]{1,0:T(1,128)S(1)} %bitcast.6, bf16[3840,256]{1,0:T(8,128)(2,1)S(1)} %bitcast.5), custom_call_target="tpu_custom_call" | custom-call | tf_op jit(solution)/shard_map/pallas_call | solution.py:36
  4.9 7.4 %all-to-all-start = ((bf16[32,8,3840]{2,1,0:T(8,128)(2,1)}), bf16[32,8,3840]{2,1,0:T(8,128)(2,1)}, u32[]{:S(2)}, u32[]{:S(2)}) async-start(bf16[32,8,3840]{2,1,0:T(8,128)(2,1)} %shard_map.37), calls=%async_computation | async-start | bytes 3932160 | tf_op jit(solution)/shard_map/all_to_all | solution.py:114
  12.3 0.0 copy-start.2
  12.3 2.1 %copy.4.tables_ref = bf16[4,2,129,1280]{3,2,1,0:T(8,128)(2,1)S(1)} copy(bf16[4,2,129,1280]{3,1,2,0:T(2,128)(2,1)} %param.5) | data formatting | bytes 5283840 | tf_op args[2]
  14.4 0.0 copy-done.2
  14.4 0.1 dynamic-slice_subtract_fusion
  14.5 0.1 add_select_fusion.first_ref
  14.6 42.2 %all-to-all-done = bf16[32,8,3840]{2,1,0:T(8,128)(2,1)} async-done(((bf16[32,8,3840]{2,1,0:T(8,128)(2,1)}), bf16[32,8,3840]{2,1,0:T(8,128)(2,1)}, u32[]{:S(2)}, u32[]{:S(2)}) %all-to-all-start) | async-done | bytes 1966112 | tf_op jit(solution)/shard_map/all_to_all | solution.py:114
  56.8 5.1 %shard_map.38 = bf16[4,2,48,129]{3,2,1,0:T(8,128)(2,1)} custom-call(s32[4,2]{1,0:T(4,128)S(1)} %add_select_fusion.first_ref, bf16[8,4,8,3840]{3,2,1,0:T(8,128)(2,1)} %bitcast.3.arrived_ref, bf16[4,2,129,1280]{3,2,1,0:T(8,128)(2,1)S(1)} %copy.4.tables_ref), custom_call_target="tpu_custom_call" | custom-call | tf_op jit(solution)/shard_map/pallas_call | solution.py:89
Async XLA Ops:
  0.0 1.5 %copy-start = (bf16[320,12,256]{2,0,1:T(8,128)(2,1)S(1)}, bf16[320,12,256]{2,0,1:T(8,128)(2,1)}, u32[]{:S(2)}) copy-start(bf16[320,12,256]{2,0,1:T(8,128)(2,1)} %param.3) | copy-start | bytes 5898244
  1.5 0.7 %copy-start.1 = (s32[128]{0:T(128)S(1)}, s32[128]{0:T(128)}, u32[]{:S(2)}) copy-start(s32[128]{0:T(128)} %param.4) | copy-start | bytes 1540
  4.9 51.9 %all-to-all-start = ((bf16[32,8,3840]{2,1,0:T(8,128)(2,1)}), bf16[32,8,3840]{2,1,0:T(8,128)(2,1)}, u32[]{:S(2)}, u32[]{:S(2)}) async-start(bf16[32,8,3840]{2,1,0:T(8,128)(2,1)} %shard_map.37), calls=%async_computation | async-start | bytes 3932160 | tf_op jit(solution)/shard_map/all_to_all | solution.py:114
  12.3 2.1 %copy-start.2 = (s32[128]{0:T(128)S(1)}, s32[128]{0:T(128)}, u32[]{:S(2)}) copy-start(s32[128]{0:T(128)} %param.4) | copy-start | bytes 1540

commit v2 on v0

v2 whole, which is shorter than its diff:
```python
import functools

import jax
import jax.numpy as jnp
from jax import lax
from jax.experimental import pallas as pl
from jax.experimental.pallas import tpu as pltpu
from jax.sharding import PartitionSpec as P

NT = (((1,), (1,)), ((), ()))
VMEM = pl.BlockSpec(memory_space=pltpu.VMEM)
SMEM = pl.BlockSpec(memory_space=pltpu.SMEM)
HBM = pl.BlockSpec(memory_space=pltpu.HBM)
Y, X, CORE = 16, 8, 4
NEAR = (0, 1, 2, 3, Y, Y + 1, Y + 2, Y + 3)
FAR = tuple(X + d for d in NEAR)
EARLY = (2, 3)
JOINED = tuple(d for d in NEAR[1:] + FAR if d not in EARLY)
ORDER = (X, Y, X + 2, X + Y, X + 3, 1, Y + 2, X + 1, Y + 3, Y + 1, X + Y + 2, X + Y + 1, X + Y + 3)
WIDE, REST = 256, 64


def here():
    return lax.axis_index("lat") * lax.axis_size("lev") + lax.axis_index("lev")


def pick_kernel(table_ref, x_ref, mine_ref, theirs_ref, *refs, early):
    early_refs, (table, wide, rest, onehot, sems) = refs[:early], refs[early:]
    width = onehot.shape[0]
    channels = x_ref.shape[0]
    me = here()
    core = (me >> 2) & 1
    first = pl.multiple_of(core * REST, REST)
    last = pl.multiple_of((1 - core) * WIDE, REST)
    parts = 3
    step = channels // parts
    copies = [pltpu.make_async_copy(table_ref, table, sems.at[0])]
    for i in range(parts):
        at = pl.ds(i * step, step)
        copies.append(
            pltpu.make_async_copy(x_ref.at[at, pl.ds(first, WIDE)], wide.at[at], sems.at[i + 1])
        )
    copies.append(pltpu.make_async_copy(x_ref.at[:, pl.ds(last, REST)], rest, sems.at[parts + 1]))
    for copy in copies:
        copy.start()
    copies[0].wait()
    row = lax.broadcasted_iota(jnp.int32, (width, 1), 0)
    block = row >> 3
    distance = ((block >> 2) & 1) * Y | ((block >> 3) & 1) * X | (block >> 4) * CORE | block & 3
    slot = (distance ^ me) * 4 + ((row >> 1) & 3)
    lane = lax.broadcasted_iota(jnp.int32, (width, table.shape[1]), 1)
    pair = jnp.sum(jnp.where(lane == slot, table[...], 0), axis=1, keepdims=True)
    column = jnp.where(row & 1 == 1, width - 1 - pair, pair)
    at = lax.broadcasted_iota(jnp.int32, (width, width), 1)
    onehot[...] = jnp.where(at == column, 1.0, 0.0).astype(jnp.bfloat16)

    def emit(x, lanes):
        picked = lax.dot_general(onehot[...], x, NT, preferred_element_type=jnp.float32)
        picked = picked.astype(jnp.bfloat16).reshape(32, 8, picked.shape[1])
        for i, d in enumerate(JOINED):
            mine_ref[i, :, lanes] = picked[(NEAR + FAR).index(d)]
            theirs_ref[i + 1, :, lanes] = picked[16 + (NEAR + FAR).index(d)]
        theirs_ref[0, :, lanes] = picked[16]
        early_refs[0][:, lanes] = picked[0]
        for i, d in enumerate(EARLY):
            early_refs[i + 1][0, :, lanes] = picked[NEAR.index(d)]
            early_refs[i + 1][1, :, lanes] = picked[16 + NEAR.index(d)]

    for i in range(parts):
        copies[i + 1].wait()
        x = wide[i * step : (i + 1) * step].reshape(step * WIDE, width)
        emit(x, pl.ds(i * step * WIDE, step * WIDE))
    copies[parts + 1].wait()
    emit(rest[...].reshape(channels * REST, width), pl.ds(channels * WIDE, channels * REST))


def pick(table, x):
    channels, lat_rows, width = x.shape
    block = (8, channels * lat_rows)
    early = 1 + len(EARLY)
    shapes = [(len(JOINED),) + block, (len(JOINED) + 1,) + block, block] + [(2,) + block] * len(EARLY)
    return pl.pallas_call(
        functools.partial(pick_kernel, early=early),
        in_specs=[HBM] * 2,
        out_specs=[VMEM] * len(shapes),
        out_shape=[jax.ShapeDtypeStruct(s, jnp.bfloat16) for s in shapes],
        scratch_shapes=[
            pltpu.VMEM((1, table.shape[0]), jnp.int32),
            pltpu.VMEM((channels, WIDE, width), jnp.bfloat16),
            pltpu.VMEM((channels, REST, width), jnp.bfloat16),
            pltpu.VMEM((width, width), jnp.bfloat16),
            pltpu.SemaphoreType.DMA((5,)),
        ],
        compiler_params=pltpu.CompilerParams(vmem_limit_bytes=51 * 2**20),
    )(table.reshape(1, -1), x)


def join_kernel(mine_ref, theirs_ref, *outs):
    for i, out in enumerate(outs):
        out[0] = mine_ref[i]
        out[1] = theirs_ref[i + 1]


def join(mine, theirs):
    count = mine.shape[0]
    shape = jax.ShapeDtypeStruct((2,) + mine.shape[1:], mine.dtype)
    return pl.pallas_call(
        join_kernel,
        in_specs=[VMEM] * 2,
        out_specs=[VMEM] * count,
        out_shape=[shape] * count,
        compiler_params=pltpu.CompilerParams(vmem_limit_bytes=16 * 2**20),
    )(mine, theirs)


def second_kernel(*refs):
    for i, ref in enumerate(refs[:-1]):
        refs[-1][i] = ref[1]


def second_blocks(*pieces):
    shape = jax.ShapeDtypeStruct((len(pieces),) + pieces[0].shape[1:], pieces[0].dtype)
    return pl.pallas_call(
        second_kernel,
        in_specs=[VMEM] * len(pieces),
        out_specs=VMEM,
        out_shape=shape,
        compiler_params=pltpu.CompilerParams(vmem_limit_bytes=16 * 2**20),
    )(*pieces)


def transform_kernel(*refs, skip, far, width):
    table_ref, tables_ref, *refs = refs[skip:]
    if far:
        blocks = [(r.at[0], r.at[1]) for r in refs[:8]]
        before, out_ref, held = refs[8:]
    else:
        own, theirs, one, two, three, changed = refs[:6]
        blocks = [
            (own, theirs.at[0]),
            (one.at[0], one.at[1]),
            (two.at[0], changed.at[0]),
            (three.at[0], changed.at[1]),
        ] + [(r.at[0], r.at[1]) for r in refs[6:10]]
        out_ref, held = refs[10:]
    me = here()
    core, z = (me >> 2) & 1, me & 3
    x = (me >> 3) & 1 ^ (1 if far else 0)
    sign = jnp.where(me < Y, 1.0, -1.0).astype(jnp.float32)
    channels = held.shape[3] // 8
    whole = 2 * (WIDE + REST)

    def put(e, lev, row, lane, value):
        for i in range(value.shape[1] // 128):
            held[e, lane // 128 + i, lev, pl.ds(row, 8), :] = value[:, i * 128 : (i + 1) * 128]

    def stage(flip):
        for j in range(4):
            lev = z ^ j

            def both(half, at, size):
                a = blocks[j][half ^ flip][:, at : at + size].astype(jnp.float32)
                b = blocks[4 + j][half ^ flip][:, at : at + size].astype(jnp.float32)
                return a + b, (a - b) * sign

            for half in range(2):
                for c in range(channels):
                    for e, value in enumerate(both(half, c * WIDE, WIDE)):
                        put(e, lev, c * 8, half * (WIDE + 2 * REST), value)
            for c in range(0, channels, 2):
                zero, one = [both(half, channels * WIDE + c * REST, 2 * REST) for half in range(2)]
                for e in range(2):
                    even = jnp.concatenate([zero[e][:, :REST], one[e][:, :REST]], 1)
                    odd = jnp.concatenate([zero[e][:, REST:], one[e][:, REST:]], 1)
                    put(e, lev, c * 8, WIDE, even)
                    put(e, lev, c * 8 + 8, WIDE, odd)

    for flip in range(2):
        pl.when(core == flip)(functools.partial(stage, flip))

    lanes = pl.ds(pl.multiple_of(x * whole, 128), whole)
    for e in range(2):
        tiles = [held.at[e, i].reshape(4 * channels * 8, 128) for i in range(whole // 128)]
        for s in range(4):
            rows = [
                jnp.concatenate([t[pl.ds(2 * s + w, 4 * channels, stride=8), :] for t in tiles], 1)
                for w in range(2)
            ]
            products = lax.dot_general(
                jnp.concatenate(rows, 0).astype(jnp.bfloat16),
                tables_ref[s, e, :, lanes],
                NT,
                preferred_element_type=jnp.float32,
            )
            count = (width - table_ref[me * 4 + s] - e + 1) // 2
            one, two = products[: 4 * channels], products[4 * channels :]
            degree = lax.broadcasted_iota(jnp.int32, one.shape, 1)
            chosen = jnp.where(degree < count, one, two)
            if far:
                chosen = chosen + before[s, e]
            out_ref[s, e] = chosen.astype(out_ref.dtype)


def transform(table, tables, blocks, far, width, rest=()):
    slots, _, degrees, lats = tables.shape
    channels = blocks[0].shape[-1] // (WIDE + REST)
    return pl.pallas_call(
        functools.partial(transform_kernel, skip=len(rest), far=far, width=width),
        in_specs=[pl.BlockSpec(memory_space=pl.ANY)] * len(rest) + [SMEM] + [VMEM] * (1 + len(blocks)),
        out_specs=VMEM,
        out_shape=jax.ShapeDtypeStruct(
            (slots, 2, 4 * channels, degrees), jnp.bfloat16 if far else jnp.float32
        ),
        scratch_shapes=[
            pltpu.VMEM((2, 2 * (WIDE + REST) // 128, 4, channels * 8, 128), jnp.float32)
        ],
        compiler_params=pltpu.CompilerParams(vmem_limit_bytes=20 * 2**20),
    )(*rest, table, tables, *blocks)


def send(piece, distance):
    count = lax.axis_size("lat") * lax.axis_size("lev")
    return lax.ppermute(piece, ("lat", "lev"), [(i, i ^ distance) for i in range(count)])


def on_block(fourier, table, legendre):
    width = fourier.shape[2]
    mine, theirs, own, *early = pick(table, fourier.transpose(1, 0, 2))
    got = {d: send(piece, d) for d, piece in zip(EARLY, early)}
    theirs = send(theirs, CORE)
    ready = dict(zip(JOINED, join(mine, theirs)))
    got.update({d: send(ready[d], d) for d in ORDER})
    came = [got[d] for d in EARLY]
    *came, got[1] = lax.optimization_barrier((*came, got[1]))
    changed = send(second_blocks(*came), CORE)
    near = [own, theirs] + [got[d] for d in NEAR[1:4]] + [changed] + [got[d] for d in NEAR[4:]]
    partial = transform(table, legendre, near, False, width)
    far = [got[d] for d in FAR] + [partial]
    return transform(table, legendre, far, True, width, list(got.values()))


def row_counts(table, slot_count, wavenumbers):
    position = lax.axis_index(("lat", "lev")) * slot_count
    owned = lax.dynamic_slice_in_dim(table, position, slot_count)
    parity = jnp.arange(2, dtype=jnp.int32)
    return (wavenumbers - owned[:, None] - parity[None, :] + 1) // 2


def on_any(fourier, table, legendre):
    lat_count, lev_count = lax.axis_size("lat"), lax.axis_size("lev")
    devices, half_lat = lat_count * lev_count, lat_count // 2
    lat_rows, channels, wavenumbers = fourier.shape
    slot_count, _, degree_rows, _ = legendre.shape
    columns = jnp.stack([table, wavenumbers - 1 - table], axis=1).reshape(-1)
    picked = jnp.take(fourier, columns, axis=2)
    shaped = picked.reshape((1, lat_rows, channels, devices, wavenumbers // devices))
    arrived = lax.all_to_all(shaped, ("lat", "lev"), split_axis=3, concat_axis=0, tiled=True)
    halves = arrived.reshape(2, half_lat, lev_count, lat_rows, channels, slot_count, 2)
    north, south = halves[0].astype(jnp.float32), halves[1].astype(jnp.float32)
    merged = jnp.stack([north + south, north - south]).astype(jnp.bfloat16)
    tables = legendre.reshape(slot_count, 2, degree_rows, half_lat, lat_rows)
    products = jnp.einsum(
        "ealbcsw,serab->selcwr", merged, tables, preferred_element_type=jnp.float32
    )
    products = products.reshape(slot_count, 2, lev_count * channels, 2, degree_rows)
    first = row_counts(table, slot_count, wavenumbers)
    in_first = jnp.arange(degree_rows, dtype=jnp.int32)[None, None, :] < first[:, :, None]
    spectral = jnp.where(in_first[:, :, None, :], products[:, :, :, 0], products[:, :, :, 1])
    return spectral.astype(jnp.bfloat16)


def solution(mesh):
    in_specs = (P("lat", "lev", None), P(), P(("lat", "lev"), None, None, None))
    out_specs = P(("lat", "lev"), None, None, None)
    on_device = on_block if dict(mesh.shape) == {"lat": 8, "lev": 4} else on_any
    return jax.shard_map(
        on_device, mesh=mesh, in_specs=in_specs, out_specs=out_specs, check_vma=False
    )
```

time: 136 us -> 55.3 us (0.41)
  waiting for transfers between devices: 87.1 us -> 14.7 us
  local copies, waits for them, and re-layouts: 28 us -> 1.01 us
  starting transfers between devices: 9.04 us -> 32.9 us
  other arithmetic: 7.24 us -> 0 us
  Pallas kernels: 0 us -> 6.42 us
  matrix products: 3.64 us -> 0 us
    all_to_all x1 -> x0, waiting for transfers between devices: 44 us -> none  [regroup(): lax.all_to_all(shaped, ('lat', 'lev'), split_axis=3, concat_axis=0, tiled...]
    ppermute x1 -> x17, starting transfers between devices: 2.97 us -> 32.9 us  [send(): lax.ppermute(piece, ('lat', 'lev'), [(i, i ^ distance) for i in range(cou...]
    ppermute x1 -> x17, waiting for transfers between devices: 43.1 us -> 14.7 us  [send(): lax.ppermute(piece, ('lat', 'lev'), [(i, i ^ distance) for i in range(cou...]
    reshape x4 -> x0, local copies, waits for them, and re-layouts: 11 us -> none  [the longest x1 9.07 us: on_device(): tables = legendre.reshape(slot_count, 2, degree_rows, half_lat, lat_rows)]
    gather x2 -> x0, local copies, waits for them, and re-layouts: 6.75 us -> none  [on_device(): picked = jnp.take(fourier, columns, axis=2)]
    pallas_call x0 -> x5, Pallas kernels: none -> 6.42 us  [the longest x2 3.77 us: transform(): pl.pallas_call(functools.partial(transform_kernel, skip=len(rest), far=fa...]
    all_to_all x1 -> x0, starting transfers between devices: 6.07 us -> none  [regroup(): lax.all_to_all(shaped, ('lat', 'lev'), split_axis=3, concat_axis=0, tiled...]
    convert_element_type x2 -> x0, other arithmetic: 4.23 us -> none  [the longest x1 3.5 us: on_device(): (partner.astype(jnp.float32) + mirror_sign * picked.astype(jnp.float32))....]
  transfers between devices with their start and end apart: 2 -> 17, of which waited for: 2 -> 3; matrix products, arithmetic and copies ran while one was open for 7% -> 1% of each run, Pallas kernels for 0% -> 3%
where the time goes in v2:
time: 55.3 us; the launch traced here: 55.1 us
  starting transfers between devices  32.9 us (59%)
  waiting for transfers between devices  14.7 us (27%)
  Pallas kernels  6.42 us (12%)
  local copies, waits for them, and re-layouts  1.01 us (2%)
    ppermute x17, starting transfers between devices, send(): lax.ppermute(piece, ('lat', 'lev'), [(i, i ^ distance) for i in range(cou...  32.9 us
    ppermute x17, waiting for transfers between devices, send(): lax.ppermute(piece, ('lat', 'lev'), [(i, i ^ distance) for i in range(cou...  14.7 us
    pallas_call x2, Pallas kernels, transform(): pl.pallas_call(functools.partial(transform_kernel, skip=len(rest), far=fa...  3.77 us
    pallas_call x1, Pallas kernels, pick(): pl.pallas_call(functools.partial(pick_kernel, early=early), in_specs=[HBM...  2.54 us
  transfers between devices with their start and end apart: 17, of which 3 were waited for; matrix products, arithmetic and copies ran while one was open for 1% of the time, Pallas kernels for 3%

profile of v2, /device:TPU:0, one launch (start us, length us, event | category | flops | bytes accessed | tf_op | source)
XLA Modules:
  0.0 55.1 jit_solution(6731389120430807853)
XLA Ops:
  0.0 0.7 %copy-done = s32[128]{0:T(128)S(1)} copy-done((s32[128]{0:T(128)S(1)}, s32[128]{0:T(128)}, u32[]{:S(2)}) %copy-start) | copy-done | bytes 536
  0.7 2.5 %shard_map.37 = (bf16[13,8,3840]{2,1,0:T(8,128)(2,1)S(1)}, bf16[14,8,3840]{2,1,0:T(8,128)(2,1)S(1)}, bf16[8,3840]{1,0:T(8,128)(2,1)S(1)}, bf16[2,8,3840]{2,1,0:T(8,128)(2,1)S(1)}, bf16[2,8,3840]{2,1,0:T(8,128)(2,1)S(1)}) custom-call(s32[1,128]{1,0:T(1,128)S(1)} %bitcast.2, bf16[12,320,256]{2,1,0:T(8,128)(2,1)} %bitcast.3), custom_call_target="tpu_custom_call" | custom-call | tf_op jit(solution)/shard_map/pallas_call | solution.py:82
  3.2 0.5 collective-permute-start.2
  3.7 3.7 %collective-permute-start = (bf16[2,8,3840]{2,1,0:T(8,128)(2,1)S(1)}, bf16[2,8,3840]{2,1,0:T(8,128)(2,1)S(1)}, u32[]{:S(2)}, u32[]{:S(2)}) collective-permute-start(bf16[2,8,3840]{2,1,0:T(8,128)(2,1)S(1)} %get-tuple-element.26), channel_id=1, source_target_pairs={{0,2},{1,3},{2,0},{3,1},{4,6},{5,7},{6,4},{7,5},{8,10},{9,11},{10,... | collective-permute-start | bytes 368648 | tf_op jit(solution)/shard_map/ppermute | solution.py:223
  7.4 1.3 %collective-permute-start.1 = (bf16[2,8,3840]{2,1,0:T(8,128)(2,1)S(1)}, bf16[2,8,3840]{2,1,0:T(8,128)(2,1)S(1)}, u32[]{:S(2)}, u32[]{:S(2)}) collective-permute-start(bf16[2,8,3840]{2,1,0:T(8,128)(2,1)S(1)} %get-tuple-element.27), channel_id=1, source_target_pairs={{0,3},{1,2},{2,1},{3,0},{4,7},{5,6},{6,5},{7,4},{8,11},{9,10},{10,... | collective-permute-start | bytes 368648 | tf_op jit(solution)/shard_map/ppermute | solution.py:223
  8.7 0.1 shard_map.38
  8.9 0.3 collective-permute-start.8
  9.2 1.5 %collective-permute-start.3 = (bf16[2,8,3840]{2,1,0:T(8,128)(2,1)S(1)}, bf16[2,8,3840]{2,1,0:T(8,128)(2,1)S(1)}, u32[]{:S(2)}, u32[]{:S(2)}) collective-permute-start(bf16[2,8,3840]{2,1,0:T(8,128)(2,1)S(1)} %get-tuple-element.30), channel_id=1, source_target_pairs={{0,8},{1,9},{2,10},{3,11},{4,12},{5,13},{6,14},{7,15},{8,0},{9,1},... | collective-permute-start | bytes 368648 | tf_op jit(solution)/shard_map/ppermute | solution.py:223
  10.6 1.5 %collective-permute-start.4 = (bf16[2,8,3840]{2,1,0:T(8,128)(2,1)S(1)}, bf16[2,8,3840]{2,1,0:T(8,128)(2,1)S(1)}, u32[]{:S(2)}, u32[]{:S(2)}) collective-permute-start(bf16[2,8,3840]{2,1,0:T(8,128)(2,1)S(1)} %get-tuple-element.31), channel_id=1, source_target_pairs={{0,16},{1,17},{2,18},{3,19},{4,20},{5,21},{6,22},{7,23},{8,24},{9,... | collective-permute-start | bytes 368648 | tf_op jit(solution)/shard_map/ppermute | solution.py:223
  12.2 4.7 %collective-permute-done.refs_0_.refs_5_ = bf16[2,8,3840]{2,1,0:T(8,128)(2,1)S(1)} collective-permute-done((bf16[2,8,3840]{2,1,0:T(8,128)(2,1)S(1)}, bf16[2,8,3840]{2,1,0:T(8,128)(2,1)S(1)}, u32[]{:S(2)}, u32[]{:S(2)}) %collective-permute-start) | collective-permute-done | bytes 122912 | tf_op jit(solution)/shard_map/ppermute | solution.py:223
  16.9 0.7 %collective-permute-start.5 = (bf16[2,8,3840]{2,1,0:T(8,128)(2,1)S(1)}, bf16[2,8,3840]{2,1,0:T(8,128)(2,1)S(1)}, u32[]{:S(2)}, u32[]{:S(2)}) collective-permute-start(bf16[2,8,3840]{2,1,0:T(8,128)(2,1)S(1)} %get-tuple-element.32), channel_id=1, source_target_pairs={{0,10},{1,11},{2,8},{3,9},{4,14},{5,15},{6,12},{7,13},{8,2},{9,3},... | collective-permute-start | bytes 368648 | tf_op jit(solution)/shard_map/ppermute | solution.py:223
  17.6 0.0 collective-permute-done.1.refs_1_.refs_6_
  17.6 2.0 %collective-permute-start.6 = (bf16[2,8,3840]{2,1,0:T(8,128)(2,1)S(1)}, bf16[2,8,3840]{2,1,0:T(8,128)(2,1)S(1)}, u32[]{:S(2)}, u32[]{:S(2)}) collective-permute-start(bf16[2,8,3840]{2,1,0:T(8,128)(2,1)S(1)} %get-tuple-element.33), channel_id=1, source_target_pairs={{0,24},{1,25},{2,26},{3,27},{4,28},{5,29},{6,30},{7,31},{8,16},{9,... | collective-permute-start | bytes 368648 | tf_op jit(solution)/shard_map/ppermute | solution.py:223
  19.6 0.0 collective-permute-done.8.refs_4_.refs_7_
  19.6 7.4 %collective-permute-start.9 = (bf16[2,8,3840]{2,1,0:T(8,128)(2,1)S(1)}, bf16[2,8,3840]{2,1,0:T(8,128)(2,1)S(1)}, u32[]{:S(2)}, u32[]{:S(2)}) collective-permute-start(bf16[2,8,3840]{2,1,0:T(8,128)(2,1)S(1)} %get-tuple-element.37), channel_id=1, source_target_pairs={{0,18},{1,19},{2,16},{3,17},{4,22},{5,23},{6,20},{7,21},{8,26},{9,... | collective-permute-start | bytes 368648 | tf_op jit(solution)/shard_map/ppermute | solution.py:223
  27.0 0.0 collective-permute-done.3.refs_2_.refs_17_
  27.0 1.4 %collective-permute-start.11 = (bf16[2,8,3840]{2,1,0:T(8,128)(2,1)S(1)}, bf16[2,8,3840]{2,1,0:T(8,128)(2,1)S(1)}, u32[]{:S(2)}, u32[]{:S(2)}) collective-permute-start(bf16[2,8,3840]{2,1,0:T(8,128)(2,1)S(1)} %get-tuple-element.39), channel_id=1, source_target_pairs={{0,19},{1,18},{2,17},{3,16},{4,23},{5,22},{6,21},{7,20},{8,27},{9,... | collective-permute-start | bytes 368648 | tf_op jit(solution)/shard_map/ppermute | solution.py:223
  28.4 0.0 collective-permute-done.4.refs_8_.refs_3_
  28.4 0.2 collective-permute-start.12
  28.6 0.0 collective-permute-done.5.refs_4_.refs_19_
  28.6 0.1 collective-permute-start.16
  28.7 3.2 %collective-permute-start.7 = (bf16[2,8,3840]{2,1,0:T(8,128)(2,1)S(1)}, bf16[2,8,3840]{2,1,0:T(8,128)(2,1)S(1)}, u32[]{:S(2)}, u32[]{:S(2)}) collective-permute-start(bf16[2,8,3840]{2,1,0:T(8,128)(2,1)S(1)} %get-tuple-element.34), channel_id=1, source_target_pairs={{0,11},{1,10},{2,9},{3,8},{4,15},{5,14},{6,13},{7,12},{8,3},{9,2},... | collective-permute-start | bytes 368648 | tf_op jit(solution)/shard_map/ppermute | solution.py:223
  31.9 5.5 %collective-permute-done.9.refs_10_.refs_8_ = bf16[2,8,3840]{2,1,0:T(8,128)(2,1)S(1)} collective-permute-done((bf16[2,8,3840]{2,1,0:T(8,128)(2,1)S(1)}, bf16[2,8,3840]{2,1,0:T(8,128)(2,1)S(1)}, u32[]{:S(2)}, u32[]{:S(2)}) %collective-permute-start.9) | collective-permute-done | bytes 122912 | tf_op jit(solution)/shard_map/ppermute | solution.py:223
  37.5 0.0 collective-permute-done.11.refs_11_.refs_10_
  37.5 3.8 %collective-permute-start.13 = (bf16[2,8,3840]{2,1,0:T(8,128)(2,1)S(1)}, bf16[2,8,3840]{2,1,0:T(8,128)(2,1)S(1)}, u32[]{:S(2)}, u32[]{:S(2)}) collective-permute-start(bf16[2,8,3840]{2,1,0:T(8,128)(2,1)S(1)} %get-tuple-element.41), channel_id=1, source_target_pairs={{0,26},{1,27},{2,24},{3,25},{4,30},{5,31},{6,28},{7,29},{8,18},{9,... | collective-permute-start | bytes 368648 | tf_op jit(solution)/shard_map/ppermute | solution.py:223
  41.2 0.9 %collective-permute-start.14 = (bf16[2,8,3840]{2,1,0:T(8,128)(2,1)S(1)}, bf16[2,8,3840]{2,1,0:T(8,128)(2,1)S(1)}, u32[]{:S(2)}, u32[]{:S(2)}) collective-permute-start(bf16[2,8,3840]{2,1,0:T(8,128)(2,1)S(1)} %get-tuple-element.42), channel_id=1, source_target_pairs={{0,25},{1,24},{2,27},{3,26},{4,29},{5,28},{6,31},{7,30},{8,17},{9,... | collective-permute-start | bytes 368648 | tf_op jit(solution)/shard_map/ppermute | solution.py:223
  42.2 4.3 %collective-permute-start.15 = (bf16[2,8,3840]{2,1,0:T(8,128)(2,1)S(1)}, bf16[2,8,3840]{2,1,0:T(8,128)(2,1)S(1)}, u32[]{:S(2)}, u32[]{:S(2)}) collective-permute-start(bf16[2,8,3840]{2,1,0:T(8,128)(2,1)S(1)} %get-tuple-element.43), channel_id=1, source_target_pairs={{0,27},{1,26},{2,25},{3,24},{4,31},{5,30},{6,29},{7,28},{8,19},{9,... | collective-permute-start | bytes 368648 | tf_op jit(solution)/shard_map/ppermute | solution.py:223
  46.5 0.3 copy.5.refs_1_.refs_16_
  46.9 1.5 %shard_map.40.refs_25_ = f32[4,2,48,129]{3,2,1,0:T(8,128)S(1)} custom-call(s32[128]{0:T(128)S(1)} %copy-done, bf16[4,2,129,1280]{3,2,1,0:T(8,128)(2,1)S(1)} %copy.5.refs_1_.refs_16_, bf16[8,3840]{1,0:T(8,128)(2,1)S(1)} %get-tuple-element.44.refs_2_, bf16[14,8,3840]{2,1,0:T(8,128)(2,1)S(1)} %collective-permute-done.2.theirs_ref.refs_3_, ...), custom_call_target="tpu_custom_call" | custom-call | tf_op jit(solution)/shard_map/pallas_call | solution.py:207
  48.4 4.4 %collective-permute-done.13.refs_12_.refs_23_ = bf16[2,8,3840]{2,1,0:T(8,128)(2,1)S(1)} collective-permute-done((bf16[2,8,3840]{2,1,0:T(8,128)(2,1)S(1)}, bf16[2,8,3840]{2,1,0:T(8,128)(2,1)S(1)}, u32[]{:S(2)}, u32[]{:S(2)}) %collective-permute-start.13) | collective-permute-done | bytes 122912 | tf_op jit(solution)/shard_map/ppermute | solution.py:223
  52.9 0.0 collective-permute-done.14.refs_13_.refs_22_
  52.9 2.2 %shard_map.41 = bf16[4,2,48,129]{3,2,1,0:T(8,128)(2,1)} custom-call(bf16[2,8,3840]{2,1,0:T(8,128)(2,1)S(1)} %collective-permute-done.refs_0_.refs_5_, bf16[2,8,3840]{2,1,0:T(8,128)(2,1)S(1)} %collective-permute-done.1.refs_1_.refs_6_, bf16[2,8,3840]{2,1,0:T(8,128)(2,1)S(1)} %collective-permute-done.3.refs_2_.refs_17_, ...), custom_call_target="tpu_custom_call" | custom-call | tf_op jit(solution)/shard_map/pallas_call | solution.py:207
  (12 shorter events, 0.0 us)
Async XLA Ops:
  0.0 0.7 %copy-start = (s32[128]{0:T(128)S(1)}, s32[128]{0:T(128)}, u32[]{:S(2)}) copy-start(s32[128]{0:T(128)} %refs_15_.1) | copy-start | bytes 1540
  0.7 45.9 %copy-start.1 = (bf16[4,2,129,1280]{3,1,2,0:T(2,128)(2,1)S(1)}, bf16[4,2,129,1280]{3,1,2,0:T(2,128)(2,1)}, u32[]{:S(2)}) copy-start(bf16[4,2,129,1280]{3,1,2,0:T(2,128)(2,1)} %param.5) | copy-start | bytes 7925764
  3.2 5.5 %collective-permute-start.2 = (bf16[14,8,3840]{2,1,0:T(8,128)(2,1)S(1)}, bf16[14,8,3840]{2,1,0:T(8,128)(2,1)S(1)}, u32[]{:S(2)}, u32[]{:S(2)}) collective-permute-start(bf16[14,8,3840]{2,1,0:T(8,128)(2,1)S(1)} %get-tuple-element.29), channel_id=1, source_target_pairs={{0,4},{1,5},{2,6},{3,7},{4,0},{5,1},{6,2},{7,3},{8,12},{9,13},{10,... | collective-permute-start | bytes 2580488 | tf_op jit(solution)/shard_map/ppermute | solution.py:223
  3.7 13.2 %collective-permute-start = (bf16[2,8,3840]{2,1,0:T(8,128)(2,1)S(1)}, bf16[2,8,3840]{2,1,0:T(8,128)(2,1)S(1)}, u32[]{:S(2)}, u32[]{:S(2)}) collective-permute-start(bf16[2,8,3840]{2,1,0:T(8,128)(2,1)S(1)} %get-tuple-element.26), channel_id=1, source_target_pairs={{0,2},{1,3},{2,0},{3,1},{4,6},{5,7},{6,4},{7,5},{8,10},{9,11},{10,... | collective-permute-start | bytes 368648 | tf_op jit(solution)/shard_map/ppermute | solution.py:223
  7.4 10.2 %collective-permute-start.1 = (bf16[2,8,3840]{2,1,0:T(8,128)(2,1)S(1)}, bf16[2,8,3840]{2,1,0:T(8,128)(2,1)S(1)}, u32[]{:S(2)}, u32[]{:S(2)}) collective-permute-start(bf16[2,8,3840]{2,1,0:T(8,128)(2,1)S(1)} %get-tuple-element.27), channel_id=1, source_target_pairs={{0,3},{1,2},{2,1},{3,0},{4,7},{5,6},{6,5},{7,4},{8,11},{9,10},{10,... | collective-permute-start | bytes 368648 | tf_op jit(solution)/shard_map/ppermute | solution.py:223
  8.9 10.7 %collective-permute-start.8 = (bf16[2,8,3840]{2,1,0:T(8,128)(2,1)S(1)}, bf16[2,8,3840]{2,1,0:T(8,128)(2,1)S(1)}, u32[]{:S(2)}, u32[]{:S(2)}) collective-permute-start(bf16[2,8,3840]{2,1,0:T(8,128)(2,1)S(1)} %get-tuple-element.35), channel_id=1, source_target_pairs={{0,1},{1,0},{2,3},{3,2},{4,5},{5,4},{6,7},{7,6},{8,9},{9,8},{10,11... | collective-permute-start | bytes 368648 | tf_op jit(solution)/shard_map/ppermute | solution.py:223
  9.2 17.8 %collective-permute-start.3 = (bf16[2,8,3840]{2,1,0:T(8,128)(2,1)S(1)}, bf16[2,8,3840]{2,1,0:T(8,128)(2,1)S(1)}, u32[]{:S(2)}, u32[]{:S(2)}) collective-permute-start(bf16[2,8,3840]{2,1,0:T(8,128)(2,1)S(1)} %get-tuple-element.30), channel_id=1, source_target_pairs={{0,8},{1,9},{2,10},{3,11},{4,12},{5,13},{6,14},{7,15},{8,0},{9,1},... | collective-permute-start | bytes 368648 | tf_op jit(solution)/shard_map/ppermute | solution.py:223
  10.6 17.7 %collective-permute-start.4 = (bf16[2,8,3840]{2,1,0:T(8,128)(2,1)S(1)}, bf16[2,8,3840]{2,1,0:T(8,128)(2,1)S(1)}, u32[]{:S(2)}, u32[]{:S(2)}) collective-permute-start(bf16[2,8,3840]{2,1,0:T(8,128)(2,1)S(1)} %get-tuple-element.31), channel_id=1, source_target_pairs={{0,16},{1,17},{2,18},{3,19},{4,20},{5,21},{6,22},{7,23},{8,24},{9,... | collective-permute-start | bytes 368648 | tf_op jit(solution)/shard_map/ppermute | solution.py:223
  16.9 11.7 %collective-permute-start.5 = (bf16[2,8,3840]{2,1,0:T(8,128)(2,1)S(1)}, bf16[2,8,3840]{2,1,0:T(8,128)(2,1)S(1)}, u32[]{:S(2)}, u32[]{:S(2)}) collective-permute-start(bf16[2,8,3840]{2,1,0:T(8,128)(2,1)S(1)} %get-tuple-element.32), channel_id=1, source_target_pairs={{0,10},{1,11},{2,8},{3,9},{4,14},{5,15},{6,12},{7,13},{8,2},{9,3},... | collective-permute-start | bytes 368648 | tf_op jit(solution)/shard_map/ppermute | solution.py:223
  17.6 11.1 %collective-permute-start.6 = (bf16[2,8,3840]{2,1,0:T(8,128)(2,1)S(1)}, bf16[2,8,3840]{2,1,0:T(8,128)(2,1)S(1)}, u32[]{:S(2)}, u32[]{:S(2)}) collective-permute-start(bf16[2,8,3840]{2,1,0:T(8,128)(2,1)S(1)} %get-tuple-element.33), channel_id=1, source_target_pairs={{0,24},{1,25},{2,26},{3,27},{4,28},{5,29},{6,30},{7,31},{8,16},{9,... | collective-permute-start | bytes 368648 | tf_op jit(solution)/shard_map/ppermute | solution.py:223
  19.6 17.9 %collective-permute-start.9 = (bf16[2,8,3840]{2,1,0:T(8,128)(2,1)S(1)}, bf16[2,8,3840]{2,1,0:T(8,128)(2,1)S(1)}, u32[]{:S(2)}, u32[]{:S(2)}) collective-permute-start(bf16[2,8,3840]{2,1,0:T(8,128)(2,1)S(1)} %get-tuple-element.37), channel_id=1, source_target_pairs={{0,18},{1,19},{2,16},{3,17},{4,22},{5,23},{6,20},{7,21},{8,26},{9,... | collective-permute-start | bytes 368648 | tf_op jit(solution)/shard_map/ppermute | solution.py:223
  27.0 10.5 %collective-permute-start.11 = (bf16[2,8,3840]{2,1,0:T(8,128)(2,1)S(1)}, bf16[2,8,3840]{2,1,0:T(8,128)(2,1)S(1)}, u32[]{:S(2)}, u32[]{:S(2)}) collective-permute-start(bf16[2,8,3840]{2,1,0:T(8,128)(2,1)S(1)} %get-tuple-element.39), channel_id=1, source_target_pairs={{0,19},{1,18},{2,17},{3,16},{4,23},{5,22},{6,21},{7,20},{8,27},{9,... | collective-permute-start | bytes 368648 | tf_op jit(solution)/shard_map/ppermute | solution.py:223
  28.4 12.9 %collective-permute-start.12 = (bf16[2,8,3840]{2,1,0:T(8,128)(2,1)S(1)}, bf16[2,8,3840]{2,1,0:T(8,128)(2,1)S(1)}, u32[]{:S(2)}, u32[]{:S(2)}) collective-permute-start(bf16[2,8,3840]{2,1,0:T(8,128)(2,1)S(1)} %get-tuple-element.40), channel_id=1, source_target_pairs={{0,17},{1,16},{2,19},{3,18},{4,21},{5,20},{6,23},{7,22},{8,25},{9,... | collective-permute-start | bytes 368648 | tf_op jit(solution)/shard_map/ppermute | solution.py:223
  28.6 13.6 %collective-permute-start.16 = (bf16[2,8,3840]{2,1,0:T(8,128)(2,1)S(1)}, bf16[2,8,3840]{2,1,0:T(8,128)(2,1)S(1)}, u32[]{:S(2)}, u32[]{:S(2)}) collective-permute-start(bf16[2,8,3840]{2,1,0:T(8,128)(2,1)S(1)} %shard_map.39), channel_id=1, source_target_pairs={{0,4},{1,5},{2,6},{3,7},{4,0},{5,1},{6,2},{7,3},{8,12},{9,13},{10,... | collective-permute-start | bytes 368648 | tf_op jit(solution)/shard_map/ppermute | solution.py:223
  28.7 19.7 %collective-permute-start.7 = (bf16[2,8,3840]{2,1,0:T(8,128)(2,1)S(1)}, bf16[2,8,3840]{2,1,0:T(8,128)(2,1)S(1)}, u32[]{:S(2)}, u32[]{:S(2)}) collective-permute-start(bf16[2,8,3840]{2,1,0:T(8,128)(2,1)S(1)} %get-tuple-element.34), channel_id=1, source_target_pairs={{0,11},{1,10},{2,9},{3,8},{4,15},{5,14},{6,13},{7,12},{8,3},{9,2},... | collective-permute-start | bytes 368648 | tf_op jit(solution)/shard_map/ppermute | solution.py:223
  37.5 10.9 %collective-permute-start.10 = (bf16[2,8,3840]{2,1,0:T(8,128)(2,1)S(1)}, bf16[2,8,3840]{2,1,0:T(8,128)(2,1)S(1)}, u32[]{:S(2)}, u32[]{:S(2)}) collective-permute-start(bf16[2,8,3840]{2,1,0:T(8,128)(2,1)S(1)} %get-tuple-element.38), channel_id=1, source_target_pairs={{0,9},{1,8},{2,11},{3,10},{4,13},{5,12},{6,15},{7,14},{8,1},{9,0},... | collective-permute-start | bytes 368648 | tf_op jit(solution)/shard_map/ppermute | solution.py:223
  37.5 15.4 %collective-permute-start.13 = (bf16[2,8,3840]{2,1,0:T(8,128)(2,1)S(1)}, bf16[2,8,3840]{2,1,0:T(8,128)(2,1)S(1)}, u32[]{:S(2)}, u32[]{:S(2)}) collective-permute-start(bf16[2,8,3840]{2,1,0:T(8,128)(2,1)S(1)} %get-tuple-element.41), channel_id=1, source_target_pairs={{0,26},{1,27},{2,24},{3,25},{4,30},{5,31},{6,28},{7,29},{8,18},{9,... | collective-permute-start | bytes 368648 | tf_op jit(solution)/shard_map/ppermute | solution.py:223
  41.2 11.6 %collective-permute-start.14 = (bf16[2,8,3840]{2,1,0:T(8,128)(2,1)S(1)}, bf16[2,8,3840]{2,1,0:T(8,128)(2,1)S(1)}, u32[]{:S(2)}, u32[]{:S(2)}) collective-permute-start(bf16[2,8,3840]{2,1,0:T(8,128)(2,1)S(1)} %get-tuple-element.42), channel_id=1, source_target_pairs={{0,25},{1,24},{2,27},{3,26},{4,29},{5,28},{6,31},{7,30},{8,17},{9,... | collective-permute-start | bytes 368648 | tf_op jit(solution)/shard_map/ppermute | solution.py:223
  42.2 10.7 %collective-permute-start.15 = (bf16[2,8,3840]{2,1,0:T(8,128)(2,1)S(1)}, bf16[2,8,3840]{2,1,0:T(8,128)(2,1)S(1)}, u32[]{:S(2)}, u32[]{:S(2)}) collective-permute-start(bf16[2,8,3840]{2,1,0:T(8,128)(2,1)S(1)} %get-tuple-element.43), channel_id=1, source_target_pairs={{0,27},{1,26},{2,25},{3,24},{4,31},{5,30},{6,29},{7,28},{8,19},{9,... | collective-permute-start | bytes 368648 | tf_op jit(solution)/shard_map/ppermute | solution.py:223

commit v3 on v2

--- a/solution.py
+++ b/solution.py
@@ -9,14 +9,13 @@
 
 NT = (((1,), (1,)), ((), ()))
 VMEM = pl.BlockSpec(memory_space=pltpu.VMEM)
-SMEM = pl.BlockSpec(memory_space=pltpu.SMEM)
 HBM = pl.BlockSpec(memory_space=pltpu.HBM)
 Y, X, CORE = 16, 8, 4
 NEAR = (0, 1, 2, 3, Y, Y + 1, Y + 2, Y + 3)
 FAR = tuple(X + d for d in NEAR)
 EARLY = (2, 3)
 JOINED = tuple(d for d in NEAR[1:] + FAR if d not in EARLY)
-ORDER = (X, Y, X + 2, X + Y, X + 3, 1, Y + 2, X + 1, Y + 3, Y + 1, X + Y + 2, X + Y + 1, X + Y + 3)
+ORDER = (1, 16, 18, 17, 19, 8, 10, 9, 11, 24, 26, 25, 27)
 WIDE, REST = 256, 64
 
 
@@ -25,7 +24,7 @@
 
 
 def pick_kernel(table_ref, x_ref, mine_ref, theirs_ref, *refs, early):
-    early_refs, (table, wide, rest, onehot, sems) = refs[:early], refs[early:]
+    early_refs, (wide, rest, onehot, sems) = refs[:early], refs[early:]
     width = onehot.shape[0]
     channels = x_ref.shape[0]
     me = here()
@@ -34,22 +33,21 @@
     last = pl.multiple_of((1 - core) * WIDE, REST)
     parts = 3
     step = channels // parts
-    copies = [pltpu.make_async_copy(table_ref, table, sems.at[0])]
+    copies = []
     for i in range(parts):
         at = pl.ds(i * step, step)
         copies.append(
-            pltpu.make_async_copy(x_ref.at[at, pl.ds(first, WIDE)], wide.at[at], sems.at[i + 1])
+            pltpu.make_async_copy(x_ref.at[at, pl.ds(first, WIDE)], wide.at[at], sems.at[i])
         )
-    copies.append(pltpu.make_async_copy(x_ref.at[:, pl.ds(last, REST)], rest, sems.at[parts + 1]))
+    copies.append(pltpu.make_async_copy(x_ref.at[:, pl.ds(last, REST)], rest, sems.at[parts]))
     for copy in copies:
         copy.start()
-    copies[0].wait()
     row = lax.broadcasted_iota(jnp.int32, (width, 1), 0)
     block = row >> 3
     distance = ((block >> 2) & 1) * Y | ((block >> 3) & 1) * X | (block >> 4) * CORE | block & 3
     slot = (distance ^ me) * 4 + ((row >> 1) & 3)
-    lane = lax.broadcasted_iota(jnp.int32, (width, table.shape[1]), 1)
-    pair = jnp.sum(jnp.where(lane == slot, table[...], 0), axis=1, keepdims=True)
+    lane = lax.broadcasted_iota(jnp.int32, (width, table_ref.shape[1]), 1)
+    pair = jnp.sum(jnp.where(lane == slot, table_ref[...], 0), axis=1, keepdims=True)
     column = jnp.where(row & 1 == 1, width - 1 - pair, pair)
     at = lax.broadcasted_iota(jnp.int32, (width, width), 1)
     onehot[...] = jnp.where(at == column, 1.0, 0.0).astype(jnp.bfloat16)
@@ -67,10 +65,10 @@
             early_refs[i + 1][1, :, lanes] = picked[16 + NEAR.index(d)]
 
     for i in range(parts):
-        copies[i + 1].wait()
+        copies[i].wait()
         x = wide[i * step : (i + 1) * step].reshape(step * WIDE, width)
         emit(x, pl.ds(i * step * WIDE, step * WIDE))
-    copies[parts + 1].wait()
+    copies[parts].wait()
     emit(rest[...].reshape(channels * REST, width), pl.ds(channels * WIDE, channels * REST))
 
 
@@ -81,18 +79,17 @@
     shapes = [(len(JOINED),) + block, (len(JOINED) + 1,) + block, block] + [(2,) + block] * len(EARLY)
     return pl.pallas_call(
         functools.partial(pick_kernel, early=early),
-        in_specs=[HBM] * 2,
+        in_specs=[VMEM, HBM],
         out_specs=[VMEM] * len(shapes),
         out_shape=[jax.ShapeDtypeStruct(s, jnp.bfloat16) for s in shapes],
         scratch_shapes=[
-            pltpu.VMEM((1, table.shape[0]), jnp.int32),
             pltpu.VMEM((channels, WIDE, width), jnp.bfloat16),
             pltpu.VMEM((channels, REST, width), jnp.bfloat16),
             pltpu.VMEM((width, width), jnp.bfloat16),
-            pltpu.SemaphoreType.DMA((5,)),
+            pltpu.SemaphoreType.DMA((4,)),
         ],
         compiler_params=pltpu.CompilerParams(vmem_limit_bytes=51 * 2**20),
-    )(table.reshape(1, -1), x)
+    )(table, x)
 
 
 def join_kernel(mine_ref, theirs_ref, *outs):
@@ -129,11 +126,11 @@
     )(*pieces)
 
 
-def transform_kernel(*refs, skip, far, width):
+def transform_kernel(*refs, skip, far, steps, width, added):
     table_ref, tables_ref, *refs = refs[skip:]
     if far:
-        blocks = [(r.at[0], r.at[1]) for r in refs[:8]]
-        before, out_ref, held = refs[8:]
+        blocks = [(r.at[0], r.at[1]) for r in refs[: 2 * len(steps)]]
+        refs = refs[2 * len(steps) :]
     else:
         own, theirs, one, two, three, changed = refs[:6]
         blocks = [
@@ -142,12 +139,14 @@
             (two.at[0], changed.at[0]),
             (three.at[0], changed.at[1]),
         ] + [(r.at[0], r.at[1]) for r in refs[6:10]]
-        out_ref, held = refs[10:]
+        refs = refs[10:]
+    before = refs[0] if added else None
+    out_ref, held = refs[-2:]
     me = here()
     core, z = (me >> 2) & 1, me & 3
     x = (me >> 3) & 1 ^ (1 if far else 0)
     sign = jnp.where(me < Y, 1.0, -1.0).astype(jnp.float32)
-    channels = held.shape[3] // 8
+    levs, channels = held.shape[2], held.shape[3] // 8
     whole = 2 * (WIDE + REST)
 
     def put(e, lev, row, lane, value):
@@ -155,12 +154,12 @@
             held[e, lane // 128 + i, lev, pl.ds(row, 8), :] = value[:, i * 128 : (i + 1) * 128]
 
     def stage(flip):
-        for j in range(4):
-            lev = z ^ j
+        for j, step in enumerate(steps):
+            lev = (z ^ step) & (levs - 1)
 
             def both(half, at, size):
                 a = blocks[j][half ^ flip][:, at : at + size].astype(jnp.float32)
-                b = blocks[4 + j][half ^ flip][:, at : at + size].astype(jnp.float32)
+                b = blocks[len(steps) + j][half ^ flip][:, at : at + size].astype(jnp.float32)
                 return a + b, (a - b) * sign
 
             for half in range(2):
@@ -178,44 +177,59 @@
     for flip in range(2):
         pl.when(core == flip)(functools.partial(stage, flip))
 
+    rows = levs * channels
+    low = (z ^ steps[0]) < levs
     lanes = pl.ds(pl.multiple_of(x * whole, 128), whole)
-    for e in range(2):
-        tiles = [held.at[e, i].reshape(4 * channels * 8, 128) for i in range(whole // 128)]
-        for s in range(4):
-            rows = [
-                jnp.concatenate([t[pl.ds(2 * s + w, 4 * channels, stride=8), :] for t in tiles], 1)
+    slot = lax.broadcasted_iota(jnp.int32, table_ref.shape, 1) - me * 4
+    for s in range(4):
+        pair = jnp.sum(jnp.where(slot == s, table_ref[...], 0), axis=1, keepdims=True)
+        for e in range(2):
+            tiles = [held.at[e, i].reshape(rows * 8, 128) for i in range(whole // 128)]
+            picked = [
+                jnp.concatenate([t[pl.ds(2 * s + w, rows, stride=8), :] for t in tiles], 1)
                 for w in range(2)
             ]
             products = lax.dot_general(
-                jnp.concatenate(rows, 0).astype(jnp.bfloat16),
+                jnp.concatenate(picked, 0).astype(jnp.bfloat16),
                 tables_ref[s, e, :, lanes],
                 NT,
                 preferred_element_type=jnp.float32,
             )
-            count = (width - table_ref[me * 4 + s] - e + 1) // 2
-            one, two = products[: 4 * channels], products[4 * channels :]
-            degree = lax.broadcasted_iota(jnp.int32, one.shape, 1)
-            chosen = jnp.where(degree < count, one, two)
-            if far:
+            count = (width - pair - e + 1) >> 1
+            degree = lax.broadcasted_iota(jnp.int32, (rows, products.shape[1]), 1)
+            chosen = jnp.where(degree < count, products[:rows], products[rows:])
+            if levs < 4:
+                parts = [jnp.where(low, chosen, 0.0), jnp.where(low, 0.0, chosen)]
+                chosen = jnp.concatenate(parts, 0)
+            if added:
                 chosen = chosen + before[s, e]
             out_ref[s, e] = chosen.astype(out_ref.dtype)
 
 
-def transform(table, tables, blocks, far, width, rest=()):
+def transform(table, tables, blocks, far, steps, width, before=None, last=False, rest=()):
     slots, _, degrees, lats = tables.shape
     channels = blocks[0].shape[-1] // (WIDE + REST)
-    return pl.pallas_call(
-        functools.partial(transform_kernel, skip=len(rest), far=far, width=width),
-        in_specs=[pl.BlockSpec(memory_space=pl.ANY)] * len(rest) + [SMEM] + [VMEM] * (1 + len(blocks)),
+    more = [] if before is None else [before]
+    return pl.pallas_call(
+        functools.partial(
+            transform_kernel,
+            skip=len(rest),
+            far=far,
+            steps=steps,
+            width=width,
+            added=before is not None,
+        ),
+        in_specs=[pl.BlockSpec(memory_space=pl.ANY)] * len(rest)
+        + [VMEM] * (2 + len(blocks) + len(more)),
         out_specs=VMEM,
         out_shape=jax.ShapeDtypeStruct(
-            (slots, 2, 4 * channels, degrees), jnp.bfloat16 if far else jnp.float32
+            (slots, 2, 4 * channels, degrees), jnp.bfloat16 if last else jnp.float32
         ),
         scratch_shapes=[
-            pltpu.VMEM((2, 2 * (WIDE + REST) // 128, 4, channels * 8, 128), jnp.float32)
+            pltpu.VMEM((2, 2 * (WIDE + REST) // 128, len(steps), channels * 8, 128), jnp.float32)
         ],
         compiler_params=pltpu.CompilerParams(vmem_limit_bytes=20 * 2**20),
-    )(*rest, table, tables, *blocks)
+    )(*rest, table, tables, *blocks, *more)
 
 
 def send(piece, distance):
@@ -225,7 +239,8 @@
 
 def on_block(fourier, table, legendre):
     width = fourier.shape[2]
-    mine, theirs, own, *early = pick(table, fourier.transpose(1, 0, 2))
+    entries = table.reshape(1, -1)
+    mine, theirs, own, *early = pick(entries, fourier.transpose(1, 0, 2))
     got = {d: send(piece, d) for d, piece in zip(EARLY, early)}
     theirs = send(theirs, CORE)
     ready = dict(zip(JOINED, join(mine, theirs)))
@@ -234,9 +249,11 @@
     *came, got[1] = lax.optimization_barrier((*came, got[1]))
     changed = send(second_blocks(*came), CORE)
     near = [own, theirs] + [got[d] for d in NEAR[1:4]] + [changed] + [got[d] for d in NEAR[4:]]
-    partial = transform(table, legendre, near, False, width)
-    far = [got[d] for d in FAR] + [partial]
-    return transform(table, legendre, far, True, width, list(got.values()))
+    total = transform(entries, legendre, near, False, (0, 1, 2, 3), width)
+    far = [got[d] for d in FAR]
+    return transform(
+        entries, legendre, far, True, (0, 1, 2, 3), width, total, True, list(got.values())
+    )
 
 
 def row_counts(table, slot_count, wavenumbers):

time: 55.3 us -> 54.2 us (0.980)
  starting transfers between devices: 32.9 us -> 35.7 us
  waiting for transfers between devices: 14.7 us -> 11.9 us
  Pallas kernels: 6.42 us -> 5.34 us
    ppermute x17, waiting for transfers between devices: 14.7 us -> 11.9 us  [send(): lax.ppermute(piece, ('lat', 'lev'), [(i, i ^ distance) for i in range(cou...]
    ppermute x17, starting transfers between devices: 32.9 us -> 35.7 us  [send(): lax.ppermute(piece, ('lat', 'lev'), [(i, i ^ distance) for i in range(cou...]
    pallas_call x2, Pallas kernels: 3.77 us -> 2.61 us  [transform(): pl.pallas_call(functools.partial(transform_kernel, skip=len(rest), far=fa...]
  transfers between devices with their start and end apart: 17 -> 17, of which waited for: 3 -> 5; matrix products, arithmetic and copies ran while one was open for 1% -> 1% of each run, Pallas kernels for 3% -> 2%
where the time goes in v3:
time: 54.2 us; the launch traced here: 54 us
  starting transfers between devices  35.7 us (66%)
  waiting for transfers between devices  11.9 us (22%)
  Pallas kernels  5.34 us (10%)
  local copies, waits for them, and re-layouts  1.01 us (2%)
    ppermute x17, starting transfers between devices, send(): lax.ppermute(piece, ('lat', 'lev'), [(i, i ^ distance) for i in range(cou...  35.7 us
    ppermute x17, waiting for transfers between devices, send(): lax.ppermute(piece, ('lat', 'lev'), [(i, i ^ distance) for i in range(cou...  11.9 us
    pallas_call x1, Pallas kernels, pick(): pl.pallas_call(functools.partial(pick_kernel, early=early), in_specs=[VME...  2.61 us
    pallas_call x2, Pallas kernels, transform(): pl.pallas_call(functools.partial(transform_kernel, skip=len(rest), far=fa...  2.61 us
  transfers between devices with their start and end apart: 17, of which 5 were waited for; matrix products, arithmetic and copies ran while one was open for 1% of the time, Pallas kernels for 2%

profile of v3, /device:TPU:0, one launch (start us, length us, event | category | flops | bytes accessed | tf_op | source)
XLA Modules:
  0.0 54.0 jit_solution(1862318094402502553)
XLA Ops:
  0.0 0.7 %copy-done = s32[128]{0:T(128)S(1)} copy-done((s32[128]{0:T(128)S(1)}, s32[128]{0:T(128)}, u32[]{:S(2)}) %copy-start) | copy-done | bytes 536
  0.7 2.6 %shard_map.37 = (bf16[13,8,3840]{2,1,0:T(8,128)(2,1)S(1)}, bf16[14,8,3840]{2,1,0:T(8,128)(2,1)S(1)}, bf16[8,3840]{1,0:T(8,128)(2,1)S(1)}, bf16[2,8,3840]{2,1,0:T(8,128)(2,1)S(1)}, bf16[2,8,3840]{2,1,0:T(8,128)(2,1)S(1)}) custom-call(s32[1,128]{1,0:T(1,128)S(1)} %bitcast.2, bf16[12,320,256]{2,1,0:T(8,128)(2,1)} %bitcast.5), custom_call_target="tpu_custom_call" | custom-call | tf_op jit(solution)/shard_map/pallas_call | solution.py:80
  3.3 0.5 collective-permute-start.2
  3.8 3.7 %collective-permute-start = (bf16[2,8,3840]{2,1,0:T(8,128)(2,1)S(1)}, bf16[2,8,3840]{2,1,0:T(8,128)(2,1)S(1)}, u32[]{:S(2)}, u32[]{:S(2)}) collective-permute-start(bf16[2,8,3840]{2,1,0:T(8,128)(2,1)S(1)} %get-tuple-element.26), channel_id=1, source_target_pairs={{0,2},{1,3},{2,0},{3,1},{4,6},{5,7},{6,4},{7,5},{8,10},{9,11},{10,... | collective-permute-start | bytes 368648 | tf_op jit(solution)/shard_map/ppermute | solution.py:237
  7.5 1.3 %collective-permute-start.1 = (bf16[2,8,3840]{2,1,0:T(8,128)(2,1)S(1)}, bf16[2,8,3840]{2,1,0:T(8,128)(2,1)S(1)}, u32[]{:S(2)}, u32[]{:S(2)}) collective-permute-start(bf16[2,8,3840]{2,1,0:T(8,128)(2,1)S(1)} %get-tuple-element.27), channel_id=1, source_target_pairs={{0,3},{1,2},{2,1},{3,0},{4,7},{5,6},{6,5},{7,4},{8,11},{9,10},{10,... | collective-permute-start | bytes 368648 | tf_op jit(solution)/shard_map/ppermute | solution.py:237
  8.8 0.1 shard_map.38
  8.9 0.3 collective-permute-start.3
  9.2 1.5 %collective-permute-start.4 = (bf16[2,8,3840]{2,1,0:T(8,128)(2,1)S(1)}, bf16[2,8,3840]{2,1,0:T(8,128)(2,1)S(1)}, u32[]{:S(2)}, u32[]{:S(2)}) collective-permute-start(bf16[2,8,3840]{2,1,0:T(8,128)(2,1)S(1)} %get-tuple-element.32), channel_id=1, source_target_pairs={{0,16},{1,17},{2,18},{3,19},{4,20},{5,21},{6,22},{7,23},{8,24},{9,... | collective-permute-start | bytes 368648 | tf_op jit(solution)/shard_map/ppermute | solution.py:237
  10.7 2.8 %collective-permute-start.5 = (bf16[2,8,3840]{2,1,0:T(8,128)(2,1)S(1)}, bf16[2,8,3840]{2,1,0:T(8,128)(2,1)S(1)}, u32[]{:S(2)}, u32[]{:S(2)}) collective-permute-start(bf16[2,8,3840]{2,1,0:T(8,128)(2,1)S(1)} %get-tuple-element.33), channel_id=1, source_target_pairs={{0,18},{1,19},{2,16},{3,17},{4,22},{5,23},{6,20},{7,21},{8,26},{9,... | collective-permute-start | bytes 368648 | tf_op jit(solution)/shard_map/ppermute | solution.py:237
  13.5 3.5 %collective-permute-done.refs_0_.refs_5_ = bf16[2,8,3840]{2,1,0:T(8,128)(2,1)S(1)} collective-permute-done((bf16[2,8,3840]{2,1,0:T(8,128)(2,1)S(1)}, bf16[2,8,3840]{2,1,0:T(8,128)(2,1)S(1)}, u32[]{:S(2)}, u32[]{:S(2)}) %collective-permute-start) | collective-permute-done | bytes 122912 | tf_op jit(solution)/shard_map/ppermute | solution.py:237
  17.0 1.7 %collective-permute-start.6 = (bf16[2,8,3840]{2,1,0:T(8,128)(2,1)S(1)}, bf16[2,8,3840]{2,1,0:T(8,128)(2,1)S(1)}, u32[]{:S(2)}, u32[]{:S(2)}) collective-permute-start(bf16[2,8,3840]{2,1,0:T(8,128)(2,1)S(1)} %get-tuple-element.34), channel_id=1, source_target_pairs={{0,17},{1,16},{2,19},{3,18},{4,21},{5,20},{6,23},{7,22},{8,25},{9,... | collective-permute-start | bytes 368648 | tf_op jit(solution)/shard_map/ppermute | solution.py:237
  18.7 0.0 collective-permute-done.1.refs_1_.refs_6_
  18.7 3.0 %collective-permute-start.7 = (bf16[2,8,3840]{2,1,0:T(8,128)(2,1)S(1)}, bf16[2,8,3840]{2,1,0:T(8,128)(2,1)S(1)}, u32[]{:S(2)}, u32[]{:S(2)}) collective-permute-start(bf16[2,8,3840]{2,1,0:T(8,128)(2,1)S(1)} %get-tuple-element.35), channel_id=1, source_target_pairs={{0,19},{1,18},{2,17},{3,16},{4,23},{5,22},{6,21},{7,20},{8,27},{9,... | collective-permute-start | bytes 368648 | tf_op jit(solution)/shard_map/ppermute | solution.py:237
  21.7 0.0 collective-permute-done.3.refs_4_.refs_2_
  21.7 1.5 %collective-permute-start.8 = (bf16[2,8,3840]{2,1,0:T(8,128)(2,1)S(1)}, bf16[2,8,3840]{2,1,0:T(8,128)(2,1)S(1)}, u32[]{:S(2)}, u32[]{:S(2)}) collective-permute-start(bf16[2,8,3840]{2,1,0:T(8,128)(2,1)S(1)} %get-tuple-element.36), channel_id=1, source_target_pairs={{0,8},{1,9},{2,10},{3,11},{4,12},{5,13},{6,14},{7,15},{8,0},{9,1},... | collective-permute-start | bytes 368648 | tf_op jit(solution)/shard_map/ppermute | solution.py:237
  23.2 3.7 %collective-permute-start.9 = (bf16[2,8,3840]{2,1,0:T(8,128)(2,1)S(1)}, bf16[2,8,3840]{2,1,0:T(8,128)(2,1)S(1)}, u32[]{:S(2)}, u32[]{:S(2)}) collective-permute-start(bf16[2,8,3840]{2,1,0:T(8,128)(2,1)S(1)} %get-tuple-element.37), channel_id=1, source_target_pairs={{0,10},{1,11},{2,8},{3,9},{4,14},{5,15},{6,12},{7,13},{8,2},{9,3},... | collective-permute-start | bytes 368648 | tf_op jit(solution)/shard_map/ppermute | solution.py:237
  26.9 1.5 %collective-permute-done.5.refs_10_.refs_4_ = bf16[2,8,3840]{2,1,0:T(8,128)(2,1)S(1)} collective-permute-done((bf16[2,8,3840]{2,1,0:T(8,128)(2,1)S(1)}, bf16[2,8,3840]{2,1,0:T(8,128)(2,1)S(1)}, u32[]{:S(2)}, u32[]{:S(2)}) %collective-permute-start.5) | collective-permute-done | bytes 122912 | tf_op jit(solution)/shard_map/ppermute | solution.py:237
  28.4 1.8 %collective-permute-start.10 = (bf16[2,8,3840]{2,1,0:T(8,128)(2,1)S(1)}, bf16[2,8,3840]{2,1,0:T(8,128)(2,1)S(1)}, u32[]{:S(2)}, u32[]{:S(2)}) collective-permute-start(bf16[2,8,3840]{2,1,0:T(8,128)(2,1)S(1)} %get-tuple-element.38), channel_id=1, source_target_pairs={{0,9},{1,8},{2,11},{3,10},{4,13},{5,12},{6,15},{7,14},{8,1},{9,0},... | collective-permute-start | bytes 368648 | tf_op jit(solution)/shard_map/ppermute | solution.py:237
  30.3 0.1 collective-permute-start.16
  30.4 0.0 collective-permute-done.7.refs_11_.refs_6_
  30.4 4.3 %collective-permute-start.11 = (bf16[2,8,3840]{2,1,0:T(8,128)(2,1)S(1)}, bf16[2,8,3840]{2,1,0:T(8,128)(2,1)S(1)}, u32[]{:S(2)}, u32[]{:S(2)}) collective-permute-start(bf16[2,8,3840]{2,1,0:T(8,128)(2,1)S(1)} %get-tuple-element.39), channel_id=1, source_target_pairs={{0,11},{1,10},{2,9},{3,8},{4,15},{5,14},{6,13},{7,12},{8,3},{9,2},... | collective-permute-start | bytes 368648 | tf_op jit(solution)/shard_map/ppermute | solution.py:237
  34.7 0.0 collective-permute-done.8.refs_7_.refs_17_
  34.7 0.1 collective-permute-start.12
  34.7 1.4 %collective-permute-done.9.refs_8_.refs_19_ = bf16[2,8,3840]{2,1,0:T(8,128)(2,1)S(1)} collective-permute-done((bf16[2,8,3840]{2,1,0:T(8,128)(2,1)S(1)}, bf16[2,8,3840]{2,1,0:T(8,128)(2,1)S(1)}, u32[]{:S(2)}, u32[]{:S(2)}) %collective-permute-start.9) | collective-permute-done | bytes 122912 | tf_op jit(solution)/shard_map/ppermute | solution.py:237
  36.2 2.9 %collective-permute-start.13 = (bf16[2,8,3840]{2,1,0:T(8,128)(2,1)S(1)}, bf16[2,8,3840]{2,1,0:T(8,128)(2,1)S(1)}, u32[]{:S(2)}, u32[]{:S(2)}) collective-permute-start(bf16[2,8,3840]{2,1,0:T(8,128)(2,1)S(1)} %get-tuple-element.41), channel_id=1, source_target_pairs={{0,26},{1,27},{2,24},{3,25},{4,30},{5,31},{6,28},{7,29},{8,18},{9,... | collective-permute-start | bytes 368648 | tf_op jit(solution)/shard_map/ppermute | solution.py:237
  39.0 3.2 %collective-permute-start.14 = (bf16[2,8,3840]{2,1,0:T(8,128)(2,1)S(1)}, bf16[2,8,3840]{2,1,0:T(8,128)(2,1)S(1)}, u32[]{:S(2)}, u32[]{:S(2)}) collective-permute-start(bf16[2,8,3840]{2,1,0:T(8,128)(2,1)S(1)} %get-tuple-element.42), channel_id=1, source_target_pairs={{0,25},{1,24},{2,27},{3,26},{4,29},{5,28},{6,31},{7,30},{8,17},{9,... | collective-permute-start | bytes 368648 | tf_op jit(solution)/shard_map/ppermute | solution.py:237
  42.2 3.3 %collective-permute-start.15 = (bf16[2,8,3840]{2,1,0:T(8,128)(2,1)S(1)}, bf16[2,8,3840]{2,1,0:T(8,128)(2,1)S(1)}, u32[]{:S(2)}, u32[]{:S(2)}) collective-permute-start(bf16[2,8,3840]{2,1,0:T(8,128)(2,1)S(1)} %get-tuple-element.43), channel_id=1, source_target_pairs={{0,27},{1,26},{2,25},{3,24},{4,31},{5,30},{6,29},{7,28},{8,19},{9,... | collective-permute-start | bytes 368648 | tf_op jit(solution)/shard_map/ppermute | solution.py:237
  45.5 0.3 copy.5.refs_1_.refs_16_
  45.9 1.0 %shard_map.40.refs_25_ = f32[4,2,48,129]{3,2,1,0:T(8,128)S(1)} custom-call(s32[1,128]{1,0:T(1,128)S(1)} %bitcast.3, bf16[4,2,129,1280]{3,2,1,0:T(8,128)(2,1)S(1)} %copy.5.refs_1_.refs_16_, bf16[8,3840]{1,0:T(8,128)(2,1)S(1)} %get-tuple-element.44.refs_2_, bf16[14,8,3840]{2,1,0:T(8,128)(2,1)S(1)} %collective-permute-done.2.theirs_ref.refs_3_, ...), custom_call_target="tpu_custom_call" | custom-call | tf_op jit(solution)/shard_map/pallas_call | solution.py:213
  46.8 1.3 %collective-permute-done.12.refs_11_.refs_21_ = bf16[2,8,3840]{2,1,0:T(8,128)(2,1)S(1)} collective-permute-done((bf16[2,8,3840]{2,1,0:T(8,128)(2,1)S(1)}, bf16[2,8,3840]{2,1,0:T(8,128)(2,1)S(1)}, u32[]{:S(2)}, u32[]{:S(2)}) %collective-permute-start.12) | collective-permute-done | bytes 122912 | tf_op jit(solution)/shard_map/ppermute | solution.py:237
  48.1 4.2 %collective-permute-done.15.refs_14_.refs_24_ = bf16[2,8,3840]{2,1,0:T(8,128)(2,1)S(1)} collective-permute-done((bf16[2,8,3840]{2,1,0:T(8,128)(2,1)S(1)}, bf16[2,8,3840]{2,1,0:T(8,128)(2,1)S(1)}, u32[]{:S(2)}, u32[]{:S(2)}) %collective-permute-start.15) | collective-permute-done | bytes 122912 | tf_op jit(solution)/shard_map/ppermute | solution.py:237
  52.4 1.7 %shard_map.41 = bf16[4,2,48,129]{3,2,1,0:T(8,128)(2,1)} custom-call(bf16[2,8,3840]{2,1,0:T(8,128)(2,1)S(1)} %collective-permute-done.refs_0_.refs_5_, bf16[2,8,3840]{2,1,0:T(8,128)(2,1)S(1)} %collective-permute-done.1.refs_1_.refs_6_, bf16[2,8,3840]{2,1,0:T(8,128)(2,1)S(1)} %collective-permute-done.3.refs_4_.refs_2_, ...), custom_call_target="tpu_custom_call" | custom-call | tf_op jit(solution)/shard_map/pallas_call | solution.py:213
  (12 shorter events, 0.0 us)
Async XLA Ops:
  0.0 0.7 %copy-start = (s32[128]{0:T(128)S(1)}, s32[128]{0:T(128)}, u32[]{:S(2)}) copy-start(s32[128]{0:T(128)} %param.4) | copy-start | bytes 1540
  0.7 44.9 %copy-start.1 = (bf16[4,2,129,1280]{3,1,2,0:T(2,128)(2,1)S(1)}, bf16[4,2,129,1280]{3,1,2,0:T(2,128)(2,1)}, u32[]{:S(2)}) copy-start(bf16[4,2,129,1280]{3,1,2,0:T(2,128)(2,1)} %param.5) | copy-start | bytes 7925764
  3.3 5.5 %collective-permute-start.2 = (bf16[14,8,3840]{2,1,0:T(8,128)(2,1)S(1)}, bf16[14,8,3840]{2,1,0:T(8,128)(2,1)S(1)}, u32[]{:S(2)}, u32[]{:S(2)}) collective-permute-start(bf16[14,8,3840]{2,1,0:T(8,128)(2,1)S(1)} %get-tuple-element.29), channel_id=1, source_target_pairs={{0,4},{1,5},{2,6},{3,7},{4,0},{5,1},{6,2},{7,3},{8,12},{9,13},{10,... | collective-permute-start | bytes 2580488 | tf_op jit(solution)/shard_map/ppermute | solution.py:237
  3.8 13.1 %collective-permute-start = (bf16[2,8,3840]{2,1,0:T(8,128)(2,1)S(1)}, bf16[2,8,3840]{2,1,0:T(8,128)(2,1)S(1)}, u32[]{:S(2)}, u32[]{:S(2)}) collective-permute-start(bf16[2,8,3840]{2,1,0:T(8,128)(2,1)S(1)} %get-tuple-element.26), channel_id=1, source_target_pairs={{0,2},{1,3},{2,0},{3,1},{4,6},{5,7},{6,4},{7,5},{8,10},{9,11},{10,... | collective-permute-start | bytes 368648 | tf_op jit(solution)/shard_map/ppermute | solution.py:237
  7.5 11.2 %collective-permute-start.1 = (bf16[2,8,3840]{2,1,0:T(8,128)(2,1)S(1)}, bf16[2,8,3840]{2,1,0:T(8,128)(2,1)S(1)}, u32[]{:S(2)}, u32[]{:S(2)}) collective-permute-start(bf16[2,8,3840]{2,1,0:T(8,128)(2,1)S(1)} %get-tuple-element.27), channel_id=1, source_target_pairs={{0,3},{1,2},{2,1},{3,0},{4,7},{5,6},{6,5},{7,4},{8,11},{9,10},{10,... | collective-permute-start | bytes 368648 | tf_op jit(solution)/shard_map/ppermute | solution.py:237
  8.9 12.8 %collective-permute-start.3 = (bf16[2,8,3840]{2,1,0:T(8,128)(2,1)S(1)}, bf16[2,8,3840]{2,1,0:T(8,128)(2,1)S(1)}, u32[]{:S(2)}, u32[]{:S(2)}) collective-permute-start(bf16[2,8,3840]{2,1,0:T(8,128)(2,1)S(1)} %get-tuple-element.30), channel_id=1, source_target_pairs={{0,1},{1,0},{2,3},{3,2},{4,5},{5,4},{6,7},{7,6},{8,9},{9,8},{10,11... | collective-permute-start | bytes 368648 | tf_op jit(solution)/shard_map/ppermute | solution.py:237
  9.2 14.0 %collective-permute-start.4 = (bf16[2,8,3840]{2,1,0:T(8,128)(2,1)S(1)}, bf16[2,8,3840]{2,1,0:T(8,128)(2,1)S(1)}, u32[]{:S(2)}, u32[]{:S(2)}) collective-permute-start(bf16[2,8,3840]{2,1,0:T(8,128)(2,1)S(1)} %get-tuple-element.32), channel_id=1, source_target_pairs={{0,16},{1,17},{2,18},{3,19},{4,20},{5,21},{6,22},{7,23},{8,24},{9,... | collective-permute-start | bytes 368648 | tf_op jit(solution)/shard_map/ppermute | solution.py:237
  10.7 17.7 %collective-permute-start.5 = (bf16[2,8,3840]{2,1,0:T(8,128)(2,1)S(1)}, bf16[2,8,3840]{2,1,0:T(8,128)(2,1)S(1)}, u32[]{:S(2)}, u32[]{:S(2)}) collective-permute-start(bf16[2,8,3840]{2,1,0:T(8,128)(2,1)S(1)} %get-tuple-element.33), channel_id=1, source_target_pairs={{0,18},{1,19},{2,16},{3,17},{4,22},{5,23},{6,20},{7,21},{8,26},{9,... | collective-permute-start | bytes 368648 | tf_op jit(solution)/shard_map/ppermute | solution.py:237
  17.0 13.3 %collective-permute-start.6 = (bf16[2,8,3840]{2,1,0:T(8,128)(2,1)S(1)}, bf16[2,8,3840]{2,1,0:T(8,128)(2,1)S(1)}, u32[]{:S(2)}, u32[]{:S(2)}) collective-permute-start(bf16[2,8,3840]{2,1,0:T(8,128)(2,1)S(1)} %get-tuple-element.34), channel_id=1, source_target_pairs={{0,17},{1,16},{2,19},{3,18},{4,21},{5,20},{6,23},{7,22},{8,25},{9,... | collective-permute-start | bytes 368648 | tf_op jit(solution)/shard_map/ppermute | solution.py:237
  18.7 11.7 %collective-permute-start.7 = (bf16[2,8,3840]{2,1,0:T(8,128)(2,1)S(1)}, bf16[2,8,3840]{2,1,0:T(8,128)(2,1)S(1)}, u32[]{:S(2)}, u32[]{:S(2)}) collective-permute-start(bf16[2,8,3840]{2,1,0:T(8,128)(2,1)S(1)} %get-tuple-element.35), channel_id=1, source_target_pairs={{0,19},{1,18},{2,17},{3,16},{4,23},{5,22},{6,21},{7,20},{8,27},{9,... | collective-permute-start | bytes 368648 | tf_op jit(solution)/shard_map/ppermute | solution.py:237
  21.7 13.0 %collective-permute-start.8 = (bf16[2,8,3840]{2,1,0:T(8,128)(2,1)S(1)}, bf16[2,8,3840]{2,1,0:T(8,128)(2,1)S(1)}, u32[]{:S(2)}, u32[]{:S(2)}) collective-permute-start(bf16[2,8,3840]{2,1,0:T(8,128)(2,1)S(1)} %get-tuple-element.36), channel_id=1, source_target_pairs={{0,8},{1,9},{2,10},{3,11},{4,12},{5,13},{6,14},{7,15},{8,0},{9,1},... | collective-permute-start | bytes 368648 | tf_op jit(solution)/shard_map/ppermute | solution.py:237
  23.2 12.9 %collective-permute-start.9 = (bf16[2,8,3840]{2,1,0:T(8,128)(2,1)S(1)}, bf16[2,8,3840]{2,1,0:T(8,128)(2,1)S(1)}, u32[]{:S(2)}, u32[]{:S(2)}) collective-permute-start(bf16[2,8,3840]{2,1,0:T(8,128)(2,1)S(1)} %get-tuple-element.37), channel_id=1, source_target_pairs={{0,10},{1,11},{2,8},{3,9},{4,14},{5,15},{6,12},{7,13},{8,2},{9,3},... | collective-permute-start | bytes 368648 | tf_op jit(solution)/shard_map/ppermute | solution.py:237
  28.4 10.6 %collective-permute-start.10 = (bf16[2,8,3840]{2,1,0:T(8,128)(2,1)S(1)}, bf16[2,8,3840]{2,1,0:T(8,128)(2,1)S(1)}, u32[]{:S(2)}, u32[]{:S(2)}) collective-permute-start(bf16[2,8,3840]{2,1,0:T(8,128)(2,1)S(1)} %get-tuple-element.38), channel_id=1, source_target_pairs={{0,9},{1,8},{2,11},{3,10},{4,13},{5,12},{6,15},{7,14},{8,1},{9,0},... | collective-permute-start | bytes 368648 | tf_op jit(solution)/shard_map/ppermute | solution.py:237
  30.3 11.9 %collective-permute-start.16 = (bf16[2,8,3840]{2,1,0:T(8,128)(2,1)S(1)}, bf16[2,8,3840]{2,1,0:T(8,128)(2,1)S(1)}, u32[]{:S(2)}, u32[]{:S(2)}) collective-permute-start(bf16[2,8,3840]{2,1,0:T(8,128)(2,1)S(1)} %shard_map.39), channel_id=1, source_target_pairs={{0,4},{1,5},{2,6},{3,7},{4,0},{5,1},{6,2},{7,3},{8,12},{9,13},{10,... | collective-permute-start | bytes 368648 | tf_op jit(solution)/shard_map/ppermute | solution.py:237
  30.4 16.4 %collective-permute-start.11 = (bf16[2,8,3840]{2,1,0:T(8,128)(2,1)S(1)}, bf16[2,8,3840]{2,1,0:T(8,128)(2,1)S(1)}, u32[]{:S(2)}, u32[]{:S(2)}) collective-permute-start(bf16[2,8,3840]{2,1,0:T(8,128)(2,1)S(1)} %get-tuple-element.39), channel_id=1, source_target_pairs={{0,11},{1,10},{2,9},{3,8},{4,15},{5,14},{6,13},{7,12},{8,3},{9,2},... | collective-permute-start | bytes 368648 | tf_op jit(solution)/shard_map/ppermute | solution.py:237
  34.7 13.5 %collective-permute-start.12 = (bf16[2,8,3840]{2,1,0:T(8,128)(2,1)S(1)}, bf16[2,8,3840]{2,1,0:T(8,128)(2,1)S(1)}, u32[]{:S(2)}, u32[]{:S(2)}) collective-permute-start(bf16[2,8,3840]{2,1,0:T(8,128)(2,1)S(1)} %get-tuple-element.40), channel_id=1, source_target_pairs={{0,24},{1,25},{2,26},{3,27},{4,28},{5,29},{6,30},{7,31},{8,16},{9,... | collective-permute-start | bytes 368648 | tf_op jit(solution)/shard_map/ppermute | solution.py:237
  36.2 12.0 %collective-permute-start.13 = (bf16[2,8,3840]{2,1,0:T(8,128)(2,1)S(1)}, bf16[2,8,3840]{2,1,0:T(8,128)(2,1)S(1)}, u32[]{:S(2)}, u32[]{:S(2)}) collective-permute-start(bf16[2,8,3840]{2,1,0:T(8,128)(2,1)S(1)} %get-tuple-element.41), channel_id=1, source_target_pairs={{0,26},{1,27},{2,24},{3,25},{4,30},{5,31},{6,28},{7,29},{8,18},{9,... | collective-permute-start | bytes 368648 | tf_op jit(solution)/shard_map/ppermute | solution.py:237
  39.0 9.1 %collective-permute-start.14 = (bf16[2,8,3840]{2,1,0:T(8,128)(2,1)S(1)}, bf16[2,8,3840]{2,1,0:T(8,128)(2,1)S(1)}, u32[]{:S(2)}, u32[]{:S(2)}) collective-permute-start(bf16[2,8,3840]{2,1,0:T(8,128)(2,1)S(1)} %get-tuple-element.42), channel_id=1, source_target_pairs={{0,25},{1,24},{2,27},{3,26},{4,29},{5,28},{6,31},{7,30},{8,17},{9,... | collective-permute-start | bytes 368648 | tf_op jit(solution)/shard_map/ppermute | solution.py:237
  42.2 10.1 %collective-permute-start.15 = (bf16[2,8,3840]{2,1,0:T(8,128)(2,1)S(1)}, bf16[2,8,3840]{2,1,0:T(8,128)(2,1)S(1)}, u32[]{:S(2)}, u32[]{:S(2)}) collective-permute-start(bf16[2,8,3840]{2,1,0:T(8,128)(2,1)S(1)} %get-tuple-element.43), channel_id=1, source_target_pairs={{0,27},{1,26},{2,25},{3,24},{4,31},{5,30},{6,29},{7,28},{8,19},{9,... | collective-permute-start | bytes 368648 | tf_op jit(solution)/shard_map/ppermute | solution.py:237

commit v4 on v3

--- a/solution.py
+++ b/solution.py
@@ -13,7 +13,7 @@
 Y, X, CORE = 16, 8, 4
 NEAR = (0, 1, 2, 3, Y, Y + 1, Y + 2, Y + 3)
 FAR = tuple(X + d for d in NEAR)
-EARLY = (2, 3)
+EARLY = (3, 2)
 JOINED = tuple(d for d in NEAR[1:] + FAR if d not in EARLY)
 ORDER = (1, 16, 18, 17, 19, 8, 10, 9, 11, 24, 26, 25, 27)
 WIDE, REST = 256, 64
@@ -23,25 +23,39 @@
     return lax.axis_index("lat") * lax.axis_size("lev") + lax.axis_index("lev")
 
 
-def pick_kernel(table_ref, x_ref, mine_ref, theirs_ref, *refs, early):
-    early_refs, (wide, rest, onehot, sems) = refs[:early], refs[early:]
-    width = onehot.shape[0]
-    channels = x_ref.shape[0]
-    me = here()
-    core = (me >> 2) & 1
+def load_kernel(x_ref, wide_ref, rest_ref, sems):
+    core = (here() >> 2) & 1
     first = pl.multiple_of(core * REST, REST)
     last = pl.multiple_of((1 - core) * WIDE, REST)
-    parts = 3
-    step = channels // parts
-    copies = []
-    for i in range(parts):
-        at = pl.ds(i * step, step)
-        copies.append(
-            pltpu.make_async_copy(x_ref.at[at, pl.ds(first, WIDE)], wide.at[at], sems.at[i])
-        )
-    copies.append(pltpu.make_async_copy(x_ref.at[:, pl.ds(last, REST)], rest, sems.at[parts]))
+    copies = [
+        pltpu.make_async_copy(x_ref.at[:, pl.ds(first, WIDE)], wide_ref, sems.at[0]),
+        pltpu.make_async_copy(x_ref.at[:, pl.ds(last, REST)], rest_ref, sems.at[1]),
+    ]
     for copy in copies:
         copy.start()
+    for copy in copies:
+        copy.wait()
+
+
+def load(x):
+    channels, _, width = x.shape
+    shapes = [(channels, WIDE, width), (channels, REST, width)]
+    return pl.pallas_call(
+        load_kernel,
+        in_specs=[HBM],
+        out_specs=[VMEM] * 2,
+        out_shape=[jax.ShapeDtypeStruct(s, x.dtype) for s in shapes],
+        scratch_shapes=[pltpu.SemaphoreType.DMA((2,))],
+        cost_estimate=pl.CostEstimate(flops=10**9, bytes_accessed=4 * x.size, transcendentals=0),
+        compiler_params=pltpu.CompilerParams(vmem_limit_bytes=51 * 2**20),
+    )(x)
+
+
+def pick_kernel(table_ref, wide_ref, rest_ref, mine_ref, theirs_ref, *refs, early):
+    early_refs, (onehot,) = refs[:early], refs[early:]
+    width = onehot.shape[0]
+    channels = wide_ref.shape[0]
+    me = here()
     row = lax.broadcasted_iota(jnp.int32, (width, 1), 0)
     block = row >> 3
     distance = ((block >> 2) & 1) * Y | ((block >> 3) & 1) * X | (block >> 4) * CORE | block & 3
@@ -64,12 +78,10 @@
             early_refs[i + 1][0, :, lanes] = picked[NEAR.index(d)]
             early_refs[i + 1][1, :, lanes] = picked[16 + NEAR.index(d)]
 
-    for i in range(parts):
-        copies[i].wait()
-        x = wide[i * step : (i + 1) * step].reshape(step * WIDE, width)
-        emit(x, pl.ds(i * step * WIDE, step * WIDE))
-    copies[parts].wait()
-    emit(rest[...].reshape(channels * REST, width), pl.ds(channels * WIDE, channels * REST))
+    for c in range(0, channels, 2):
+        x = wide_ref[c : c + 2].reshape(2 * WIDE, width)
+        emit(x, pl.ds(c * WIDE, 2 * WIDE))
+    emit(rest_ref[...].reshape(channels * REST, width), pl.ds(channels * WIDE, channels * REST))
 
 
 def pick(table, x):
@@ -79,17 +91,12 @@
     shapes = [(len(JOINED),) + block, (len(JOINED) + 1,) + block, block] + [(2,) + block] * len(EARLY)
     return pl.pallas_call(
         functools.partial(pick_kernel, early=early),
-        in_specs=[VMEM, HBM],
+        in_specs=[VMEM] * 3,
         out_specs=[VMEM] * len(shapes),
         out_shape=[jax.ShapeDtypeStruct(s, jnp.bfloat16) for s in shapes],
-        scratch_shapes=[
-            pltpu.VMEM((channels, WIDE, width), jnp.bfloat16),
-            pltpu.VMEM((channels, REST, width), jnp.bfloat16),
-            pltpu.VMEM((width, width), jnp.bfloat16),
-            pltpu.SemaphoreType.DMA((4,)),
-        ],
-        compiler_params=pltpu.CompilerParams(vmem_limit_bytes=51 * 2**20),
-    )(table, x)
+        scratch_shapes=[pltpu.VMEM((width, width), jnp.bfloat16)],
+        compiler_params=pltpu.CompilerParams(vmem_limit_bytes=16 * 2**20),
+    )(table, *load(x))
 
 
 def join_kernel(mine_ref, theirs_ref, *outs):
@@ -132,13 +139,10 @@
         blocks = [(r.at[0], r.at[1]) for r in refs[: 2 * len(steps)]]
         refs = refs[2 * len(steps) :]
     else:
-        own, theirs, one, two, three, changed = refs[:6]
-        blocks = [
-            (own, theirs.at[0]),
-            (one.at[0], one.at[1]),
-            (two.at[0], changed.at[0]),
-            (three.at[0], changed.at[1]),
-        ] + [(r.at[0], r.at[1]) for r in refs[6:10]]
+        own, theirs, changed = refs[:3]
+        blocks = [(own, theirs.at[0])]
+        for d, r in zip(NEAR[1:], refs[3:10]):
+            blocks.append((r.at[0], changed.at[EARLY.index(d)] if d in EARLY else r.at[1]))
         refs = refs[10:]
     before = refs[0] if added else None
     out_ref, held = refs[-2:]
@@ -246,9 +250,9 @@
     ready = dict(zip(JOINED, join(mine, theirs)))
     got.update({d: send(ready[d], d) for d in ORDER})
     came = [got[d] for d in EARLY]
-    *came, got[1] = lax.optimization_barrier((*came, got[1]))
+    *came, got[ORDER[0]] = lax.optimization_barrier((*came, got[ORDER[0]]))
     changed = send(second_blocks(*came), CORE)
-    near = [own, theirs] + [got[d] for d in NEAR[1:4]] + [changed] + [got[d] for d in NEAR[4:]]
+    near = [own, theirs, changed] + [got[d] for d in NEAR[1:]]
     total = transform(entries, legendre, near, False, (0, 1, 2, 3), width)
     far = [got[d] for d in FAR]
     return transform(

time: 54.2 us -> 52.3 us (0.965)
  waiting for transfers between devices: 11.9 us -> 11 us
  local copies, waits for them, and re-layouts: 1.01 us -> 0.36 us
    pallas_call x1, Pallas kernels: 2.61 us -> 0.79 us  [pick(): pl.pallas_call(functools.partial(pick_kernel, early=early), in_specs=[VME...]
    pallas_call x0 -> x1, Pallas kernels: none -> 1.5 us  [load(): pl.pallas_call(load_kernel, in_specs=[HBM], out_specs=[VMEM] * 2, out_sha...]
    ppermute x17, waiting for transfers between devices: 11.9 us -> 11 us  [send(): lax.ppermute(piece, ('lat', 'lev'), [(i, i ^ distance) for i in range(cou...]
    unnamed x5, local copies, waits for them, and re-layouts: 1.01 us -> 0.36 us
  transfers between devices with their start and end apart: 17 -> 17, of which waited for: 5 -> 6; matrix products, arithmetic and copies ran while one was open for 1% -> 1% of each run, Pallas kernels for 2% -> 2%
where the time goes in v4:
time: 52.3 us; the launch traced here: 52.2 us
  starting transfers between devices  35.7 us (68%)
  waiting for transfers between devices  11 us (21%)
  Pallas kernels  5.02 us (10%)
    ppermute x17, starting transfers between devices, send(): lax.ppermute(piece, ('lat', 'lev'), [(i, i ^ distance) for i in range(cou...  35.7 us
    ppermute x17, waiting for transfers between devices, send(): lax.ppermute(piece, ('lat', 'lev'), [(i, i ^ distance) for i in range(cou...  11 us
    pallas_call x2, Pallas kernels, transform(): pl.pallas_call(functools.partial(transform_kernel, skip=len(rest), far=fa...  2.62 us
    pallas_call x1, Pallas kernels, load(): pl.pallas_call(load_kernel, in_specs=[HBM], out_specs=[VMEM] * 2, out_sha...  1.5 us
  transfers between devices with their start and end apart: 17, of which 6 were waited for; matrix products, arithmetic and copies ran while one was open for 1% of the time, Pallas kernels for 2%

profile of v4, /device:TPU:0, one launch (start us, length us, event | category | flops | bytes accessed | tf_op | source)
XLA Modules:
  0.0 52.2 jit_solution(17454824147701706502)
XLA Ops:
  0.0 1.5 %shard_map.37 = (bf16[12,256,256]{2,1,0:T(8,128)(2,1)S(1)}, bf16[12,64,256]{2,1,0:T(8,128)(2,1)S(1)}) custom-call(bf16[12,320,256]{2,1,0:T(8,128)(2,1)} %bitcast.5), custom_call_target="tpu_custom_call" | custom-call | flops 1000000000 | bytes 3932160 | tf_op jit(solution)/shard_map/pallas_call | solution.py:43
  1.5 0.0 copy-start.1
  1.5 0.8 %shard_map.38 = (bf16[13,8,3840]{2,1,0:T(8,128)(2,1)S(1)}, bf16[14,8,3840]{2,1,0:T(8,128)(2,1)S(1)}, bf16[8,3840]{1,0:T(8,128)(2,1)S(1)}, bf16[2,8,3840]{2,1,0:T(8,128)(2,1)S(1)}, bf16[2,8,3840]{2,1,0:T(8,128)(2,1)S(1)}) custom-call(s32[1,128]{1,0:T(1,128)S(1)} %bitcast.2, bf16[12,256,256]{2,1,0:T(8,128)(2,1)S(1)} %get-tuple-element.28.wide_ref, ...), custom_call_target="tpu_custom_call" | custom-call | tf_op jit(solution)/shard_map/pallas_call | solution.py:92
  2.3 0.5 collective-permute-start.2
  2.8 4.7 %collective-permute-start = (bf16[2,8,3840]{2,1,0:T(8,128)(2,1)S(1)}, bf16[2,8,3840]{2,1,0:T(8,128)(2,1)S(1)}, u32[]{:S(2)}, u32[]{:S(2)}) collective-permute-start(bf16[2,8,3840]{2,1,0:T(8,128)(2,1)S(1)} %get-tuple-element.30), channel_id=1, source_target_pairs={{0,3},{1,2},{2,1},{3,0},{4,7},{5,6},{6,5},{7,4},{8,11},{9,10},{10,... | collective-permute-start | bytes 368648 | tf_op jit(solution)/shard_map/ppermute | solution.py:241
  7.5 0.1 shard_map.39
  7.6 0.7 %collective-permute-start.3 = (bf16[2,8,3840]{2,1,0:T(8,128)(2,1)S(1)}, bf16[2,8,3840]{2,1,0:T(8,128)(2,1)S(1)}, u32[]{:S(2)}, u32[]{:S(2)}) collective-permute-start(bf16[2,8,3840]{2,1,0:T(8,128)(2,1)S(1)} %get-tuple-element.34), channel_id=1, source_target_pairs={{0,1},{1,0},{2,3},{3,2},{4,5},{5,4},{6,7},{7,6},{8,9},{9,8},{10,11... | collective-permute-start | bytes 368648 | tf_op jit(solution)/shard_map/ppermute | solution.py:241
  8.3 1.7 %collective-permute-start.4 = (bf16[2,8,3840]{2,1,0:T(8,128)(2,1)S(1)}, bf16[2,8,3840]{2,1,0:T(8,128)(2,1)S(1)}, u32[]{:S(2)}, u32[]{:S(2)}) collective-permute-start(bf16[2,8,3840]{2,1,0:T(8,128)(2,1)S(1)} %get-tuple-element.36), channel_id=1, source_target_pairs={{0,16},{1,17},{2,18},{3,19},{4,20},{5,21},{6,22},{7,23},{8,24},{9,... | collective-permute-start | bytes 368648 | tf_op jit(solution)/shard_map/ppermute | solution.py:241
  10.0 2.2 %collective-permute-start.5 = (bf16[2,8,3840]{2,1,0:T(8,128)(2,1)S(1)}, bf16[2,8,3840]{2,1,0:T(8,128)(2,1)S(1)}, u32[]{:S(2)}, u32[]{:S(2)}) collective-permute-start(bf16[2,8,3840]{2,1,0:T(8,128)(2,1)S(1)} %get-tuple-element.37), channel_id=1, source_target_pairs={{0,18},{1,19},{2,16},{3,17},{4,22},{5,23},{6,20},{7,21},{8,26},{9,... | collective-permute-start | bytes 368648 | tf_op jit(solution)/shard_map/ppermute | solution.py:241
  12.2 0.0 collective-permute-done.refs_0_.refs_7_
  12.2 5.7 %collective-permute-start.6 = (bf16[2,8,3840]{2,1,0:T(8,128)(2,1)S(1)}, bf16[2,8,3840]{2,1,0:T(8,128)(2,1)S(1)}, u32[]{:S(2)}, u32[]{:S(2)}) collective-permute-start(bf16[2,8,3840]{2,1,0:T(8,128)(2,1)S(1)} %get-tuple-element.38), channel_id=1, source_target_pairs={{0,17},{1,16},{2,19},{3,18},{4,21},{5,20},{6,23},{7,22},{8,25},{9,... | collective-permute-start | bytes 368648 | tf_op jit(solution)/shard_map/ppermute | solution.py:241
  17.8 3.8 %collective-permute-done.1.refs_1_.refs_6_ = bf16[2,8,3840]{2,1,0:T(8,128)(2,1)S(1)} collective-permute-done((bf16[2,8,3840]{2,1,0:T(8,128)(2,1)S(1)}, bf16[2,8,3840]{2,1,0:T(8,128)(2,1)S(1)}, u32[]{:S(2)}, u32[]{:S(2)}) %collective-permute-start.1) | collective-permute-done | bytes 122912 | tf_op jit(solution)/shard_map/ppermute | solution.py:241
  21.7 3.3 %collective-permute-start.7 = (bf16[2,8,3840]{2,1,0:T(8,128)(2,1)S(1)}, bf16[2,8,3840]{2,1,0:T(8,128)(2,1)S(1)}, u32[]{:S(2)}, u32[]{:S(2)}) collective-permute-start(bf16[2,8,3840]{2,1,0:T(8,128)(2,1)S(1)} %get-tuple-element.39), channel_id=1, source_target_pairs={{0,19},{1,18},{2,17},{3,16},{4,23},{5,22},{6,21},{7,20},{8,27},{9,... | collective-permute-start | bytes 368648 | tf_op jit(solution)/shard_map/ppermute | solution.py:241
  25.0 0.0 collective-permute-done.3.refs_5_.refs_2_
  25.0 1.5 %collective-permute-start.8 = (bf16[2,8,3840]{2,1,0:T(8,128)(2,1)S(1)}, bf16[2,8,3840]{2,1,0:T(8,128)(2,1)S(1)}, u32[]{:S(2)}, u32[]{:S(2)}) collective-permute-start(bf16[2,8,3840]{2,1,0:T(8,128)(2,1)S(1)} %get-tuple-element.40), channel_id=1, source_target_pairs={{0,8},{1,9},{2,10},{3,11},{4,12},{5,13},{6,14},{7,15},{8,0},{9,1},... | collective-permute-start | bytes 368648 | tf_op jit(solution)/shard_map/ppermute | solution.py:241
  26.5 2.9 %collective-permute-start.10 = (bf16[2,8,3840]{2,1,0:T(8,128)(2,1)S(1)}, bf16[2,8,3840]{2,1,0:T(8,128)(2,1)S(1)}, u32[]{:S(2)}, u32[]{:S(2)}) collective-permute-start(bf16[2,8,3840]{2,1,0:T(8,128)(2,1)S(1)} %get-tuple-element.42), channel_id=1, source_target_pairs={{0,9},{1,8},{2,11},{3,10},{4,13},{5,12},{6,15},{7,14},{8,1},{9,0},... | collective-permute-start | bytes 368648 | tf_op jit(solution)/shard_map/ppermute | solution.py:241
  29.4 0.0 collective-permute-done.6.refs_9_.refs_5_
  29.5 0.1 collective-permute-start.16
  29.5 0.7 %collective-permute-done.7.refs_11_.refs_6_ = bf16[2,8,3840]{2,1,0:T(8,128)(2,1)S(1)} collective-permute-done((bf16[2,8,3840]{2,1,0:T(8,128)(2,1)S(1)}, bf16[2,8,3840]{2,1,0:T(8,128)(2,1)S(1)}, u32[]{:S(2)}, u32[]{:S(2)}) %collective-permute-start.7) | collective-permute-done | bytes 122912 | tf_op jit(solution)/shard_map/ppermute | solution.py:241
  30.3 3.4 %collective-permute-start.11 = (bf16[2,8,3840]{2,1,0:T(8,128)(2,1)S(1)}, bf16[2,8,3840]{2,1,0:T(8,128)(2,1)S(1)}, u32[]{:S(2)}, u32[]{:S(2)}) collective-permute-start(bf16[2,8,3840]{2,1,0:T(8,128)(2,1)S(1)} %get-tuple-element.43), channel_id=1, source_target_pairs={{0,11},{1,10},{2,9},{3,8},{4,15},{5,14},{6,13},{7,12},{8,3},{9,2},... | collective-permute-start | bytes 368648 | tf_op jit(solution)/shard_map/ppermute | solution.py:241
  33.7 0.3 collective-permute-done.8.refs_7_.refs_17_
  34.0 0.2 collective-permute-start.12
  34.2 1.1 %collective-permute-done.9.refs_8_.refs_19_ = bf16[2,8,3840]{2,1,0:T(8,128)(2,1)S(1)} collective-permute-done((bf16[2,8,3840]{2,1,0:T(8,128)(2,1)S(1)}, bf16[2,8,3840]{2,1,0:T(8,128)(2,1)S(1)}, u32[]{:S(2)}, u32[]{:S(2)}) %collective-permute-start.9) | collective-permute-done | bytes 122912 | tf_op jit(solution)/shard_map/ppermute | solution.py:241
  35.3 3.4 %collective-permute-start.13 = (bf16[2,8,3840]{2,1,0:T(8,128)(2,1)S(1)}, bf16[2,8,3840]{2,1,0:T(8,128)(2,1)S(1)}, u32[]{:S(2)}, u32[]{:S(2)}) collective-permute-start(bf16[2,8,3840]{2,1,0:T(8,128)(2,1)S(1)} %get-tuple-element.45), channel_id=1, source_target_pairs={{0,26},{1,27},{2,24},{3,25},{4,30},{5,31},{6,28},{7,29},{8,18},{9,... | collective-permute-start | bytes 368648 | tf_op jit(solution)/shard_map/ppermute | solution.py:241
  38.7 0.0 collective-permute-done.10.refs_9_.refs_18_
  38.7 1.4 %collective-permute-start.14 = (bf16[2,8,3840]{2,1,0:T(8,128)(2,1)S(1)}, bf16[2,8,3840]{2,1,0:T(8,128)(2,1)S(1)}, u32[]{:S(2)}, u32[]{:S(2)}) collective-permute-start(bf16[2,8,3840]{2,1,0:T(8,128)(2,1)S(1)} %get-tuple-element.46), channel_id=1, source_target_pairs={{0,25},{1,24},{2,27},{3,26},{4,29},{5,28},{6,31},{7,30},{8,17},{9,... | collective-permute-start | bytes 368648 | tf_op jit(solution)/shard_map/ppermute | solution.py:241
  40.2 4.0 %collective-permute-start.15 = (bf16[2,8,3840]{2,1,0:T(8,128)(2,1)S(1)}, bf16[2,8,3840]{2,1,0:T(8,128)(2,1)S(1)}, u32[]{:S(2)}, u32[]{:S(2)}) collective-permute-start(bf16[2,8,3840]{2,1,0:T(8,128)(2,1)S(1)} %get-tuple-element.47), channel_id=1, source_target_pairs={{0,27},{1,26},{2,25},{3,24},{4,31},{5,30},{6,29},{7,28},{8,19},{9,... | collective-permute-start | bytes 368648 | tf_op jit(solution)/shard_map/ppermute | solution.py:241
  44.2 0.3 copy.5.refs_1_.refs_16_
  44.5 1.0 %shard_map.41.refs_25_ = f32[4,2,48,129]{3,2,1,0:T(8,128)S(1)} custom-call(s32[1,128]{1,0:T(1,128)S(1)} %bitcast.3, bf16[4,2,129,1280]{3,2,1,0:T(8,128)(2,1)S(1)} %copy.5.refs_1_.refs_16_, bf16[8,3840]{1,0:T(8,128)(2,1)S(1)} %get-tuple-element.48.refs_2_, bf16[14,8,3840]{2,1,0:T(8,128)(2,1)S(1)} %collective-permute-done.2.theirs_ref.refs_3_, ...), custom_call_target="tpu_custom_call" | custom-call | tf_op jit(solution)/shard_map/pallas_call | solution.py:217
  45.5 4.4 %collective-permute-done.13.refs_12_.refs_23_ = bf16[2,8,3840]{2,1,0:T(8,128)(2,1)S(1)} collective-permute-done((bf16[2,8,3840]{2,1,0:T(8,128)(2,1)S(1)}, bf16[2,8,3840]{2,1,0:T(8,128)(2,1)S(1)}, u32[]{:S(2)}, u32[]{:S(2)}) %collective-permute-start.13) | collective-permute-done | bytes 122912 | tf_op jit(solution)/shard_map/ppermute | solution.py:241
  49.9 0.5 %collective-permute-done.14.refs_13_.refs_22_ = bf16[2,8,3840]{2,1,0:T(8,128)(2,1)S(1)} collective-permute-done((bf16[2,8,3840]{2,1,0:T(8,128)(2,1)S(1)}, bf16[2,8,3840]{2,1,0:T(8,128)(2,1)S(1)}, u32[]{:S(2)}, u32[]{:S(2)}) %collective-permute-start.14) | collective-permute-done | bytes 122912 | tf_op jit(solution)/shard_map/ppermute | solution.py:241
  50.5 1.7 %shard_map.42 = bf16[4,2,48,129]{3,2,1,0:T(8,128)(2,1)} custom-call(bf16[2,8,3840]{2,1,0:T(8,128)(2,1)S(1)} %collective-permute-done.refs_0_.refs_7_, bf16[2,8,3840]{2,1,0:T(8,128)(2,1)S(1)} %collective-permute-done.1.refs_1_.refs_6_, bf16[2,8,3840]{2,1,0:T(8,128)(2,1)S(1)} %collective-permute-done.3.refs_5_.refs_2_, ...), custom_call_target="tpu_custom_call" | custom-call | tf_op jit(solution)/shard_map/pallas_call | solution.py:217
  (13 shorter events, 0.0 us)
Async XLA Ops:
  0.0 1.5 %copy-start = (s32[128]{0:T(128)S(1)}, s32[128]{0:T(128)}, u32[]{:S(2)}) copy-start(s32[128]{0:T(128)} %param.4) | copy-start | bytes 1540
  1.5 42.7 %copy-start.1 = (bf16[4,2,129,1280]{3,1,2,0:T(2,128)(2,1)S(1)}, bf16[4,2,129,1280]{3,1,2,0:T(2,128)(2,1)}, u32[]{:S(2)}) copy-start(bf16[4,2,129,1280]{3,1,2,0:T(2,128)(2,1)} %param.5) | copy-start | bytes 7925764
  2.3 5.2 %collective-permute-start.2 = (bf16[14,8,3840]{2,1,0:T(8,128)(2,1)S(1)}, bf16[14,8,3840]{2,1,0:T(8,128)(2,1)S(1)}, u32[]{:S(2)}, u32[]{:S(2)}) collective-permute-start(bf16[14,8,3840]{2,1,0:T(8,128)(2,1)S(1)} %get-tuple-element.33), channel_id=1, source_target_pairs={{0,4},{1,5},{2,6},{3,7},{4,0},{5,1},{6,2},{7,3},{8,12},{9,13},{10,... | collective-permute-start | bytes 2580488 | tf_op jit(solution)/shard_map/ppermute | solution.py:241
  2.8 9.3 %collective-permute-start = (bf16[2,8,3840]{2,1,0:T(8,128)(2,1)S(1)}, bf16[2,8,3840]{2,1,0:T(8,128)(2,1)S(1)}, u32[]{:S(2)}, u32[]{:S(2)}) collective-permute-start(bf16[2,8,3840]{2,1,0:T(8,128)(2,1)S(1)} %get-tuple-element.30), channel_id=1, source_target_pairs={{0,3},{1,2},{2,1},{3,0},{4,7},{5,6},{6,5},{7,4},{8,11},{9,10},{10,... | collective-permute-start | bytes 368648 | tf_op jit(solution)/shard_map/ppermute | solution.py:241
  7.5 14.2 %collective-permute-start.1 = (bf16[2,8,3840]{2,1,0:T(8,128)(2,1)S(1)}, bf16[2,8,3840]{2,1,0:T(8,128)(2,1)S(1)}, u32[]{:S(2)}, u32[]{:S(2)}) collective-permute-start(bf16[2,8,3840]{2,1,0:T(8,128)(2,1)S(1)} %get-tuple-element.31), channel_id=1, source_target_pairs={{0,2},{1,3},{2,0},{3,1},{4,6},{5,7},{6,4},{7,5},{8,10},{9,11},{10,... | collective-permute-start | bytes 368648 | tf_op jit(solution)/shard_map/ppermute | solution.py:241
  7.6 17.4 %collective-permute-start.3 = (bf16[2,8,3840]{2,1,0:T(8,128)(2,1)S(1)}, bf16[2,8,3840]{2,1,0:T(8,128)(2,1)S(1)}, u32[]{:S(2)}, u32[]{:S(2)}) collective-permute-start(bf16[2,8,3840]{2,1,0:T(8,128)(2,1)S(1)} %get-tuple-element.34), channel_id=1, source_target_pairs={{0,1},{1,0},{2,3},{3,2},{4,5},{5,4},{6,7},{7,6},{8,9},{9,8},{10,11... | collective-permute-start | bytes 368648 | tf_op jit(solution)/shard_map/ppermute | solution.py:241
  8.3 18.2 %collective-permute-start.4 = (bf16[2,8,3840]{2,1,0:T(8,128)(2,1)S(1)}, bf16[2,8,3840]{2,1,0:T(8,128)(2,1)S(1)}, u32[]{:S(2)}, u32[]{:S(2)}) collective-permute-start(bf16[2,8,3840]{2,1,0:T(8,128)(2,1)S(1)} %get-tuple-element.36), channel_id=1, source_target_pairs={{0,16},{1,17},{2,18},{3,19},{4,20},{5,21},{6,22},{7,23},{8,24},{9,... | collective-permute-start | bytes 368648 | tf_op jit(solution)/shard_map/ppermute | solution.py:241
  10.0 16.5 %collective-permute-start.5 = (bf16[2,8,3840]{2,1,0:T(8,128)(2,1)S(1)}, bf16[2,8,3840]{2,1,0:T(8,128)(2,1)S(1)}, u32[]{:S(2)}, u32[]{:S(2)}) collective-permute-start(bf16[2,8,3840]{2,1,0:T(8,128)(2,1)S(1)} %get-tuple-element.37), channel_id=1, source_target_pairs={{0,18},{1,19},{2,16},{3,17},{4,22},{5,23},{6,20},{7,21},{8,26},{9,... | collective-permute-start | bytes 368648 | tf_op jit(solution)/shard_map/ppermute | solution.py:241
  12.2 17.3 %collective-permute-start.6 = (bf16[2,8,3840]{2,1,0:T(8,128)(2,1)S(1)}, bf16[2,8,3840]{2,1,0:T(8,128)(2,1)S(1)}, u32[]{:S(2)}, u32[]{:S(2)}) collective-permute-start(bf16[2,8,3840]{2,1,0:T(8,128)(2,1)S(1)} %get-tuple-element.38), channel_id=1, source_target_pairs={{0,17},{1,16},{2,19},{3,18},{4,21},{5,20},{6,23},{7,22},{8,25},{9,... | collective-permute-start | bytes 368648 | tf_op jit(solution)/shard_map/ppermute | solution.py:241
  21.7 8.6 %collective-permute-start.7 = (bf16[2,8,3840]{2,1,0:T(8,128)(2,1)S(1)}, bf16[2,8,3840]{2,1,0:T(8,128)(2,1)S(1)}, u32[]{:S(2)}, u32[]{:S(2)}) collective-permute-start(bf16[2,8,3840]{2,1,0:T(8,128)(2,1)S(1)} %get-tuple-element.39), channel_id=1, source_target_pairs={{0,19},{1,18},{2,17},{3,16},{4,23},{5,22},{6,21},{7,20},{8,27},{9,... | collective-permute-start | bytes 368648 | tf_op jit(solution)/shard_map/ppermute | solution.py:241
  25.0 9.0 %collective-permute-start.8 = (bf16[2,8,3840]{2,1,0:T(8,128)(2,1)S(1)}, bf16[2,8,3840]{2,1,0:T(8,128)(2,1)S(1)}, u32[]{:S(2)}, u32[]{:S(2)}) collective-permute-start(bf16[2,8,3840]{2,1,0:T(8,128)(2,1)S(1)} %get-tuple-element.40), channel_id=1, source_target_pairs={{0,8},{1,9},{2,10},{3,11},{4,12},{5,13},{6,14},{7,15},{8,0},{9,1},... | collective-permute-start | bytes 368648 | tf_op jit(solution)/shard_map/ppermute | solution.py:241
  26.5 8.8 %collective-permute-start.9 = (bf16[2,8,3840]{2,1,0:T(8,128)(2,1)S(1)}, bf16[2,8,3840]{2,1,0:T(8,128)(2,1)S(1)}, u32[]{:S(2)}, u32[]{:S(2)}) collective-permute-start(bf16[2,8,3840]{2,1,0:T(8,128)(2,1)S(1)} %get-tuple-element.41), channel_id=1, source_target_pairs={{0,10},{1,11},{2,8},{3,9},{4,14},{5,15},{6,12},{7,13},{8,2},{9,3},... | collective-permute-start | bytes 368648 | tf_op jit(solution)/shard_map/ppermute | solution.py:241
  26.5 12.2 %collective-permute-start.10 = (bf16[2,8,3840]{2,1,0:T(8,128)(2,1)S(1)}, bf16[2,8,3840]{2,1,0:T(8,128)(2,1)S(1)}, u32[]{:S(2)}, u32[]{:S(2)}) collective-permute-start(bf16[2,8,3840]{2,1,0:T(8,128)(2,1)S(1)} %get-tuple-element.42), channel_id=1, source_target_pairs={{0,9},{1,8},{2,11},{3,10},{4,13},{5,12},{6,15},{7,14},{8,1},{9,0},... | collective-permute-start | bytes 368648 | tf_op jit(solution)/shard_map/ppermute | solution.py:241
  29.5 10.7 %collective-permute-start.16 = (bf16[2,8,3840]{2,1,0:T(8,128)(2,1)S(1)}, bf16[2,8,3840]{2,1,0:T(8,128)(2,1)S(1)}, u32[]{:S(2)}, u32[]{:S(2)}) collective-permute-start(bf16[2,8,3840]{2,1,0:T(8,128)(2,1)S(1)} %shard_map.40), channel_id=1, source_target_pairs={{0,4},{1,5},{2,6},{3,7},{4,0},{5,1},{6,2},{7,3},{8,12},{9,13},{10,... | collective-permute-start | bytes 368648 | tf_op jit(solution)/shard_map/ppermute | solution.py:241
  30.3 15.2 %collective-permute-start.11 = (bf16[2,8,3840]{2,1,0:T(8,128)(2,1)S(1)}, bf16[2,8,3840]{2,1,0:T(8,128)(2,1)S(1)}, u32[]{:S(2)}, u32[]{:S(2)}) collective-permute-start(bf16[2,8,3840]{2,1,0:T(8,128)(2,1)S(1)} %get-tuple-element.43), channel_id=1, source_target_pairs={{0,11},{1,10},{2,9},{3,8},{4,15},{5,14},{6,13},{7,12},{8,3},{9,2},... | collective-permute-start | bytes 368648 | tf_op jit(solution)/shard_map/ppermute | solution.py:241
  34.0 11.5 %collective-permute-start.12 = (bf16[2,8,3840]{2,1,0:T(8,128)(2,1)S(1)}, bf16[2,8,3840]{2,1,0:T(8,128)(2,1)S(1)}, u32[]{:S(2)}, u32[]{:S(2)}) collective-permute-start(bf16[2,8,3840]{2,1,0:T(8,128)(2,1)S(1)} %get-tuple-element.44), channel_id=1, source_target_pairs={{0,24},{1,25},{2,26},{3,27},{4,28},{5,29},{6,30},{7,31},{8,16},{9,... | collective-permute-start | bytes 368648 | tf_op jit(solution)/shard_map/ppermute | solution.py:241
  35.3 14.7 %collective-permute-start.13 = (bf16[2,8,3840]{2,1,0:T(8,128)(2,1)S(1)}, bf16[2,8,3840]{2,1,0:T(8,128)(2,1)S(1)}, u32[]{:S(2)}, u32[]{:S(2)}) collective-permute-start(bf16[2,8,3840]{2,1,0:T(8,128)(2,1)S(1)} %get-tuple-element.45), channel_id=1, source_target_pairs={{0,26},{1,27},{2,24},{3,25},{4,30},{5,31},{6,28},{7,29},{8,18},{9,... | collective-permute-start | bytes 368648 | tf_op jit(solution)/shard_map/ppermute | solution.py:241
  38.7 11.8 %collective-permute-start.14 = (bf16[2,8,3840]{2,1,0:T(8,128)(2,1)S(1)}, bf16[2,8,3840]{2,1,0:T(8,128)(2,1)S(1)}, u32[]{:S(2)}, u32[]{:S(2)}) collective-permute-start(bf16[2,8,3840]{2,1,0:T(8,128)(2,1)S(1)} %get-tuple-element.46), channel_id=1, source_target_pairs={{0,25},{1,24},{2,27},{3,26},{4,29},{5,28},{6,31},{7,30},{8,17},{9,... | collective-permute-start | bytes 368648 | tf_op jit(solution)/shard_map/ppermute | solution.py:241
  40.2 10.3 %collective-permute-start.15 = (bf16[2,8,3840]{2,1,0:T(8,128)(2,1)S(1)}, bf16[2,8,3840]{2,1,0:T(8,128)(2,1)S(1)}, u32[]{:S(2)}, u32[]{:S(2)}) collective-permute-start(bf16[2,8,3840]{2,1,0:T(8,128)(2,1)S(1)} %get-tuple-element.47), channel_id=1, source_target_pairs={{0,27},{1,26},{2,25},{3,24},{4,31},{5,30},{6,29},{7,28},{8,19},{9,... | collective-permute-start | bytes 368648 | tf_op jit(solution)/shard_map/ppermute | solution.py:241

commit v5 on v4

--- a/solution.py
+++ b/solution.py
@@ -15,7 +15,8 @@
 FAR = tuple(X + d for d in NEAR)
 EARLY = (3, 2)
 JOINED = tuple(d for d in NEAR[1:] + FAR if d not in EARLY)
-ORDER = (1, 16, 18, 17, 19, 8, 10, 9, 11, 24, 26, 25, 27)
+LATE = 4
+ORDER = (17, 16, 18, 1, 19, 8, 10, 9, 26, 24, 25, 11, 27)
 WIDE, REST = 256, 64
 
 
@@ -139,9 +140,9 @@
         blocks = [(r.at[0], r.at[1]) for r in refs[: 2 * len(steps)]]
         refs = refs[2 * len(steps) :]
     else:
-        own, theirs, changed = refs[:3]
+        own, theirs, *came, changed = refs[:10]
         blocks = [(own, theirs.at[0])]
-        for d, r in zip(NEAR[1:], refs[3:10]):
+        for d, r in zip(NEAR[1:], came):
             blocks.append((r.at[0], changed.at[EARLY.index(d)] if d in EARLY else r.at[1]))
         refs = refs[10:]
     before = refs[0] if added else None
@@ -252,11 +253,13 @@
     came = [got[d] for d in EARLY]
     *came, got[ORDER[0]] = lax.optimization_barrier((*came, got[ORDER[0]]))
     changed = send(second_blocks(*came), CORE)
-    near = [own, theirs, changed] + [got[d] for d in NEAR[1:]]
+    near = [own, theirs] + [got[d] for d in NEAR[1:]] + [changed]
     total = transform(entries, legendre, near, False, (0, 1, 2, 3), width)
     far = [got[d] for d in FAR]
+    rest = list(got.values())
+    rest.insert(len(rest) - LATE, changed)
     return transform(
-        entries, legendre, far, True, (0, 1, 2, 3), width, total, True, list(got.values())
+        entries, legendre, far, True, (0, 1, 2, 3), width, total, True, rest
     )
 
 

time: 52.3 us -> 51.4 us (0.983)
  starting transfers between devices: 35.7 us -> 34.5 us
    ppermute x17, starting transfers between devices: 35.7 us -> 34.5 us  [send(): lax.ppermute(piece, ('lat', 'lev'), [(i, i ^ distance) for i in range(cou...]
  transfers between devices with their start and end apart: 17 -> 17, of which waited for: 6 -> 4; matrix products, arithmetic and copies ran while one was open for 1% -> 1% of each run, Pallas kernels for 2% -> 2%
where the time goes in v5:
time: 51.4 us; the launch traced here: 51 us
  starting transfers between devices  34.5 us (67%)
  waiting for transfers between devices  11.1 us (22%)
  Pallas kernels  5.04 us (10%)
    ppermute x17, starting transfers between devices, send(): lax.ppermute(piece, ('lat', 'lev'), [(i, i ^ distance) for i in range(cou...  34.5 us
    ppermute x17, waiting for transfers between devices, send(): lax.ppermute(piece, ('lat', 'lev'), [(i, i ^ distance) for i in range(cou...  11.1 us
    pallas_call x2, Pallas kernels, transform(): pl.pallas_call(functools.partial(transform_kernel, skip=len(rest), far=fa...  2.64 us
    pallas_call x1, Pallas kernels, load(): pl.pallas_call(load_kernel, in_specs=[HBM], out_specs=[VMEM] * 2, out_sha...  1.5 us
  transfers between devices with their start and end apart: 17, of which 4 were waited for; matrix products, arithmetic and copies ran while one was open for 1% of the time, Pallas kernels for 2%

profile of v5, /device:TPU:0, one launch (start us, length us, event | category | flops | bytes accessed | tf_op | source)
XLA Modules:
  0.0 51.0 jit_solution(17970374296659270769)
XLA Ops:
  0.0 1.5 %shard_map.37 = (bf16[12,256,256]{2,1,0:T(8,128)(2,1)S(1)}, bf16[12,64,256]{2,1,0:T(8,128)(2,1)S(1)}) custom-call(bf16[12,320,256]{2,1,0:T(8,128)(2,1)} %bitcast.5), custom_call_target="tpu_custom_call" | custom-call | flops 1000000000 | bytes 3932160 | tf_op jit(solution)/shard_map/pallas_call | solution.py:44
  1.5 0.0 copy-start.1
  1.5 0.8 %shard_map.38 = (bf16[13,8,3840]{2,1,0:T(8,128)(2,1)S(1)}, bf16[14,8,3840]{2,1,0:T(8,128)(2,1)S(1)}, bf16[8,3840]{1,0:T(8,128)(2,1)S(1)}, bf16[2,8,3840]{2,1,0:T(8,128)(2,1)S(1)}, bf16[2,8,3840]{2,1,0:T(8,128)(2,1)S(1)}) custom-call(s32[1,128]{1,0:T(1,128)S(1)} %bitcast.2, bf16[12,256,256]{2,1,0:T(8,128)(2,1)S(1)} %get-tuple-element.28.wide_ref, ...), custom_call_target="tpu_custom_call" | custom-call | tf_op jit(solution)/shard_map/pallas_call | solution.py:93
  2.3 0.5 collective-permute-start.2
  2.8 4.7 %collective-permute-start = (bf16[2,8,3840]{2,1,0:T(8,128)(2,1)S(1)}, bf16[2,8,3840]{2,1,0:T(8,128)(2,1)S(1)}, u32[]{:S(2)}, u32[]{:S(2)}) collective-permute-start(bf16[2,8,3840]{2,1,0:T(8,128)(2,1)S(1)} %get-tuple-element.30), channel_id=1, source_target_pairs={{0,3},{1,2},{2,1},{3,0},{4,7},{5,6},{6,5},{7,4},{8,11},{9,10},{10,... | collective-permute-start | bytes 368648 | tf_op jit(solution)/shard_map/ppermute | solution.py:242
  7.5 0.1 shard_map.39
  7.6 1.8 %collective-permute-start.3 = (bf16[2,8,3840]{2,1,0:T(8,128)(2,1)S(1)}, bf16[2,8,3840]{2,1,0:T(8,128)(2,1)S(1)}, u32[]{:S(2)}, u32[]{:S(2)}) collective-permute-start(bf16[2,8,3840]{2,1,0:T(8,128)(2,1)S(1)} %get-tuple-element.34), channel_id=1, source_target_pairs={{0,17},{1,16},{2,19},{3,18},{4,21},{5,20},{6,23},{7,22},{8,25},{9,... | collective-permute-start | bytes 368648 | tf_op jit(solution)/shard_map/ppermute | solution.py:242
  9.4 0.4 collective-permute-start.4
  9.8 3.2 %collective-permute-start.5 = (bf16[2,8,3840]{2,1,0:T(8,128)(2,1)S(1)}, bf16[2,8,3840]{2,1,0:T(8,128)(2,1)S(1)}, u32[]{:S(2)}, u32[]{:S(2)}) collective-permute-start(bf16[2,8,3840]{2,1,0:T(8,128)(2,1)S(1)} %get-tuple-element.37), channel_id=1, source_target_pairs={{0,18},{1,19},{2,16},{3,17},{4,22},{5,23},{6,20},{7,21},{8,26},{9,... | collective-permute-start | bytes 368648 | tf_op jit(solution)/shard_map/ppermute | solution.py:242
  13.0 3.9 %collective-permute-start.6 = (bf16[2,8,3840]{2,1,0:T(8,128)(2,1)S(1)}, bf16[2,8,3840]{2,1,0:T(8,128)(2,1)S(1)}, u32[]{:S(2)}, u32[]{:S(2)}) collective-permute-start(bf16[2,8,3840]{2,1,0:T(8,128)(2,1)S(1)} %get-tuple-element.38), channel_id=1, source_target_pairs={{0,1},{1,0},{2,3},{3,2},{4,5},{5,4},{6,7},{7,6},{8,9},{9,8},{10,11... | collective-permute-start | bytes 368648 | tf_op jit(solution)/shard_map/ppermute | solution.py:242
  16.9 4.7 %collective-permute-done.1.refs_1_.refs_5_ = bf16[2,8,3840]{2,1,0:T(8,128)(2,1)S(1)} collective-permute-done((bf16[2,8,3840]{2,1,0:T(8,128)(2,1)S(1)}, bf16[2,8,3840]{2,1,0:T(8,128)(2,1)S(1)}, u32[]{:S(2)}, u32[]{:S(2)}) %collective-permute-start.1) | collective-permute-done | bytes 122912 | tf_op jit(solution)/shard_map/ppermute | solution.py:242
  21.6 3.4 %collective-permute-start.7 = (bf16[2,8,3840]{2,1,0:T(8,128)(2,1)S(1)}, bf16[2,8,3840]{2,1,0:T(8,128)(2,1)S(1)}, u32[]{:S(2)}, u32[]{:S(2)}) collective-permute-start(bf16[2,8,3840]{2,1,0:T(8,128)(2,1)S(1)} %get-tuple-element.39), channel_id=1, source_target_pairs={{0,19},{1,18},{2,17},{3,16},{4,23},{5,22},{6,21},{7,20},{8,27},{9,... | collective-permute-start | bytes 368648 | tf_op jit(solution)/shard_map/ppermute | solution.py:242
  25.0 1.5 %collective-permute-start.8 = (bf16[2,8,3840]{2,1,0:T(8,128)(2,1)S(1)}, bf16[2,8,3840]{2,1,0:T(8,128)(2,1)S(1)}, u32[]{:S(2)}, u32[]{:S(2)}) collective-permute-start(bf16[2,8,3840]{2,1,0:T(8,128)(2,1)S(1)} %get-tuple-element.40), channel_id=1, source_target_pairs={{0,8},{1,9},{2,10},{3,11},{4,12},{5,13},{6,14},{7,15},{8,0},{9,1},... | collective-permute-start | bytes 368648 | tf_op jit(solution)/shard_map/ppermute | solution.py:242
  26.5 0.0 collective-permute-done.5.refs_9_.refs_4_
  26.5 2.9 %collective-permute-start.10 = (bf16[2,8,3840]{2,1,0:T(8,128)(2,1)S(1)}, bf16[2,8,3840]{2,1,0:T(8,128)(2,1)S(1)}, u32[]{:S(2)}, u32[]{:S(2)}) collective-permute-start(bf16[2,8,3840]{2,1,0:T(8,128)(2,1)S(1)} %get-tuple-element.42), channel_id=1, source_target_pairs={{0,9},{1,8},{2,11},{3,10},{4,13},{5,12},{6,15},{7,14},{8,1},{9,0},... | collective-permute-start | bytes 368648 | tf_op jit(solution)/shard_map/ppermute | solution.py:242
  29.4 0.1 collective-permute-start.12
  29.5 0.7 %collective-permute-done.7.refs_10_.refs_6_ = bf16[2,8,3840]{2,1,0:T(8,128)(2,1)S(1)} collective-permute-done((bf16[2,8,3840]{2,1,0:T(8,128)(2,1)S(1)}, bf16[2,8,3840]{2,1,0:T(8,128)(2,1)S(1)}, u32[]{:S(2)}, u32[]{:S(2)}) %collective-permute-start.7) | collective-permute-done | bytes 122912 | tf_op jit(solution)/shard_map/ppermute | solution.py:242
  30.2 4.2 %collective-permute-start.11 = (bf16[2,8,3840]{2,1,0:T(8,128)(2,1)S(1)}, bf16[2,8,3840]{2,1,0:T(8,128)(2,1)S(1)}, u32[]{:S(2)}, u32[]{:S(2)}) collective-permute-start(bf16[2,8,3840]{2,1,0:T(8,128)(2,1)S(1)} %get-tuple-element.43), channel_id=1, source_target_pairs={{0,26},{1,27},{2,24},{3,25},{4,30},{5,31},{6,28},{7,29},{8,18},{9,... | collective-permute-start | bytes 368648 | tf_op jit(solution)/shard_map/ppermute | solution.py:242
  34.4 0.0 collective-permute-done.8.refs_7_.refs_18_
  34.4 2.6 %collective-permute-start.13 = (bf16[2,8,3840]{2,1,0:T(8,128)(2,1)S(1)}, bf16[2,8,3840]{2,1,0:T(8,128)(2,1)S(1)}, u32[]{:S(2)}, u32[]{:S(2)}) collective-permute-start(bf16[2,8,3840]{2,1,0:T(8,128)(2,1)S(1)} %get-tuple-element.46), channel_id=1, source_target_pairs={{0,24},{1,25},{2,26},{3,27},{4,28},{5,29},{6,30},{7,31},{8,16},{9,... | collective-permute-start | bytes 368648 | tf_op jit(solution)/shard_map/ppermute | solution.py:242
  37.0 0.1 collective-permute-done.9.refs_8_.refs_20_
  37.1 0.8 %collective-permute-start.14 = (bf16[2,8,3840]{2,1,0:T(8,128)(2,1)S(1)}, bf16[2,8,3840]{2,1,0:T(8,128)(2,1)S(1)}, u32[]{:S(2)}, u32[]{:S(2)}) collective-permute-start(bf16[2,8,3840]{2,1,0:T(8,128)(2,1)S(1)} %get-tuple-element.47), channel_id=1, source_target_pairs={{0,25},{1,24},{2,27},{3,26},{4,29},{5,28},{6,31},{7,30},{8,17},{9,... | collective-permute-start | bytes 368648 | tf_op jit(solution)/shard_map/ppermute | solution.py:242
  37.8 0.0 collective-permute-done.10.refs_9_.refs_19_
  37.8 1.7 %collective-permute-start.15 = (bf16[2,8,3840]{2,1,0:T(8,128)(2,1)S(1)}, bf16[2,8,3840]{2,1,0:T(8,128)(2,1)S(1)}, u32[]{:S(2)}, u32[]{:S(2)}) collective-permute-start(bf16[2,8,3840]{2,1,0:T(8,128)(2,1)S(1)} %get-tuple-element.48), channel_id=1, source_target_pairs={{0,11},{1,10},{2,9},{3,8},{4,15},{5,14},{6,13},{7,12},{8,3},{9,2},... | collective-permute-start | bytes 368648 | tf_op jit(solution)/shard_map/ppermute | solution.py:242
  39.5 0.0 collective-permute-done.12.refs_11_
  39.5 3.0 %collective-permute-start.16 = (bf16[2,8,3840]{2,1,0:T(8,128)(2,1)S(1)}, bf16[2,8,3840]{2,1,0:T(8,128)(2,1)S(1)}, u32[]{:S(2)}, u32[]{:S(2)}) collective-permute-start(bf16[2,8,3840]{2,1,0:T(8,128)(2,1)S(1)} %get-tuple-element.49), channel_id=1, source_target_pairs={{0,27},{1,26},{2,25},{3,24},{4,31},{5,30},{6,29},{7,28},{8,19},{9,... | collective-permute-start | bytes 368648 | tf_op jit(solution)/shard_map/ppermute | solution.py:242
  42.5 0.3 copy.5.refs_1_.refs_17_
  42.9 1.0 %shard_map.41.refs_26_ = f32[4,2,48,129]{3,2,1,0:T(8,128)S(1)} custom-call(s32[1,128]{1,0:T(1,128)S(1)} %bitcast.3, bf16[4,2,129,1280]{3,2,1,0:T(8,128)(2,1)S(1)} %copy.5.refs_1_.refs_17_, bf16[8,3840]{1,0:T(8,128)(2,1)S(1)} %get-tuple-element.50.refs_2_, bf16[14,8,3840]{2,1,0:T(8,128)(2,1)S(1)} %collective-permute-done.2.theirs_ref.refs_3_, ...), custom_call_target="tpu_custom_call" | custom-call | tf_op jit(solution)/shard_map/pallas_call | solution.py:218
  43.8 5.5 %collective-permute-done.13.refs_12_.refs_22_ = bf16[2,8,3840]{2,1,0:T(8,128)(2,1)S(1)} collective-permute-done((bf16[2,8,3840]{2,1,0:T(8,128)(2,1)S(1)}, bf16[2,8,3840]{2,1,0:T(8,128)(2,1)S(1)}, u32[]{:S(2)}, u32[]{:S(2)}) %collective-permute-start.13) | collective-permute-done | bytes 122912 | tf_op jit(solution)/shard_map/ppermute | solution.py:242
  49.4 0.0 collective-permute-done.14.refs_13_.refs_23_
  49.4 0.0 collective-permute-done.15.refs_14_.refs_21_
  49.4 1.7 %shard_map.42 = bf16[4,2,48,129]{3,2,1,0:T(8,128)(2,1)} custom-call(bf16[2,8,3840]{2,1,0:T(8,128)(2,1)S(1)} %collective-permute-done.refs_0_.refs_6_, bf16[2,8,3840]{2,1,0:T(8,128)(2,1)S(1)} %collective-permute-done.1.refs_1_.refs_5_, bf16[2,8,3840]{2,1,0:T(8,128)(2,1)S(1)} %collective-permute-done.3.refs_8_.refs_2_, ...), custom_call_target="tpu_custom_call" | custom-call | tf_op jit(solution)/shard_map/pallas_call | solution.py:218
  (13 shorter events, 0.0 us)
Async XLA Ops:
  0.0 1.5 %copy-start = (s32[128]{0:T(128)S(1)}, s32[128]{0:T(128)}, u32[]{:S(2)}) copy-start(s32[128]{0:T(128)} %param.4) | copy-start | bytes 1540
  1.5 41.0 %copy-start.1 = (bf16[4,2,129,1280]{3,1,2,0:T(2,128)(2,1)S(1)}, bf16[4,2,129,1280]{3,1,2,0:T(2,128)(2,1)}, u32[]{:S(2)}) copy-start(bf16[4,2,129,1280]{3,1,2,0:T(2,128)(2,1)} %param.5) | copy-start | bytes 7925764
  2.3 5.2 %collective-permute-start.2 = (bf16[14,8,3840]{2,1,0:T(8,128)(2,1)S(1)}, bf16[14,8,3840]{2,1,0:T(8,128)(2,1)S(1)}, u32[]{:S(2)}, u32[]{:S(2)}) collective-permute-start(bf16[14,8,3840]{2,1,0:T(8,128)(2,1)S(1)} %get-tuple-element.33), channel_id=1, source_target_pairs={{0,4},{1,5},{2,6},{3,7},{4,0},{5,1},{6,2},{7,3},{8,12},{9,13},{10,... | collective-permute-start | bytes 2580488 | tf_op jit(solution)/shard_map/ppermute | solution.py:242
  2.8 10.1 %collective-permute-start = (bf16[2,8,3840]{2,1,0:T(8,128)(2,1)S(1)}, bf16[2,8,3840]{2,1,0:T(8,128)(2,1)S(1)}, u32[]{:S(2)}, u32[]{:S(2)}) collective-permute-start(bf16[2,8,3840]{2,1,0:T(8,128)(2,1)S(1)} %get-tuple-element.30), channel_id=1, source_target_pairs={{0,3},{1,2},{2,1},{3,0},{4,7},{5,6},{6,5},{7,4},{8,11},{9,10},{10,... | collective-permute-start | bytes 368648 | tf_op jit(solution)/shard_map/ppermute | solution.py:242
  7.5 14.1 %collective-permute-start.1 = (bf16[2,8,3840]{2,1,0:T(8,128)(2,1)S(1)}, bf16[2,8,3840]{2,1,0:T(8,128)(2,1)S(1)}, u32[]{:S(2)}, u32[]{:S(2)}) collective-permute-start(bf16[2,8,3840]{2,1,0:T(8,128)(2,1)S(1)} %get-tuple-element.31), channel_id=1, source_target_pairs={{0,2},{1,3},{2,0},{3,1},{4,6},{5,7},{6,4},{7,5},{8,10},{9,11},{10,... | collective-permute-start | bytes 368648 | tf_op jit(solution)/shard_map/ppermute | solution.py:242
  7.6 17.4 %collective-permute-start.3 = (bf16[2,8,3840]{2,1,0:T(8,128)(2,1)S(1)}, bf16[2,8,3840]{2,1,0:T(8,128)(2,1)S(1)}, u32[]{:S(2)}, u32[]{:S(2)}) collective-permute-start(bf16[2,8,3840]{2,1,0:T(8,128)(2,1)S(1)} %get-tuple-element.34), channel_id=1, source_target_pairs={{0,17},{1,16},{2,19},{3,18},{4,21},{5,20},{6,23},{7,22},{8,25},{9,... | collective-permute-start | bytes 368648 | tf_op jit(solution)/shard_map/ppermute | solution.py:242
  9.4 17.1 %collective-permute-start.4 = (bf16[2,8,3840]{2,1,0:T(8,128)(2,1)S(1)}, bf16[2,8,3840]{2,1,0:T(8,128)(2,1)S(1)}, u32[]{:S(2)}, u32[]{:S(2)}) collective-permute-start(bf16[2,8,3840]{2,1,0:T(8,128)(2,1)S(1)} %get-tuple-element.36), channel_id=1, source_target_pairs={{0,16},{1,17},{2,18},{3,19},{4,20},{5,21},{6,22},{7,23},{8,24},{9,... | collective-permute-start | bytes 368648 | tf_op jit(solution)/shard_map/ppermute | solution.py:242
  9.8 16.7 %collective-permute-start.5 = (bf16[2,8,3840]{2,1,0:T(8,128)(2,1)S(1)}, bf16[2,8,3840]{2,1,0:T(8,128)(2,1)S(1)}, u32[]{:S(2)}, u32[]{:S(2)}) collective-permute-start(bf16[2,8,3840]{2,1,0:T(8,128)(2,1)S(1)} %get-tuple-element.37), channel_id=1, source_target_pairs={{0,18},{1,19},{2,16},{3,17},{4,22},{5,23},{6,20},{7,21},{8,26},{9,... | collective-permute-start | bytes 368648 | tf_op jit(solution)/shard_map/ppermute | solution.py:242
  13.0 16.4 %collective-permute-start.6 = (bf16[2,8,3840]{2,1,0:T(8,128)(2,1)S(1)}, bf16[2,8,3840]{2,1,0:T(8,128)(2,1)S(1)}, u32[]{:S(2)}, u32[]{:S(2)}) collective-permute-start(bf16[2,8,3840]{2,1,0:T(8,128)(2,1)S(1)} %get-tuple-element.38), channel_id=1, source_target_pairs={{0,1},{1,0},{2,3},{3,2},{4,5},{5,4},{6,7},{7,6},{8,9},{9,8},{10,11... | collective-permute-start | bytes 368648 | tf_op jit(solution)/shard_map/ppermute | solution.py:242
  21.6 8.6 %collective-permute-start.7 = (bf16[2,8,3840]{2,1,0:T(8,128)(2,1)S(1)}, bf16[2,8,3840]{2,1,0:T(8,128)(2,1)S(1)}, u32[]{:S(2)}, u32[]{:S(2)}) collective-permute-start(bf16[2,8,3840]{2,1,0:T(8,128)(2,1)S(1)} %get-tuple-element.39), channel_id=1, source_target_pairs={{0,19},{1,18},{2,17},{3,16},{4,23},{5,22},{6,21},{7,20},{8,27},{9,... | collective-permute-start | bytes 368648 | tf_op jit(solution)/shard_map/ppermute | solution.py:242
  25.0 9.4 %collective-permute-start.8 = (bf16[2,8,3840]{2,1,0:T(8,128)(2,1)S(1)}, bf16[2,8,3840]{2,1,0:T(8,128)(2,1)S(1)}, u32[]{:S(2)}, u32[]{:S(2)}) collective-permute-start(bf16[2,8,3840]{2,1,0:T(8,128)(2,1)S(1)} %get-tuple-element.40), channel_id=1, source_target_pairs={{0,8},{1,9},{2,10},{3,11},{4,12},{5,13},{6,14},{7,15},{8,0},{9,1},... | collective-permute-start | bytes 368648 | tf_op jit(solution)/shard_map/ppermute | solution.py:242
  26.5 10.6 %collective-permute-start.9 = (bf16[2,8,3840]{2,1,0:T(8,128)(2,1)S(1)}, bf16[2,8,3840]{2,1,0:T(8,128)(2,1)S(1)}, u32[]{:S(2)}, u32[]{:S(2)}) collective-permute-start(bf16[2,8,3840]{2,1,0:T(8,128)(2,1)S(1)} %get-tuple-element.41), channel_id=1, source_target_pairs={{0,10},{1,11},{2,8},{3,9},{4,14},{5,15},{6,12},{7,13},{8,2},{9,3},... | collective-permute-start | bytes 368648 | tf_op jit(solution)/shard_map/ppermute | solution.py:242
  26.5 11.3 %collective-permute-start.10 = (bf16[2,8,3840]{2,1,0:T(8,128)(2,1)S(1)}, bf16[2,8,3840]{2,1,0:T(8,128)(2,1)S(1)}, u32[]{:S(2)}, u32[]{:S(2)}) collective-permute-start(bf16[2,8,3840]{2,1,0:T(8,128)(2,1)S(1)} %get-tuple-element.42), channel_id=1, source_target_pairs={{0,9},{1,8},{2,11},{3,10},{4,13},{5,12},{6,15},{7,14},{8,1},{9,0},... | collective-permute-start | bytes 368648 | tf_op jit(solution)/shard_map/ppermute | solution.py:242
  29.4 10.1 %collective-permute-start.12 = (bf16[2,8,3840]{2,1,0:T(8,128)(2,1)S(1)}, bf16[2,8,3840]{2,1,0:T(8,128)(2,1)S(1)}, u32[]{:S(2)}, u32[]{:S(2)}) collective-permute-start(bf16[2,8,3840]{2,1,0:T(8,128)(2,1)S(1)} %shard_map.40), channel_id=1, source_target_pairs={{0,4},{1,5},{2,6},{3,7},{4,0},{5,1},{6,2},{7,3},{8,12},{9,13},{10,... | collective-permute-start | bytes 368648 | tf_op jit(solution)/shard_map/ppermute | solution.py:242
  30.2 13.6 %collective-permute-start.11 = (bf16[2,8,3840]{2,1,0:T(8,128)(2,1)S(1)}, bf16[2,8,3840]{2,1,0:T(8,128)(2,1)S(1)}, u32[]{:S(2)}, u32[]{:S(2)}) collective-permute-start(bf16[2,8,3840]{2,1,0:T(8,128)(2,1)S(1)} %get-tuple-element.43), channel_id=1, source_target_pairs={{0,26},{1,27},{2,24},{3,25},{4,30},{5,31},{6,28},{7,29},{8,18},{9,... | collective-permute-start | bytes 368648 | tf_op jit(solution)/shard_map/ppermute | solution.py:242
  34.4 14.9 %collective-permute-start.13 = (bf16[2,8,3840]{2,1,0:T(8,128)(2,1)S(1)}, bf16[2,8,3840]{2,1,0:T(8,128)(2,1)S(1)}, u32[]{:S(2)}, u32[]{:S(2)}) collective-permute-start(bf16[2,8,3840]{2,1,0:T(8,128)(2,1)S(1)} %get-tuple-element.46), channel_id=1, source_target_pairs={{0,24},{1,25},{2,26},{3,27},{4,28},{5,29},{6,30},{7,31},{8,16},{9,... | collective-permute-start | bytes 368648 | tf_op jit(solution)/shard_map/ppermute | solution.py:242
  37.1 12.3 %collective-permute-start.14 = (bf16[2,8,3840]{2,1,0:T(8,128)(2,1)S(1)}, bf16[2,8,3840]{2,1,0:T(8,128)(2,1)S(1)}, u32[]{:S(2)}, u32[]{:S(2)}) collective-permute-start(bf16[2,8,3840]{2,1,0:T(8,128)(2,1)S(1)} %get-tuple-element.47), channel_id=1, source_target_pairs={{0,25},{1,24},{2,27},{3,26},{4,29},{5,28},{6,31},{7,30},{8,17},{9,... | collective-permute-start | bytes 368648 | tf_op jit(solution)/shard_map/ppermute | solution.py:242
  37.8 11.5 %collective-permute-start.15 = (bf16[2,8,3840]{2,1,0:T(8,128)(2,1)S(1)}, bf16[2,8,3840]{2,1,0:T(8,128)(2,1)S(1)}, u32[]{:S(2)}, u32[]{:S(2)}) collective-permute-start(bf16[2,8,3840]{2,1,0:T(8,128)(2,1)S(1)} %get-tuple-element.48), channel_id=1, source_target_pairs={{0,11},{1,10},{2,9},{3,8},{4,15},{5,14},{6,13},{7,12},{8,3},{9,2},... | collective-permute-start | bytes 368648 | tf_op jit(solution)/shard_map/ppermute | solution.py:242
  39.5 9.8 %collective-permute-start.16 = (bf16[2,8,3840]{2,1,0:T(8,128)(2,1)S(1)}, bf16[2,8,3840]{2,1,0:T(8,128)(2,1)S(1)}, u32[]{:S(2)}, u32[]{:S(2)}) collective-permute-start(bf16[2,8,3840]{2,1,0:T(8,128)(2,1)S(1)} %get-tuple-element.49), channel_id=1, source_target_pairs={{0,27},{1,26},{2,25},{3,24},{4,31},{5,30},{6,29},{7,28},{8,19},{9,... | collective-permute-start | bytes 368648 | tf_op jit(solution)/shard_map/ppermute | solution.py:242

commit v6 on v5

--- a/solution.py
+++ b/solution.py
@@ -16,7 +16,7 @@
 EARLY = (3, 2)
 JOINED = tuple(d for d in NEAR[1:] + FAR if d not in EARLY)
 LATE = 4
-ORDER = (17, 16, 18, 1, 19, 8, 10, 9, 26, 24, 25, 11, 27)
+ORDER = (17, 16, 18, 1, 19, 8, 9, 26, 24, 27, 10, 25, 11)
 WIDE, REST = 256, 64
 
 

time: 51.4 us -> 51.3 us (level)
  waiting for transfers between devices: 11.1 us -> 13 us
  starting transfers between devices: 34.5 us -> 32.7 us
    ppermute x17, waiting for transfers between devices: 11.1 us -> 13 us  [send(): lax.ppermute(piece, ('lat', 'lev'), [(i, i ^ distance) for i in range(cou...]
    ppermute x17, starting transfers between devices: 34.5 us -> 32.7 us  [send(): lax.ppermute(piece, ('lat', 'lev'), [(i, i ^ distance) for i in range(cou...]
  transfers between devices with their start and end apart: 17 -> 17, of which waited for: 4 -> 5; matrix products, arithmetic and copies ran while one was open for 1% -> 1% of each run, Pallas kernels for 2% -> 2%
where the time goes in v6:
time: 51.3 us; the launch traced here: 51.2 us
  starting transfers between devices  32.7 us (64%)
  waiting for transfers between devices  13 us (25%)
  Pallas kernels  5.02 us (10%)
    ppermute x17, starting transfers between devices, send(): lax.ppermute(piece, ('lat', 'lev'), [(i, i ^ distance) for i in range(cou...  32.7 us
    ppermute x17, waiting for transfers between devices, send(): lax.ppermute(piece, ('lat', 'lev'), [(i, i ^ distance) for i in range(cou...  13 us
    pallas_call x2, Pallas kernels, transform(): pl.pallas_call(functools.partial(transform_kernel, skip=len(rest), far=fa...  2.62 us
    pallas_call x1, Pallas kernels, load(): pl.pallas_call(load_kernel, in_specs=[HBM], out_specs=[VMEM] * 2, out_sha...  1.5 us
  transfers between devices with their start and end apart: 17, of which 5 were waited for; matrix products, arithmetic and copies ran while one was open for 1% of the time, Pallas kernels for 2%

profile of v6, /device:TPU:0, one launch (start us, length us, event | category | flops | bytes accessed | tf_op | source)
XLA Modules:
  0.0 51.2 jit_solution(10523367573140221791)
XLA Ops:
  0.0 1.5 %shard_map.37 = (bf16[12,256,256]{2,1,0:T(8,128)(2,1)S(1)}, bf16[12,64,256]{2,1,0:T(8,128)(2,1)S(1)}) custom-call(bf16[12,320,256]{2,1,0:T(8,128)(2,1)} %bitcast.5), custom_call_target="tpu_custom_call" | custom-call | flops 1000000000 | bytes 3932160 | tf_op jit(solution)/shard_map/pallas_call | solution.py:44
  1.5 0.0 copy-start.1
  1.5 0.8 %shard_map.38 = (bf16[13,8,3840]{2,1,0:T(8,128)(2,1)S(1)}, bf16[14,8,3840]{2,1,0:T(8,128)(2,1)S(1)}, bf16[8,3840]{1,0:T(8,128)(2,1)S(1)}, bf16[2,8,3840]{2,1,0:T(8,128)(2,1)S(1)}, bf16[2,8,3840]{2,1,0:T(8,128)(2,1)S(1)}) custom-call(s32[1,128]{1,0:T(1,128)S(1)} %bitcast.2, bf16[12,256,256]{2,1,0:T(8,128)(2,1)S(1)} %get-tuple-element.28.wide_ref, ...), custom_call_target="tpu_custom_call" | custom-call | tf_op jit(solution)/shard_map/pallas_call | solution.py:93
  2.3 0.5 collective-permute-start.2
  2.8 4.7 %collective-permute-start = (bf16[2,8,3840]{2,1,0:T(8,128)(2,1)S(1)}, bf16[2,8,3840]{2,1,0:T(8,128)(2,1)S(1)}, u32[]{:S(2)}, u32[]{:S(2)}) collective-permute-start(bf16[2,8,3840]{2,1,0:T(8,128)(2,1)S(1)} %get-tuple-element.30), channel_id=1, source_target_pairs={{0,3},{1,2},{2,1},{3,0},{4,7},{5,6},{6,5},{7,4},{8,11},{9,10},{10,... | collective-permute-start | bytes 368648 | tf_op jit(solution)/shard_map/ppermute | solution.py:242
  7.5 0.0 collective-permute-start.1
  7.5 0.1 shard_map.39
  7.6 1.8 %collective-permute-start.3 = (bf16[2,8,3840]{2,1,0:T(8,128)(2,1)S(1)}, bf16[2,8,3840]{2,1,0:T(8,128)(2,1)S(1)}, u32[]{:S(2)}, u32[]{:S(2)}) collective-permute-start(bf16[2,8,3840]{2,1,0:T(8,128)(2,1)S(1)} %get-tuple-element.34), channel_id=1, source_target_pairs={{0,17},{1,16},{2,19},{3,18},{4,21},{5,20},{6,23},{7,22},{8,25},{9,... | collective-permute-start | bytes 368648 | tf_op jit(solution)/shard_map/ppermute | solution.py:242
  9.4 0.4 collective-permute-start.4
  9.8 3.2 %collective-permute-start.5 = (bf16[2,8,3840]{2,1,0:T(8,128)(2,1)S(1)}, bf16[2,8,3840]{2,1,0:T(8,128)(2,1)S(1)}, u32[]{:S(2)}, u32[]{:S(2)}) collective-permute-start(bf16[2,8,3840]{2,1,0:T(8,128)(2,1)S(1)} %get-tuple-element.37), channel_id=1, source_target_pairs={{0,18},{1,19},{2,16},{3,17},{4,22},{5,23},{6,20},{7,21},{8,26},{9,... | collective-permute-start | bytes 368648 | tf_op jit(solution)/shard_map/ppermute | solution.py:242
  13.0 3.9 %collective-permute-start.6 = (bf16[2,8,3840]{2,1,0:T(8,128)(2,1)S(1)}, bf16[2,8,3840]{2,1,0:T(8,128)(2,1)S(1)}, u32[]{:S(2)}, u32[]{:S(2)}) collective-permute-start(bf16[2,8,3840]{2,1,0:T(8,128)(2,1)S(1)} %get-tuple-element.38), channel_id=1, source_target_pairs={{0,1},{1,0},{2,3},{3,2},{4,5},{5,4},{6,7},{7,6},{8,9},{9,8},{10,11... | collective-permute-start | bytes 368648 | tf_op jit(solution)/shard_map/ppermute | solution.py:242
  16.9 4.7 %collective-permute-done.1.refs_1_.refs_5_ = bf16[2,8,3840]{2,1,0:T(8,128)(2,1)S(1)} collective-permute-done((bf16[2,8,3840]{2,1,0:T(8,128)(2,1)S(1)}, bf16[2,8,3840]{2,1,0:T(8,128)(2,1)S(1)}, u32[]{:S(2)}, u32[]{:S(2)}) %collective-permute-start.1) | collective-permute-done | bytes 122912 | tf_op jit(solution)/shard_map/ppermute | solution.py:242
  21.6 3.4 %collective-permute-start.7 = (bf16[2,8,3840]{2,1,0:T(8,128)(2,1)S(1)}, bf16[2,8,3840]{2,1,0:T(8,128)(2,1)S(1)}, u32[]{:S(2)}, u32[]{:S(2)}) collective-permute-start(bf16[2,8,3840]{2,1,0:T(8,128)(2,1)S(1)} %get-tuple-element.39), channel_id=1, source_target_pairs={{0,19},{1,18},{2,17},{3,16},{4,23},{5,22},{6,21},{7,20},{8,27},{9,... | collective-permute-start | bytes 368648 | tf_op jit(solution)/shard_map/ppermute | solution.py:242
  25.0 1.5 %collective-permute-start.8 = (bf16[2,8,3840]{2,1,0:T(8,128)(2,1)S(1)}, bf16[2,8,3840]{2,1,0:T(8,128)(2,1)S(1)}, u32[]{:S(2)}, u32[]{:S(2)}) collective-permute-start(bf16[2,8,3840]{2,1,0:T(8,128)(2,1)S(1)} %get-tuple-element.40), channel_id=1, source_target_pairs={{0,8},{1,9},{2,10},{3,11},{4,12},{5,13},{6,14},{7,15},{8,0},{9,1},... | collective-permute-start | bytes 368648 | tf_op jit(solution)/shard_map/ppermute | solution.py:242
  26.5 2.8 %collective-permute-start.10 = (bf16[2,8,3840]{2,1,0:T(8,128)(2,1)S(1)}, bf16[2,8,3840]{2,1,0:T(8,128)(2,1)S(1)}, u32[]{:S(2)}, u32[]{:S(2)}) collective-permute-start(bf16[2,8,3840]{2,1,0:T(8,128)(2,1)S(1)} %get-tuple-element.42), channel_id=1, source_target_pairs={{0,26},{1,27},{2,24},{3,25},{4,30},{5,31},{6,28},{7,29},{8,18},{9,... | collective-permute-start | bytes 368648 | tf_op jit(solution)/shard_map/ppermute | solution.py:242
  29.3 0.0 collective-permute-done.6.refs_4_.refs_5_
  29.4 0.1 collective-permute-start.12
  29.4 0.8 %collective-permute-done.7.refs_10_.refs_6_ = bf16[2,8,3840]{2,1,0:T(8,128)(2,1)S(1)} collective-permute-done((bf16[2,8,3840]{2,1,0:T(8,128)(2,1)S(1)}, bf16[2,8,3840]{2,1,0:T(8,128)(2,1)S(1)}, u32[]{:S(2)}, u32[]{:S(2)}) %collective-permute-start.7) | collective-permute-done | bytes 122912 | tf_op jit(solution)/shard_map/ppermute | solution.py:242
  30.2 2.9 %collective-permute-start.11 = (bf16[2,8,3840]{2,1,0:T(8,128)(2,1)S(1)}, bf16[2,8,3840]{2,1,0:T(8,128)(2,1)S(1)}, u32[]{:S(2)}, u32[]{:S(2)}) collective-permute-start(bf16[2,8,3840]{2,1,0:T(8,128)(2,1)S(1)} %get-tuple-element.43), channel_id=1, source_target_pairs={{0,24},{1,25},{2,26},{3,27},{4,28},{5,29},{6,30},{7,31},{8,16},{9,... | collective-permute-start | bytes 368648 | tf_op jit(solution)/shard_map/ppermute | solution.py:242
  33.1 0.1 collective-permute-done.8.refs_7_.refs_18_
  33.2 1.7 %collective-permute-start.13 = (bf16[2,8,3840]{2,1,0:T(8,128)(2,1)S(1)}, bf16[2,8,3840]{2,1,0:T(8,128)(2,1)S(1)}, u32[]{:S(2)}, u32[]{:S(2)}) collective-permute-start(bf16[2,8,3840]{2,1,0:T(8,128)(2,1)S(1)} %get-tuple-element.46), channel_id=1, source_target_pairs={{0,27},{1,26},{2,25},{3,24},{4,31},{5,30},{6,29},{7,28},{8,19},{9,... | collective-permute-start | bytes 368648 | tf_op jit(solution)/shard_map/ppermute | solution.py:242
  34.9 0.0 collective-permute-done.9.refs_8_.refs_19_
  34.9 0.0 collective-permute-start.14
  35.0 1.8 %collective-permute-done.10.refs_9_.refs_24_ = bf16[2,8,3840]{2,1,0:T(8,128)(2,1)S(1)} collective-permute-done((bf16[2,8,3840]{2,1,0:T(8,128)(2,1)S(1)}, bf16[2,8,3840]{2,1,0:T(8,128)(2,1)S(1)}, u32[]{:S(2)}, u32[]{:S(2)}) %collective-permute-start.10) | collective-permute-done | bytes 122912 | tf_op jit(solution)/shard_map/ppermute | solution.py:242
  36.8 4.7 %collective-permute-start.15 = (bf16[2,8,3840]{2,1,0:T(8,128)(2,1)S(1)}, bf16[2,8,3840]{2,1,0:T(8,128)(2,1)S(1)}, u32[]{:S(2)}, u32[]{:S(2)}) collective-permute-start(bf16[2,8,3840]{2,1,0:T(8,128)(2,1)S(1)} %get-tuple-element.48), channel_id=1, source_target_pairs={{0,25},{1,24},{2,27},{3,26},{4,29},{5,28},{6,31},{7,30},{8,17},{9,... | collective-permute-start | bytes 368648 | tf_op jit(solution)/shard_map/ppermute | solution.py:242
  41.5 1.1 %collective-permute-start.16 = (bf16[2,8,3840]{2,1,0:T(8,128)(2,1)S(1)}, bf16[2,8,3840]{2,1,0:T(8,128)(2,1)S(1)}, u32[]{:S(2)}, u32[]{:S(2)}) collective-permute-start(bf16[2,8,3840]{2,1,0:T(8,128)(2,1)S(1)} %get-tuple-element.49), channel_id=1, source_target_pairs={{0,11},{1,10},{2,9},{3,8},{4,15},{5,14},{6,13},{7,12},{8,3},{9,2},... | collective-permute-start | bytes 368648 | tf_op jit(solution)/shard_map/ppermute | solution.py:242
  42.6 0.3 copy.5.refs_1_.refs_17_
  43.0 1.0 %shard_map.41.refs_26_ = f32[4,2,48,129]{3,2,1,0:T(8,128)S(1)} custom-call(s32[1,128]{1,0:T(1,128)S(1)} %bitcast.3, bf16[4,2,129,1280]{3,2,1,0:T(8,128)(2,1)S(1)} %copy.5.refs_1_.refs_17_, bf16[8,3840]{1,0:T(8,128)(2,1)S(1)} %get-tuple-element.50.refs_2_, bf16[14,8,3840]{2,1,0:T(8,128)(2,1)S(1)} %collective-permute-done.2.theirs_ref.refs_3_, ...), custom_call_target="tpu_custom_call" | custom-call | tf_op jit(solution)/shard_map/pallas_call | solution.py:218
  43.9 5.6 %collective-permute-done.14.refs_13_.refs_20_ = bf16[2,8,3840]{2,1,0:T(8,128)(2,1)S(1)} collective-permute-done((bf16[2,8,3840]{2,1,0:T(8,128)(2,1)S(1)}, bf16[2,8,3840]{2,1,0:T(8,128)(2,1)S(1)}, u32[]{:S(2)}, u32[]{:S(2)}) %collective-permute-start.14) | collective-permute-done | bytes 122912 | tf_op jit(solution)/shard_map/ppermute | solution.py:242
  49.5 0.0 collective-permute-done.15.refs_14_.refs_23_
  49.5 0.0 collective-permute-done.16.refs_15_.refs_21_
  49.5 1.7 %shard_map.42 = bf16[4,2,48,129]{3,2,1,0:T(8,128)(2,1)} custom-call(bf16[2,8,3840]{2,1,0:T(8,128)(2,1)S(1)} %collective-permute-done.refs_0_.refs_6_, bf16[2,8,3840]{2,1,0:T(8,128)(2,1)S(1)} %collective-permute-done.1.refs_1_.refs_5_, bf16[2,8,3840]{2,1,0:T(8,128)(2,1)S(1)} %collective-permute-done.3.refs_8_.refs_2_, ...), custom_call_target="tpu_custom_call" | custom-call | tf_op jit(solution)/shard_map/pallas_call | solution.py:218
  (13 shorter events, 0.0 us)
Async XLA Ops:
  0.0 1.5 %copy-start = (s32[128]{0:T(128)S(1)}, s32[128]{0:T(128)}, u32[]{:S(2)}) copy-start(s32[128]{0:T(128)} %param.4) | copy-start | bytes 1540
  1.5 41.1 %copy-start.1 = (bf16[4,2,129,1280]{3,1,2,0:T(2,128)(2,1)S(1)}, bf16[4,2,129,1280]{3,1,2,0:T(2,128)(2,1)}, u32[]{:S(2)}) copy-start(bf16[4,2,129,1280]{3,1,2,0:T(2,128)(2,1)} %param.5) | copy-start | bytes 7925764
  2.3 5.2 %collective-permute-start.2 = (bf16[14,8,3840]{2,1,0:T(8,128)(2,1)S(1)}, bf16[14,8,3840]{2,1,0:T(8,128)(2,1)S(1)}, u32[]{:S(2)}, u32[]{:S(2)}) collective-permute-start(bf16[14,8,3840]{2,1,0:T(8,128)(2,1)S(1)} %get-tuple-element.33), channel_id=1, source_target_pairs={{0,4},{1,5},{2,6},{3,7},{4,0},{5,1},{6,2},{7,3},{8,12},{9,13},{10,... | collective-permute-start | bytes 2580488 | tf_op jit(solution)/shard_map/ppermute | solution.py:242
  2.8 10.1 %collective-permute-start = (bf16[2,8,3840]{2,1,0:T(8,128)(2,1)S(1)}, bf16[2,8,3840]{2,1,0:T(8,128)(2,1)S(1)}, u32[]{:S(2)}, u32[]{:S(2)}) collective-permute-start(bf16[2,8,3840]{2,1,0:T(8,128)(2,1)S(1)} %get-tuple-element.30), channel_id=1, source_target_pairs={{0,3},{1,2},{2,1},{3,0},{4,7},{5,6},{6,5},{7,4},{8,11},{9,10},{10,... | collective-permute-start | bytes 368648 | tf_op jit(solution)/shard_map/ppermute | solution.py:242
  7.5 14.1 %collective-permute-start.1 = (bf16[2,8,3840]{2,1,0:T(8,128)(2,1)S(1)}, bf16[2,8,3840]{2,1,0:T(8,128)(2,1)S(1)}, u32[]{:S(2)}, u32[]{:S(2)}) collective-permute-start(bf16[2,8,3840]{2,1,0:T(8,128)(2,1)S(1)} %get-tuple-element.31), channel_id=1, source_target_pairs={{0,2},{1,3},{2,0},{3,1},{4,6},{5,7},{6,4},{7,5},{8,10},{9,11},{10,... | collective-permute-start | bytes 368648 | tf_op jit(solution)/shard_map/ppermute | solution.py:242
  7.6 17.4 %collective-permute-start.3 = (bf16[2,8,3840]{2,1,0:T(8,128)(2,1)S(1)}, bf16[2,8,3840]{2,1,0:T(8,128)(2,1)S(1)}, u32[]{:S(2)}, u32[]{:S(2)}) collective-permute-start(bf16[2,8,3840]{2,1,0:T(8,128)(2,1)S(1)} %get-tuple-element.34), channel_id=1, source_target_pairs={{0,17},{1,16},{2,19},{3,18},{4,21},{5,20},{6,23},{7,22},{8,25},{9,... | collective-permute-start | bytes 368648 | tf_op jit(solution)/shard_map/ppermute | solution.py:242
  9.4 17.1 %collective-permute-start.4 = (bf16[2,8,3840]{2,1,0:T(8,128)(2,1)S(1)}, bf16[2,8,3840]{2,1,0:T(8,128)(2,1)S(1)}, u32[]{:S(2)}, u32[]{:S(2)}) collective-permute-start(bf16[2,8,3840]{2,1,0:T(8,128)(2,1)S(1)} %get-tuple-element.36), channel_id=1, source_target_pairs={{0,16},{1,17},{2,18},{3,19},{4,20},{5,21},{6,22},{7,23},{8,24},{9,... | collective-permute-start | bytes 368648 | tf_op jit(solution)/shard_map/ppermute | solution.py:242
  9.8 16.7 %collective-permute-start.5 = (bf16[2,8,3840]{2,1,0:T(8,128)(2,1)S(1)}, bf16[2,8,3840]{2,1,0:T(8,128)(2,1)S(1)}, u32[]{:S(2)}, u32[]{:S(2)}) collective-permute-start(bf16[2,8,3840]{2,1,0:T(8,128)(2,1)S(1)} %get-tuple-element.37), channel_id=1, source_target_pairs={{0,18},{1,19},{2,16},{3,17},{4,22},{5,23},{6,20},{7,21},{8,26},{9,... | collective-permute-start | bytes 368648 | tf_op jit(solution)/shard_map/ppermute | solution.py:242
  13.0 16.4 %collective-permute-start.6 = (bf16[2,8,3840]{2,1,0:T(8,128)(2,1)S(1)}, bf16[2,8,3840]{2,1,0:T(8,128)(2,1)S(1)}, u32[]{:S(2)}, u32[]{:S(2)}) collective-permute-start(bf16[2,8,3840]{2,1,0:T(8,128)(2,1)S(1)} %get-tuple-element.38), channel_id=1, source_target_pairs={{0,1},{1,0},{2,3},{3,2},{4,5},{5,4},{6,7},{7,6},{8,9},{9,8},{10,11... | collective-permute-start | bytes 368648 | tf_op jit(solution)/shard_map/ppermute | solution.py:242
  21.6 8.6 %collective-permute-start.7 = (bf16[2,8,3840]{2,1,0:T(8,128)(2,1)S(1)}, bf16[2,8,3840]{2,1,0:T(8,128)(2,1)S(1)}, u32[]{:S(2)}, u32[]{:S(2)}) collective-permute-start(bf16[2,8,3840]{2,1,0:T(8,128)(2,1)S(1)} %get-tuple-element.39), channel_id=1, source_target_pairs={{0,19},{1,18},{2,17},{3,16},{4,23},{5,22},{6,21},{7,20},{8,27},{9,... | collective-permute-start | bytes 368648 | tf_op jit(solution)/shard_map/ppermute | solution.py:242
  25.0 8.2 %collective-permute-start.8 = (bf16[2,8,3840]{2,1,0:T(8,128)(2,1)S(1)}, bf16[2,8,3840]{2,1,0:T(8,128)(2,1)S(1)}, u32[]{:S(2)}, u32[]{:S(2)}) collective-permute-start(bf16[2,8,3840]{2,1,0:T(8,128)(2,1)S(1)} %get-tuple-element.40), channel_id=1, source_target_pairs={{0,8},{1,9},{2,10},{3,11},{4,12},{5,13},{6,14},{7,15},{8,0},{9,1},... | collective-permute-start | bytes 368648 | tf_op jit(solution)/shard_map/ppermute | solution.py:242
  26.5 8.4 %collective-permute-start.9 = (bf16[2,8,3840]{2,1,0:T(8,128)(2,1)S(1)}, bf16[2,8,3840]{2,1,0:T(8,128)(2,1)S(1)}, u32[]{:S(2)}, u32[]{:S(2)}) collective-permute-start(bf16[2,8,3840]{2,1,0:T(8,128)(2,1)S(1)} %get-tuple-element.41), channel_id=1, source_target_pairs={{0,9},{1,8},{2,11},{3,10},{4,13},{5,12},{6,15},{7,14},{8,1},{9,0},... | collective-permute-start | bytes 368648 | tf_op jit(solution)/shard_map/ppermute | solution.py:242
  26.5 10.2 %collective-permute-start.10 = (bf16[2,8,3840]{2,1,0:T(8,128)(2,1)S(1)}, bf16[2,8,3840]{2,1,0:T(8,128)(2,1)S(1)}, u32[]{:S(2)}, u32[]{:S(2)}) collective-permute-start(bf16[2,8,3840]{2,1,0:T(8,128)(2,1)S(1)} %get-tuple-element.42), channel_id=1, source_target_pairs={{0,26},{1,27},{2,24},{3,25},{4,30},{5,31},{6,28},{7,29},{8,18},{9,... | collective-permute-start | bytes 368648 | tf_op jit(solution)/shard_map/ppermute | solution.py:242
  29.4 12.1 %collective-permute-start.12 = (bf16[2,8,3840]{2,1,0:T(8,128)(2,1)S(1)}, bf16[2,8,3840]{2,1,0:T(8,128)(2,1)S(1)}, u32[]{:S(2)}, u32[]{:S(2)}) collective-permute-start(bf16[2,8,3840]{2,1,0:T(8,128)(2,1)S(1)} %shard_map.40), channel_id=1, source_target_pairs={{0,4},{1,5},{2,6},{3,7},{4,0},{5,1},{6,2},{7,3},{8,12},{9,13},{10,... | collective-permute-start | bytes 368648 | tf_op jit(solution)/shard_map/ppermute | solution.py:242
  30.2 13.7 %collective-permute-start.11 = (bf16[2,8,3840]{2,1,0:T(8,128)(2,1)S(1)}, bf16[2,8,3840]{2,1,0:T(8,128)(2,1)S(1)}, u32[]{:S(2)}, u32[]{:S(2)}) collective-permute-start(bf16[2,8,3840]{2,1,0:T(8,128)(2,1)S(1)} %get-tuple-element.43), channel_id=1, source_target_pairs={{0,24},{1,25},{2,26},{3,27},{4,28},{5,29},{6,30},{7,31},{8,16},{9,... | collective-permute-start | bytes 368648 | tf_op jit(solution)/shard_map/ppermute | solution.py:242
  33.2 10.7 %collective-permute-start.13 = (bf16[2,8,3840]{2,1,0:T(8,128)(2,1)S(1)}, bf16[2,8,3840]{2,1,0:T(8,128)(2,1)S(1)}, u32[]{:S(2)}, u32[]{:S(2)}) collective-permute-start(bf16[2,8,3840]{2,1,0:T(8,128)(2,1)S(1)} %get-tuple-element.46), channel_id=1, source_target_pairs={{0,27},{1,26},{2,25},{3,24},{4,31},{5,30},{6,29},{7,28},{8,19},{9,... | collective-permute-start | bytes 368648 | tf_op jit(solution)/shard_map/ppermute | solution.py:242
  34.9 14.6 %collective-permute-start.14 = (bf16[2,8,3840]{2,1,0:T(8,128)(2,1)S(1)}, bf16[2,8,3840]{2,1,0:T(8,128)(2,1)S(1)}, u32[]{:S(2)}, u32[]{:S(2)}) collective-permute-start(bf16[2,8,3840]{2,1,0:T(8,128)(2,1)S(1)} %get-tuple-element.47), channel_id=1, source_target_pairs={{0,10},{1,11},{2,8},{3,9},{4,14},{5,15},{6,12},{7,13},{8,2},{9,3},... | collective-permute-start | bytes 368648 | tf_op jit(solution)/shard_map/ppermute | solution.py:242
  36.8 12.7 %collective-permute-start.15 = (bf16[2,8,3840]{2,1,0:T(8,128)(2,1)S(1)}, bf16[2,8,3840]{2,1,0:T(8,128)(2,1)S(1)}, u32[]{:S(2)}, u32[]{:S(2)}) collective-permute-start(bf16[2,8,3840]{2,1,0:T(8,128)(2,1)S(1)} %get-tuple-element.48), channel_id=1, source_target_pairs={{0,25},{1,24},{2,27},{3,26},{4,29},{5,28},{6,31},{7,30},{8,17},{9,... | collective-permute-start | bytes 368648 | tf_op jit(solution)/shard_map/ppermute | solution.py:242
  41.5 8.1 %collective-permute-start.16 = (bf16[2,8,3840]{2,1,0:T(8,128)(2,1)S(1)}, bf16[2,8,3840]{2,1,0:T(8,128)(2,1)S(1)}, u32[]{:S(2)}, u32[]{:S(2)}) collective-permute-start(bf16[2,8,3840]{2,1,0:T(8,128)(2,1)S(1)} %get-tuple-element.49), channel_id=1, source_target_pairs={{0,11},{1,10},{2,9},{3,8},{4,15},{5,14},{6,13},{7,12},{8,3},{9,2},... | collective-permute-start | bytes 368648 | tf_op jit(solution)/shard_map/ppermute | solution.py:242

commit v7 on v6

--- a/solution.py
+++ b/solution.py
@@ -194,15 +194,20 @@
                 jnp.concatenate([t[pl.ds(2 * s + w, rows, stride=8), :] for t in tiles], 1)
                 for w in range(2)
             ]
+            even = tables_ref.shape[2] - 1
             products = lax.dot_general(
                 jnp.concatenate(picked, 0).astype(jnp.bfloat16),
-                tables_ref[s, e, :, lanes],
+                tables_ref[s, e, :even, lanes],
                 NT,
                 preferred_element_type=jnp.float32,
             )
+            row = tables_ref[s, e, even:, lanes].astype(jnp.float32)
+            second = picked[1].astype(jnp.bfloat16).astype(jnp.float32)
+            final = jnp.sum(second * row, axis=1, keepdims=True)
             count = (width - pair - e + 1) >> 1
-            degree = lax.broadcasted_iota(jnp.int32, (rows, products.shape[1]), 1)
+            degree = lax.broadcasted_iota(jnp.int32, (rows, even), 1)
             chosen = jnp.where(degree < count, products[:rows], products[rows:])
+            chosen = jnp.concatenate([chosen, final], 1)
             if levs < 4:
                 parts = [jnp.where(low, chosen, 0.0), jnp.where(low, 0.0, chosen)]
                 chosen = jnp.concatenate(parts, 0)

time: 51.3 us -> 51.3 us (level)
  no operation moved by 1% of the time
where the time goes in v7:
time: 51.3 us; the launch traced here: 51.2 us
  starting transfers between devices  32.7 us (64%)
  waiting for transfers between devices  13 us (25%)
  Pallas kernels  4.98 us (10%)
    ppermute x17, starting transfers between devices, send(): lax.ppermute(piece, ('lat', 'lev'), [(i, i ^ distance) for i in range(cou...  32.7 us
    ppermute x17, waiting for transfers between devices, send(): lax.ppermute(piece, ('lat', 'lev'), [(i, i ^ distance) for i in range(cou...  13 us
    pallas_call x2, Pallas kernels, transform(): pl.pallas_call(functools.partial(transform_kernel, skip=len(rest), far=fa...  2.58 us
    pallas_call x1, Pallas kernels, load(): pl.pallas_call(load_kernel, in_specs=[HBM], out_specs=[VMEM] * 2, out_sha...  1.5 us
  transfers between devices with their start and end apart: 17, of which 5 were waited for; matrix products, arithmetic and copies ran while one was open for 1% of the time, Pallas kernels for 2%

profile of v7, /device:TPU:0, one launch (start us, length us, event | category | flops | bytes accessed | tf_op | source)
XLA Modules:
  0.0 51.2 jit_solution(1904731155710592386)
XLA Ops:
  0.0 1.5 %shard_map.37 = (bf16[12,256,256]{2,1,0:T(8,128)(2,1)S(1)}, bf16[12,64,256]{2,1,0:T(8,128)(2,1)S(1)}) custom-call(bf16[12,320,256]{2,1,0:T(8,128)(2,1)} %bitcast.5), custom_call_target="tpu_custom_call" | custom-call | flops 1000000000 | bytes 3932160 | tf_op jit(solution)/shard_map/pallas_call | solution.py:44
  1.5 0.0 copy-start.1
  1.5 0.8 %shard_map.38 = (bf16[13,8,3840]{2,1,0:T(8,128)(2,1)S(1)}, bf16[14,8,3840]{2,1,0:T(8,128)(2,1)S(1)}, bf16[8,3840]{1,0:T(8,128)(2,1)S(1)}, bf16[2,8,3840]{2,1,0:T(8,128)(2,1)S(1)}, bf16[2,8,3840]{2,1,0:T(8,128)(2,1)S(1)}) custom-call(s32[1,128]{1,0:T(1,128)S(1)} %bitcast.2, bf16[12,256,256]{2,1,0:T(8,128)(2,1)S(1)} %get-tuple-element.28.wide_ref, ...), custom_call_target="tpu_custom_call" | custom-call | tf_op jit(solution)/shard_map/pallas_call | solution.py:93
  2.3 0.5 collective-permute-start.2
  2.8 4.7 %collective-permute-start = (bf16[2,8,3840]{2,1,0:T(8,128)(2,1)S(1)}, bf16[2,8,3840]{2,1,0:T(8,128)(2,1)S(1)}, u32[]{:S(2)}, u32[]{:S(2)}) collective-permute-start(bf16[2,8,3840]{2,1,0:T(8,128)(2,1)S(1)} %get-tuple-element.30), channel_id=1, source_target_pairs={{0,3},{1,2},{2,1},{3,0},{4,7},{5,6},{6,5},{7,4},{8,11},{9,10},{10,... | collective-permute-start | bytes 368648 | tf_op jit(solution)/shard_map/ppermute | solution.py:247
  7.5 0.1 shard_map.39
  7.6 1.8 %collective-permute-start.3 = (bf16[2,8,3840]{2,1,0:T(8,128)(2,1)S(1)}, bf16[2,8,3840]{2,1,0:T(8,128)(2,1)S(1)}, u32[]{:S(2)}, u32[]{:S(2)}) collective-permute-start(bf16[2,8,3840]{2,1,0:T(8,128)(2,1)S(1)} %get-tuple-element.34), channel_id=1, source_target_pairs={{0,17},{1,16},{2,19},{3,18},{4,21},{5,20},{6,23},{7,22},{8,25},{9,... | collective-permute-start | bytes 368648 | tf_op jit(solution)/shard_map/ppermute | solution.py:247
  9.4 0.4 collective-permute-start.4
  9.8 3.2 %collective-permute-start.5 = (bf16[2,8,3840]{2,1,0:T(8,128)(2,1)S(1)}, bf16[2,8,3840]{2,1,0:T(8,128)(2,1)S(1)}, u32[]{:S(2)}, u32[]{:S(2)}) collective-permute-start(bf16[2,8,3840]{2,1,0:T(8,128)(2,1)S(1)} %get-tuple-element.37), channel_id=1, source_target_pairs={{0,18},{1,19},{2,16},{3,17},{4,22},{5,23},{6,20},{7,21},{8,26},{9,... | collective-permute-start | bytes 368648 | tf_op jit(solution)/shard_map/ppermute | solution.py:247
  13.0 0.0 collective-permute-done.refs_0_.refs_6_
  13.0 3.9 %collective-permute-start.6 = (bf16[2,8,3840]{2,1,0:T(8,128)(2,1)S(1)}, bf16[2,8,3840]{2,1,0:T(8,128)(2,1)S(1)}, u32[]{:S(2)}, u32[]{:S(2)}) collective-permute-start(bf16[2,8,3840]{2,1,0:T(8,128)(2,1)S(1)} %get-tuple-element.38), channel_id=1, source_target_pairs={{0,1},{1,0},{2,3},{3,2},{4,5},{5,4},{6,7},{7,6},{8,9},{9,8},{10,11... | collective-permute-start | bytes 368648 | tf_op jit(solution)/shard_map/ppermute | solution.py:247
  16.9 4.7 %collective-permute-done.1.refs_1_.refs_5_ = bf16[2,8,3840]{2,1,0:T(8,128)(2,1)S(1)} collective-permute-done((bf16[2,8,3840]{2,1,0:T(8,128)(2,1)S(1)}, bf16[2,8,3840]{2,1,0:T(8,128)(2,1)S(1)}, u32[]{:S(2)}, u32[]{:S(2)}) %collective-permute-start.1) | collective-permute-done | bytes 122912 | tf_op jit(solution)/shard_map/ppermute | solution.py:247
  21.6 3.4 %collective-permute-start.7 = (bf16[2,8,3840]{2,1,0:T(8,128)(2,1)S(1)}, bf16[2,8,3840]{2,1,0:T(8,128)(2,1)S(1)}, u32[]{:S(2)}, u32[]{:S(2)}) collective-permute-start(bf16[2,8,3840]{2,1,0:T(8,128)(2,1)S(1)} %get-tuple-element.39), channel_id=1, source_target_pairs={{0,19},{1,18},{2,17},{3,16},{4,23},{5,22},{6,21},{7,20},{8,27},{9,... | collective-permute-start | bytes 368648 | tf_op jit(solution)/shard_map/ppermute | solution.py:247
  25.0 1.5 %collective-permute-start.8 = (bf16[2,8,3840]{2,1,0:T(8,128)(2,1)S(1)}, bf16[2,8,3840]{2,1,0:T(8,128)(2,1)S(1)}, u32[]{:S(2)}, u32[]{:S(2)}) collective-permute-start(bf16[2,8,3840]{2,1,0:T(8,128)(2,1)S(1)} %get-tuple-element.40), channel_id=1, source_target_pairs={{0,8},{1,9},{2,10},{3,11},{4,12},{5,13},{6,14},{7,15},{8,0},{9,1},... | collective-permute-start | bytes 368648 | tf_op jit(solution)/shard_map/ppermute | solution.py:247
  26.5 2.8 %collective-permute-start.10 = (bf16[2,8,3840]{2,1,0:T(8,128)(2,1)S(1)}, bf16[2,8,3840]{2,1,0:T(8,128)(2,1)S(1)}, u32[]{:S(2)}, u32[]{:S(2)}) collective-permute-start(bf16[2,8,3840]{2,1,0:T(8,128)(2,1)S(1)} %get-tuple-element.42), channel_id=1, source_target_pairs={{0,26},{1,27},{2,24},{3,25},{4,30},{5,31},{6,28},{7,29},{8,18},{9,... | collective-permute-start | bytes 368648 | tf_op jit(solution)/shard_map/ppermute | solution.py:247
  29.3 0.0 collective-permute-done.6.refs_4_.refs_5_
  29.4 0.1 collective-permute-start.12
  29.4 0.8 %collective-permute-done.7.refs_10_.refs_6_ = bf16[2,8,3840]{2,1,0:T(8,128)(2,1)S(1)} collective-permute-done((bf16[2,8,3840]{2,1,0:T(8,128)(2,1)S(1)}, bf16[2,8,3840]{2,1,0:T(8,128)(2,1)S(1)}, u32[]{:S(2)}, u32[]{:S(2)}) %collective-permute-start.7) | collective-permute-done | bytes 122912 | tf_op jit(solution)/shard_map/ppermute | solution.py:247
  30.2 2.9 %collective-permute-start.11 = (bf16[2,8,3840]{2,1,0:T(8,128)(2,1)S(1)}, bf16[2,8,3840]{2,1,0:T(8,128)(2,1)S(1)}, u32[]{:S(2)}, u32[]{:S(2)}) collective-permute-start(bf16[2,8,3840]{2,1,0:T(8,128)(2,1)S(1)} %get-tuple-element.43), channel_id=1, source_target_pairs={{0,24},{1,25},{2,26},{3,27},{4,28},{5,29},{6,30},{7,31},{8,16},{9,... | collective-permute-start | bytes 368648 | tf_op jit(solution)/shard_map/ppermute | solution.py:247
  33.1 0.1 collective-permute-done.8.refs_7_.refs_18_
  33.2 1.7 %collective-permute-start.13 = (bf16[2,8,3840]{2,1,0:T(8,128)(2,1)S(1)}, bf16[2,8,3840]{2,1,0:T(8,128)(2,1)S(1)}, u32[]{:S(2)}, u32[]{:S(2)}) collective-permute-start(bf16[2,8,3840]{2,1,0:T(8,128)(2,1)S(1)} %get-tuple-element.46), channel_id=1, source_target_pairs={{0,27},{1,26},{2,25},{3,24},{4,31},{5,30},{6,29},{7,28},{8,19},{9,... | collective-permute-start | bytes 368648 | tf_op jit(solution)/shard_map/ppermute | solution.py:247
  34.9 0.0 collective-permute-done.9.refs_8_.refs_19_
  34.9 0.0 collective-permute-start.14
  35.0 1.8 %collective-permute-done.10.refs_9_.refs_24_ = bf16[2,8,3840]{2,1,0:T(8,128)(2,1)S(1)} collective-permute-done((bf16[2,8,3840]{2,1,0:T(8,128)(2,1)S(1)}, bf16[2,8,3840]{2,1,0:T(8,128)(2,1)S(1)}, u32[]{:S(2)}, u32[]{:S(2)}) %collective-permute-start.10) | collective-permute-done | bytes 122912 | tf_op jit(solution)/shard_map/ppermute | solution.py:247
  36.8 4.7 %collective-permute-start.15 = (bf16[2,8,3840]{2,1,0:T(8,128)(2,1)S(1)}, bf16[2,8,3840]{2,1,0:T(8,128)(2,1)S(1)}, u32[]{:S(2)}, u32[]{:S(2)}) collective-permute-start(bf16[2,8,3840]{2,1,0:T(8,128)(2,1)S(1)} %get-tuple-element.48), channel_id=1, source_target_pairs={{0,25},{1,24},{2,27},{3,26},{4,29},{5,28},{6,31},{7,30},{8,17},{9,... | collective-permute-start | bytes 368648 | tf_op jit(solution)/shard_map/ppermute | solution.py:247
  41.5 1.1 %collective-permute-start.16 = (bf16[2,8,3840]{2,1,0:T(8,128)(2,1)S(1)}, bf16[2,8,3840]{2,1,0:T(8,128)(2,1)S(1)}, u32[]{:S(2)}, u32[]{:S(2)}) collective-permute-start(bf16[2,8,3840]{2,1,0:T(8,128)(2,1)S(1)} %get-tuple-element.49), channel_id=1, source_target_pairs={{0,11},{1,10},{2,9},{3,8},{4,15},{5,14},{6,13},{7,12},{8,3},{9,2},... | collective-permute-start | bytes 368648 | tf_op jit(solution)/shard_map/ppermute | solution.py:247
  42.6 0.3 copy.5.refs_1_.refs_17_
  43.0 0.9 %shard_map.41.refs_26_ = f32[4,2,48,129]{3,2,1,0:T(8,128)S(1)} custom-call(s32[1,128]{1,0:T(1,128)S(1)} %bitcast.3, bf16[4,2,129,1280]{3,2,1,0:T(8,128)(2,1)S(1)} %copy.5.refs_1_.refs_17_, bf16[8,3840]{1,0:T(8,128)(2,1)S(1)} %get-tuple-element.50.refs_2_, bf16[14,8,3840]{2,1,0:T(8,128)(2,1)S(1)} %collective-permute-done.2.theirs_ref.refs_3_, ...), custom_call_target="tpu_custom_call" | custom-call | tf_op jit(solution)/shard_map/pallas_call | solution.py:223
  43.9 0.0 collective-permute-done.11.refs_10_.refs_22_
  43.9 0.0 collective-permute-done.13.refs_12_.refs_25_
  43.9 5.6 %collective-permute-done.14.refs_13_.refs_20_ = bf16[2,8,3840]{2,1,0:T(8,128)(2,1)S(1)} collective-permute-done((bf16[2,8,3840]{2,1,0:T(8,128)(2,1)S(1)}, bf16[2,8,3840]{2,1,0:T(8,128)(2,1)S(1)}, u32[]{:S(2)}, u32[]{:S(2)}) %collective-permute-start.14) | collective-permute-done | bytes 122912 | tf_op jit(solution)/shard_map/ppermute | solution.py:247
  49.5 1.7 %shard_map.42 = bf16[4,2,48,129]{3,2,1,0:T(8,128)(2,1)} custom-call(bf16[2,8,3840]{2,1,0:T(8,128)(2,1)S(1)} %collective-permute-done.refs_0_.refs_6_, bf16[2,8,3840]{2,1,0:T(8,128)(2,1)S(1)} %collective-permute-done.1.refs_1_.refs_5_, bf16[2,8,3840]{2,1,0:T(8,128)(2,1)S(1)} %collective-permute-done.3.refs_8_.refs_2_, ...), custom_call_target="tpu_custom_call" | custom-call | tf_op jit(solution)/shard_map/pallas_call | solution.py:223
  (13 shorter events, 0.0 us)
Async XLA Ops:
  0.0 1.5 %copy-start = (s32[128]{0:T(128)S(1)}, s32[128]{0:T(128)}, u32[]{:S(2)}) copy-start(s32[128]{0:T(128)} %param.4) | copy-start | bytes 1540
  1.5 41.1 %copy-start.1 = (bf16[4,2,129,1280]{3,1,2,0:T(2,128)(2,1)S(1)}, bf16[4,2,129,1280]{3,1,2,0:T(2,128)(2,1)}, u32[]{:S(2)}) copy-start(bf16[4,2,129,1280]{3,1,2,0:T(2,128)(2,1)} %param.5) | copy-start | bytes 7925764
  2.3 5.2 %collective-permute-start.2 = (bf16[14,8,3840]{2,1,0:T(8,128)(2,1)S(1)}, bf16[14,8,3840]{2,1,0:T(8,128)(2,1)S(1)}, u32[]{:S(2)}, u32[]{:S(2)}) collective-permute-start(bf16[14,8,3840]{2,1,0:T(8,128)(2,1)S(1)} %get-tuple-element.33), channel_id=1, source_target_pairs={{0,4},{1,5},{2,6},{3,7},{4,0},{5,1},{6,2},{7,3},{8,12},{9,13},{10,... | collective-permute-start | bytes 2580488 | tf_op jit(solution)/shard_map/ppermute | solution.py:247
  2.8 10.1 %collective-permute-start = (bf16[2,8,3840]{2,1,0:T(8,128)(2,1)S(1)}, bf16[2,8,3840]{2,1,0:T(8,128)(2,1)S(1)}, u32[]{:S(2)}, u32[]{:S(2)}) collective-permute-start(bf16[2,8,3840]{2,1,0:T(8,128)(2,1)S(1)} %get-tuple-element.30), channel_id=1, source_target_pairs={{0,3},{1,2},{2,1},{3,0},{4,7},{5,6},{6,5},{7,4},{8,11},{9,10},{10,... | collective-permute-start | bytes 368648 | tf_op jit(solution)/shard_map/ppermute | solution.py:247
  7.5 14.1 %collective-permute-start.1 = (bf16[2,8,3840]{2,1,0:T(8,128)(2,1)S(1)}, bf16[2,8,3840]{2,1,0:T(8,128)(2,1)S(1)}, u32[]{:S(2)}, u32[]{:S(2)}) collective-permute-start(bf16[2,8,3840]{2,1,0:T(8,128)(2,1)S(1)} %get-tuple-element.31), channel_id=1, source_target_pairs={{0,2},{1,3},{2,0},{3,1},{4,6},{5,7},{6,4},{7,5},{8,10},{9,11},{10,... | collective-permute-start | bytes 368648 | tf_op jit(solution)/shard_map/ppermute | solution.py:247
  7.6 17.4 %collective-permute-start.3 = (bf16[2,8,3840]{2,1,0:T(8,128)(2,1)S(1)}, bf16[2,8,3840]{2,1,0:T(8,128)(2,1)S(1)}, u32[]{:S(2)}, u32[]{:S(2)}) collective-permute-start(bf16[2,8,3840]{2,1,0:T(8,128)(2,1)S(1)} %get-tuple-element.34), channel_id=1, source_target_pairs={{0,17},{1,16},{2,19},{3,18},{4,21},{5,20},{6,23},{7,22},{8,25},{9,... | collective-permute-start | bytes 368648 | tf_op jit(solution)/shard_map/ppermute | solution.py:247
  9.4 17.1 %collective-permute-start.4 = (bf16[2,8,3840]{2,1,0:T(8,128)(2,1)S(1)}, bf16[2,8,3840]{2,1,0:T(8,128)(2,1)S(1)}, u32[]{:S(2)}, u32[]{:S(2)}) collective-permute-start(bf16[2,8,3840]{2,1,0:T(8,128)(2,1)S(1)} %get-tuple-element.36), channel_id=1, source_target_pairs={{0,16},{1,17},{2,18},{3,19},{4,20},{5,21},{6,22},{7,23},{8,24},{9,... | collective-permute-start | bytes 368648 | tf_op jit(solution)/shard_map/ppermute | solution.py:247
  9.8 16.7 %collective-permute-start.5 = (bf16[2,8,3840]{2,1,0:T(8,128)(2,1)S(1)}, bf16[2,8,3840]{2,1,0:T(8,128)(2,1)S(1)}, u32[]{:S(2)}, u32[]{:S(2)}) collective-permute-start(bf16[2,8,3840]{2,1,0:T(8,128)(2,1)S(1)} %get-tuple-element.37), channel_id=1, source_target_pairs={{0,18},{1,19},{2,16},{3,17},{4,22},{5,23},{6,20},{7,21},{8,26},{9,... | collective-permute-start | bytes 368648 | tf_op jit(solution)/shard_map/ppermute | solution.py:247
  13.0 16.4 %collective-permute-start.6 = (bf16[2,8,3840]{2,1,0:T(8,128)(2,1)S(1)}, bf16[2,8,3840]{2,1,0:T(8,128)(2,1)S(1)}, u32[]{:S(2)}, u32[]{:S(2)}) collective-permute-start(bf16[2,8,3840]{2,1,0:T(8,128)(2,1)S(1)} %get-tuple-element.38), channel_id=1, source_target_pairs={{0,1},{1,0},{2,3},{3,2},{4,5},{5,4},{6,7},{7,6},{8,9},{9,8},{10,11... | collective-permute-start | bytes 368648 | tf_op jit(solution)/shard_map/ppermute | solution.py:247
  21.6 8.6 %collective-permute-start.7 = (bf16[2,8,3840]{2,1,0:T(8,128)(2,1)S(1)}, bf16[2,8,3840]{2,1,0:T(8,128)(2,1)S(1)}, u32[]{:S(2)}, u32[]{:S(2)}) collective-permute-start(bf16[2,8,3840]{2,1,0:T(8,128)(2,1)S(1)} %get-tuple-element.39), channel_id=1, source_target_pairs={{0,19},{1,18},{2,17},{3,16},{4,23},{5,22},{6,21},{7,20},{8,27},{9,... | collective-permute-start | bytes 368648 | tf_op jit(solution)/shard_map/ppermute | solution.py:247
  25.0 8.2 %collective-permute-start.8 = (bf16[2,8,3840]{2,1,0:T(8,128)(2,1)S(1)}, bf16[2,8,3840]{2,1,0:T(8,128)(2,1)S(1)}, u32[]{:S(2)}, u32[]{:S(2)}) collective-permute-start(bf16[2,8,3840]{2,1,0:T(8,128)(2,1)S(1)} %get-tuple-element.40), channel_id=1, source_target_pairs={{0,8},{1,9},{2,10},{3,11},{4,12},{5,13},{6,14},{7,15},{8,0},{9,1},... | collective-permute-start | bytes 368648 | tf_op jit(solution)/shard_map/ppermute | solution.py:247
  26.5 8.4 %collective-permute-start.9 = (bf16[2,8,3840]{2,1,0:T(8,128)(2,1)S(1)}, bf16[2,8,3840]{2,1,0:T(8,128)(2,1)S(1)}, u32[]{:S(2)}, u32[]{:S(2)}) collective-permute-start(bf16[2,8,3840]{2,1,0:T(8,128)(2,1)S(1)} %get-tuple-element.41), channel_id=1, source_target_pairs={{0,9},{1,8},{2,11},{3,10},{4,13},{5,12},{6,15},{7,14},{8,1},{9,0},... | collective-permute-start | bytes 368648 | tf_op jit(solution)/shard_map/ppermute | solution.py:247
  26.5 10.2 %collective-permute-start.10 = (bf16[2,8,3840]{2,1,0:T(8,128)(2,1)S(1)}, bf16[2,8,3840]{2,1,0:T(8,128)(2,1)S(1)}, u32[]{:S(2)}, u32[]{:S(2)}) collective-permute-start(bf16[2,8,3840]{2,1,0:T(8,128)(2,1)S(1)} %get-tuple-element.42), channel_id=1, source_target_pairs={{0,26},{1,27},{2,24},{3,25},{4,30},{5,31},{6,28},{7,29},{8,18},{9,... | collective-permute-start | bytes 368648 | tf_op jit(solution)/shard_map/ppermute | solution.py:247
  29.4 12.1 %collective-permute-start.12 = (bf16[2,8,3840]{2,1,0:T(8,128)(2,1)S(1)}, bf16[2,8,3840]{2,1,0:T(8,128)(2,1)S(1)}, u32[]{:S(2)}, u32[]{:S(2)}) collective-permute-start(bf16[2,8,3840]{2,1,0:T(8,128)(2,1)S(1)} %shard_map.40), channel_id=1, source_target_pairs={{0,4},{1,5},{2,6},{3,7},{4,0},{5,1},{6,2},{7,3},{8,12},{9,13},{10,... | collective-permute-start | bytes 368648 | tf_op jit(solution)/shard_map/ppermute | solution.py:247
  30.2 13.7 %collective-permute-start.11 = (bf16[2,8,3840]{2,1,0:T(8,128)(2,1)S(1)}, bf16[2,8,3840]{2,1,0:T(8,128)(2,1)S(1)}, u32[]{:S(2)}, u32[]{:S(2)}) collective-permute-start(bf16[2,8,3840]{2,1,0:T(8,128)(2,1)S(1)} %get-tuple-element.43), channel_id=1, source_target_pairs={{0,24},{1,25},{2,26},{3,27},{4,28},{5,29},{6,30},{7,31},{8,16},{9,... | collective-permute-start | bytes 368648 | tf_op jit(solution)/shard_map/ppermute | solution.py:247
  33.2 10.7 %collective-permute-start.13 = (bf16[2,8,3840]{2,1,0:T(8,128)(2,1)S(1)}, bf16[2,8,3840]{2,1,0:T(8,128)(2,1)S(1)}, u32[]{:S(2)}, u32[]{:S(2)}) collective-permute-start(bf16[2,8,3840]{2,1,0:T(8,128)(2,1)S(1)} %get-tuple-element.46), channel_id=1, source_target_pairs={{0,27},{1,26},{2,25},{3,24},{4,31},{5,30},{6,29},{7,28},{8,19},{9,... | collective-permute-start | bytes 368648 | tf_op jit(solution)/shard_map/ppermute | solution.py:247
  34.9 14.6 %collective-permute-start.14 = (bf16[2,8,3840]{2,1,0:T(8,128)(2,1)S(1)}, bf16[2,8,3840]{2,1,0:T(8,128)(2,1)S(1)}, u32[]{:S(2)}, u32[]{:S(2)}) collective-permute-start(bf16[2,8,3840]{2,1,0:T(8,128)(2,1)S(1)} %get-tuple-element.47), channel_id=1, source_target_pairs={{0,10},{1,11},{2,8},{3,9},{4,14},{5,15},{6,12},{7,13},{8,2},{9,3},... | collective-permute-start | bytes 368648 | tf_op jit(solution)/shard_map/ppermute | solution.py:247
  36.8 12.7 %collective-permute-start.15 = (bf16[2,8,3840]{2,1,0:T(8,128)(2,1)S(1)}, bf16[2,8,3840]{2,1,0:T(8,128)(2,1)S(1)}, u32[]{:S(2)}, u32[]{:S(2)}) collective-permute-start(bf16[2,8,3840]{2,1,0:T(8,128)(2,1)S(1)} %get-tuple-element.48), channel_id=1, source_target_pairs={{0,25},{1,24},{2,27},{3,26},{4,29},{5,28},{6,31},{7,30},{8,17},{9,... | collective-permute-start | bytes 368648 | tf_op jit(solution)/shard_map/ppermute | solution.py:247
  41.5 8.1 %collective-permute-start.16 = (bf16[2,8,3840]{2,1,0:T(8,128)(2,1)S(1)}, bf16[2,8,3840]{2,1,0:T(8,128)(2,1)S(1)}, u32[]{:S(2)}, u32[]{:S(2)}) collective-permute-start(bf16[2,8,3840]{2,1,0:T(8,128)(2,1)S(1)} %get-tuple-element.49), channel_id=1, source_target_pairs={{0,11},{1,10},{2,9},{3,8},{4,15},{5,14},{6,13},{7,12},{8,3},{9,2},... | collective-permute-start | bytes 368648 | tf_op jit(solution)/shard_map/ppermute | solution.py:247

commit v8 on v6

--- a/solution.py
+++ b/solution.py
@@ -16,7 +16,7 @@
 EARLY = (3, 2)
 JOINED = tuple(d for d in NEAR[1:] + FAR if d not in EARLY)
 LATE = 4
-ORDER = (17, 16, 18, 1, 19, 8, 9, 26, 24, 27, 10, 25, 11)
+ORDER = (17, 16, 18, 1, 19, 8, 9, 26, 24, 27, 10, 11, 25)
 WIDE, REST = 256, 64
 
 

time: 51.3 us -> 51.5 us (level)
  waiting for transfers between devices: 13 us -> 14 us
  starting transfers between devices: 32.7 us -> 31.8 us
    ppermute x17, waiting for transfers between devices: 13 us -> 14 us  [send(): lax.ppermute(piece, ('lat', 'lev'), [(i, i ^ distance) for i in range(cou...]
    ppermute x17, starting transfers between devices: 32.7 us -> 31.8 us  [send(): lax.ppermute(piece, ('lat', 'lev'), [(i, i ^ distance) for i in range(cou...]
where the time goes in v8:
time: 51.5 us; the launch traced here: 51.3 us
  starting transfers between devices  31.8 us (62%)
  waiting for transfers between devices  14 us (27%)
  Pallas kernels  5.02 us (10%)
    ppermute x17, starting transfers between devices, send(): lax.ppermute(piece, ('lat', 'lev'), [(i, i ^ distance) for i in range(cou...  31.8 us
    ppermute x17, waiting for transfers between devices, send(): lax.ppermute(piece, ('lat', 'lev'), [(i, i ^ distance) for i in range(cou...  14 us
    pallas_call x2, Pallas kernels, transform(): pl.pallas_call(functools.partial(transform_kernel, skip=len(rest), far=fa...  2.62 us
    pallas_call x1, Pallas kernels, load(): pl.pallas_call(load_kernel, in_specs=[HBM], out_specs=[VMEM] * 2, out_sha...  1.5 us
  transfers between devices with their start and end apart: 17, of which 5 were waited for; matrix products, arithmetic and copies ran while one was open for 1% of the time, Pallas kernels for 2%

profile of v8, /device:TPU:0, one launch (start us, length us, event | category | flops | bytes accessed | tf_op | source)
XLA Modules:
  0.0 51.3 jit_solution(2158002317475873504)
XLA Ops:
  0.0 1.5 %shard_map.37 = (bf16[12,256,256]{2,1,0:T(8,128)(2,1)S(1)}, bf16[12,64,256]{2,1,0:T(8,128)(2,1)S(1)}) custom-call(bf16[12,320,256]{2,1,0:T(8,128)(2,1)} %bitcast.5), custom_call_target="tpu_custom_call" | custom-call | flops 1000000000 | bytes 3932160 | tf_op jit(solution)/shard_map/pallas_call | solution.py:44
  1.5 0.0 copy-start.1
  1.5 0.8 %shard_map.38 = (bf16[13,8,3840]{2,1,0:T(8,128)(2,1)S(1)}, bf16[14,8,3840]{2,1,0:T(8,128)(2,1)S(1)}, bf16[8,3840]{1,0:T(8,128)(2,1)S(1)}, bf16[2,8,3840]{2,1,0:T(8,128)(2,1)S(1)}, bf16[2,8,3840]{2,1,0:T(8,128)(2,1)S(1)}) custom-call(s32[1,128]{1,0:T(1,128)S(1)} %bitcast.2, bf16[12,256,256]{2,1,0:T(8,128)(2,1)S(1)} %get-tuple-element.28.wide_ref, ...), custom_call_target="tpu_custom_call" | custom-call | tf_op jit(solution)/shard_map/pallas_call | solution.py:93
  2.3 0.5 collective-permute-start.2
  2.8 4.7 %collective-permute-start = (bf16[2,8,3840]{2,1,0:T(8,128)(2,1)S(1)}, bf16[2,8,3840]{2,1,0:T(8,128)(2,1)S(1)}, u32[]{:S(2)}, u32[]{:S(2)}) collective-permute-start(bf16[2,8,3840]{2,1,0:T(8,128)(2,1)S(1)} %get-tuple-element.30), channel_id=1, source_target_pairs={{0,3},{1,2},{2,1},{3,0},{4,7},{5,6},{6,5},{7,4},{8,11},{9,10},{10,... | collective-permute-start | bytes 368648 | tf_op jit(solution)/shard_map/ppermute | solution.py:242
  7.5 0.1 shard_map.39
  7.6 1.8 %collective-permute-start.3 = (bf16[2,8,3840]{2,1,0:T(8,128)(2,1)S(1)}, bf16[2,8,3840]{2,1,0:T(8,128)(2,1)S(1)}, u32[]{:S(2)}, u32[]{:S(2)}) collective-permute-start(bf16[2,8,3840]{2,1,0:T(8,128)(2,1)S(1)} %get-tuple-element.34), channel_id=1, source_target_pairs={{0,17},{1,16},{2,19},{3,18},{4,21},{5,20},{6,23},{7,22},{8,25},{9,... | collective-permute-start | bytes 368648 | tf_op jit(solution)/shard_map/ppermute | solution.py:242
  9.4 0.4 collective-permute-start.4
  9.8 3.2 %collective-permute-start.5 = (bf16[2,8,3840]{2,1,0:T(8,128)(2,1)S(1)}, bf16[2,8,3840]{2,1,0:T(8,128)(2,1)S(1)}, u32[]{:S(2)}, u32[]{:S(2)}) collective-permute-start(bf16[2,8,3840]{2,1,0:T(8,128)(2,1)S(1)} %get-tuple-element.37), channel_id=1, source_target_pairs={{0,18},{1,19},{2,16},{3,17},{4,22},{5,23},{6,20},{7,21},{8,26},{9,... | collective-permute-start | bytes 368648 | tf_op jit(solution)/shard_map/ppermute | solution.py:242
  13.0 0.0 collective-permute-done.refs_0_.refs_6_
  13.0 3.9 %collective-permute-start.6 = (bf16[2,8,3840]{2,1,0:T(8,128)(2,1)S(1)}, bf16[2,8,3840]{2,1,0:T(8,128)(2,1)S(1)}, u32[]{:S(2)}, u32[]{:S(2)}) collective-permute-start(bf16[2,8,3840]{2,1,0:T(8,128)(2,1)S(1)} %get-tuple-element.38), channel_id=1, source_target_pairs={{0,1},{1,0},{2,3},{3,2},{4,5},{5,4},{6,7},{7,6},{8,9},{9,8},{10,11... | collective-permute-start | bytes 368648 | tf_op jit(solution)/shard_map/ppermute | solution.py:242
  16.9 4.7 %collective-permute-done.1.refs_1_.refs_5_ = bf16[2,8,3840]{2,1,0:T(8,128)(2,1)S(1)} collective-permute-done((bf16[2,8,3840]{2,1,0:T(8,128)(2,1)S(1)}, bf16[2,8,3840]{2,1,0:T(8,128)(2,1)S(1)}, u32[]{:S(2)}, u32[]{:S(2)}) %collective-permute-start.1) | collective-permute-done | bytes 122912 | tf_op jit(solution)/shard_map/ppermute | solution.py:242
  21.6 3.4 %collective-permute-start.7 = (bf16[2,8,3840]{2,1,0:T(8,128)(2,1)S(1)}, bf16[2,8,3840]{2,1,0:T(8,128)(2,1)S(1)}, u32[]{:S(2)}, u32[]{:S(2)}) collective-permute-start(bf16[2,8,3840]{2,1,0:T(8,128)(2,1)S(1)} %get-tuple-element.39), channel_id=1, source_target_pairs={{0,19},{1,18},{2,17},{3,16},{4,23},{5,22},{6,21},{7,20},{8,27},{9,... | collective-permute-start | bytes 368648 | tf_op jit(solution)/shard_map/ppermute | solution.py:242
  25.0 0.0 collective-permute-done.3.refs_8_.refs_2_
  25.0 1.5 %collective-permute-start.8 = (bf16[2,8,3840]{2,1,0:T(8,128)(2,1)S(1)}, bf16[2,8,3840]{2,1,0:T(8,128)(2,1)S(1)}, u32[]{:S(2)}, u32[]{:S(2)}) collective-permute-start(bf16[2,8,3840]{2,1,0:T(8,128)(2,1)S(1)} %get-tuple-element.40), channel_id=1, source_target_pairs={{0,8},{1,9},{2,10},{3,11},{4,12},{5,13},{6,14},{7,15},{8,0},{9,1},... | collective-permute-start | bytes 368648 | tf_op jit(solution)/shard_map/ppermute | solution.py:242
  26.5 2.8 %collective-permute-start.10 = (bf16[2,8,3840]{2,1,0:T(8,128)(2,1)S(1)}, bf16[2,8,3840]{2,1,0:T(8,128)(2,1)S(1)}, u32[]{:S(2)}, u32[]{:S(2)}) collective-permute-start(bf16[2,8,3840]{2,1,0:T(8,128)(2,1)S(1)} %get-tuple-element.42), channel_id=1, source_target_pairs={{0,26},{1,27},{2,24},{3,25},{4,30},{5,31},{6,28},{7,29},{8,18},{9,... | collective-permute-start | bytes 368648 | tf_op jit(solution)/shard_map/ppermute | solution.py:242
  29.3 0.0 collective-permute-done.6.refs_4_.refs_5_
  29.4 0.1 collective-permute-start.12
  29.4 0.8 %collective-permute-done.7.refs_10_.refs_6_ = bf16[2,8,3840]{2,1,0:T(8,128)(2,1)S(1)} collective-permute-done((bf16[2,8,3840]{2,1,0:T(8,128)(2,1)S(1)}, bf16[2,8,3840]{2,1,0:T(8,128)(2,1)S(1)}, u32[]{:S(2)}, u32[]{:S(2)}) %collective-permute-start.7) | collective-permute-done | bytes 122912 | tf_op jit(solution)/shard_map/ppermute | solution.py:242
  30.2 2.9 %collective-permute-start.11 = (bf16[2,8,3840]{2,1,0:T(8,128)(2,1)S(1)}, bf16[2,8,3840]{2,1,0:T(8,128)(2,1)S(1)}, u32[]{:S(2)}, u32[]{:S(2)}) collective-permute-start(bf16[2,8,3840]{2,1,0:T(8,128)(2,1)S(1)} %get-tuple-element.43), channel_id=1, source_target_pairs={{0,24},{1,25},{2,26},{3,27},{4,28},{5,29},{6,30},{7,31},{8,16},{9,... | collective-permute-start | bytes 368648 | tf_op jit(solution)/shard_map/ppermute | solution.py:242
  33.1 0.1 collective-permute-done.8.refs_7_.refs_18_
  33.2 1.7 %collective-permute-start.13 = (bf16[2,8,3840]{2,1,0:T(8,128)(2,1)S(1)}, bf16[2,8,3840]{2,1,0:T(8,128)(2,1)S(1)}, u32[]{:S(2)}, u32[]{:S(2)}) collective-permute-start(bf16[2,8,3840]{2,1,0:T(8,128)(2,1)S(1)} %get-tuple-element.46), channel_id=1, source_target_pairs={{0,27},{1,26},{2,25},{3,24},{4,31},{5,30},{6,29},{7,28},{8,19},{9,... | collective-permute-start | bytes 368648 | tf_op jit(solution)/shard_map/ppermute | solution.py:242
  34.9 0.0 collective-permute-done.9.refs_8_.refs_19_
  34.9 0.0 collective-permute-start.14
  35.0 1.8 %collective-permute-done.10.refs_9_.refs_24_ = bf16[2,8,3840]{2,1,0:T(8,128)(2,1)S(1)} collective-permute-done((bf16[2,8,3840]{2,1,0:T(8,128)(2,1)S(1)}, bf16[2,8,3840]{2,1,0:T(8,128)(2,1)S(1)}, u32[]{:S(2)}, u32[]{:S(2)}) %collective-permute-start.10) | collective-permute-done | bytes 122912 | tf_op jit(solution)/shard_map/ppermute | solution.py:242
  36.8 2.5 %collective-permute-start.15 = (bf16[2,8,3840]{2,1,0:T(8,128)(2,1)S(1)}, bf16[2,8,3840]{2,1,0:T(8,128)(2,1)S(1)}, u32[]{:S(2)}, u32[]{:S(2)}) collective-permute-start(bf16[2,8,3840]{2,1,0:T(8,128)(2,1)S(1)} %get-tuple-element.48), channel_id=1, source_target_pairs={{0,11},{1,10},{2,9},{3,8},{4,15},{5,14},{6,13},{7,12},{8,3},{9,2},... | collective-permute-start | bytes 368648 | tf_op jit(solution)/shard_map/ppermute | solution.py:242
  39.2 0.0 collective-permute-done.12.refs_11_
  39.2 2.5 %collective-permute-start.16 = (bf16[2,8,3840]{2,1,0:T(8,128)(2,1)S(1)}, bf16[2,8,3840]{2,1,0:T(8,128)(2,1)S(1)}, u32[]{:S(2)}, u32[]{:S(2)}) collective-permute-start(bf16[2,8,3840]{2,1,0:T(8,128)(2,1)S(1)} %get-tuple-element.49), channel_id=1, source_target_pairs={{0,25},{1,24},{2,27},{3,26},{4,29},{5,28},{6,31},{7,30},{8,17},{9,... | collective-permute-start | bytes 368648 | tf_op jit(solution)/shard_map/ppermute | solution.py:242
  41.7 0.3 copy.5.refs_1_.refs_17_
  42.1 1.0 %shard_map.41.refs_26_ = f32[4,2,48,129]{3,2,1,0:T(8,128)S(1)} custom-call(s32[1,128]{1,0:T(1,128)S(1)} %bitcast.3, bf16[4,2,129,1280]{3,2,1,0:T(8,128)(2,1)S(1)} %copy.5.refs_1_.refs_17_, bf16[8,3840]{1,0:T(8,128)(2,1)S(1)} %get-tuple-element.50.refs_2_, bf16[14,8,3840]{2,1,0:T(8,128)(2,1)S(1)} %collective-permute-done.2.theirs_ref.refs_3_, ...), custom_call_target="tpu_custom_call" | custom-call | tf_op jit(solution)/shard_map/pallas_call | solution.py:218
  43.0 6.6 %collective-permute-done.14.refs_13_.refs_20_ = bf16[2,8,3840]{2,1,0:T(8,128)(2,1)S(1)} collective-permute-done((bf16[2,8,3840]{2,1,0:T(8,128)(2,1)S(1)}, bf16[2,8,3840]{2,1,0:T(8,128)(2,1)S(1)}, u32[]{:S(2)}, u32[]{:S(2)}) %collective-permute-start.14) | collective-permute-done | bytes 122912 | tf_op jit(solution)/shard_map/ppermute | solution.py:242
  49.7 1.7 %shard_map.42 = bf16[4,2,48,129]{3,2,1,0:T(8,128)(2,1)} custom-call(bf16[2,8,3840]{2,1,0:T(8,128)(2,1)S(1)} %collective-permute-done.refs_0_.refs_6_, bf16[2,8,3840]{2,1,0:T(8,128)(2,1)S(1)} %collective-permute-done.1.refs_1_.refs_5_, bf16[2,8,3840]{2,1,0:T(8,128)(2,1)S(1)} %collective-permute-done.3.refs_8_.refs_2_, ...), custom_call_target="tpu_custom_call" | custom-call | tf_op jit(solution)/shard_map/pallas_call | solution.py:218
  (13 shorter events, 0.0 us)
Async XLA Ops:
  0.0 1.5 %copy-start = (s32[128]{0:T(128)S(1)}, s32[128]{0:T(128)}, u32[]{:S(2)}) copy-start(s32[128]{0:T(128)} %param.4) | copy-start | bytes 1540
  1.5 40.2 %copy-start.1 = (bf16[4,2,129,1280]{3,1,2,0:T(2,128)(2,1)S(1)}, bf16[4,2,129,1280]{3,1,2,0:T(2,128)(2,1)}, u32[]{:S(2)}) copy-start(bf16[4,2,129,1280]{3,1,2,0:T(2,128)(2,1)} %param.5) | copy-start | bytes 7925764
  2.3 5.2 %collective-permute-start.2 = (bf16[14,8,3840]{2,1,0:T(8,128)(2,1)S(1)}, bf16[14,8,3840]{2,1,0:T(8,128)(2,1)S(1)}, u32[]{:S(2)}, u32[]{:S(2)}) collective-permute-start(bf16[14,8,3840]{2,1,0:T(8,128)(2,1)S(1)} %get-tuple-element.33), channel_id=1, source_target_pairs={{0,4},{1,5},{2,6},{3,7},{4,0},{5,1},{6,2},{7,3},{8,12},{9,13},{10,... | collective-permute-start | bytes 2580488 | tf_op jit(solution)/shard_map/ppermute | solution.py:242
  2.8 10.1 %collective-permute-start = (bf16[2,8,3840]{2,1,0:T(8,128)(2,1)S(1)}, bf16[2,8,3840]{2,1,0:T(8,128)(2,1)S(1)}, u32[]{:S(2)}, u32[]{:S(2)}) collective-permute-start(bf16[2,8,3840]{2,1,0:T(8,128)(2,1)S(1)} %get-tuple-element.30), channel_id=1, source_target_pairs={{0,3},{1,2},{2,1},{3,0},{4,7},{5,6},{6,5},{7,4},{8,11},{9,10},{10,... | collective-permute-start | bytes 368648 | tf_op jit(solution)/shard_map/ppermute | solution.py:242
  7.5 14.1 %collective-permute-start.1 = (bf16[2,8,3840]{2,1,0:T(8,128)(2,1)S(1)}, bf16[2,8,3840]{2,1,0:T(8,128)(2,1)S(1)}, u32[]{:S(2)}, u32[]{:S(2)}) collective-permute-start(bf16[2,8,3840]{2,1,0:T(8,128)(2,1)S(1)} %get-tuple-element.31), channel_id=1, source_target_pairs={{0,2},{1,3},{2,0},{3,1},{4,6},{5,7},{6,4},{7,5},{8,10},{9,11},{10,... | collective-permute-start | bytes 368648 | tf_op jit(solution)/shard_map/ppermute | solution.py:242
  7.6 17.4 %collective-permute-start.3 = (bf16[2,8,3840]{2,1,0:T(8,128)(2,1)S(1)}, bf16[2,8,3840]{2,1,0:T(8,128)(2,1)S(1)}, u32[]{:S(2)}, u32[]{:S(2)}) collective-permute-start(bf16[2,8,3840]{2,1,0:T(8,128)(2,1)S(1)} %get-tuple-element.34), channel_id=1, source_target_pairs={{0,17},{1,16},{2,19},{3,18},{4,21},{5,20},{6,23},{7,22},{8,25},{9,... | collective-permute-start | bytes 368648 | tf_op jit(solution)/shard_map/ppermute | solution.py:242
  9.4 17.1 %collective-permute-start.4 = (bf16[2,8,3840]{2,1,0:T(8,128)(2,1)S(1)}, bf16[2,8,3840]{2,1,0:T(8,128)(2,1)S(1)}, u32[]{:S(2)}, u32[]{:S(2)}) collective-permute-start(bf16[2,8,3840]{2,1,0:T(8,128)(2,1)S(1)} %get-tuple-element.36), channel_id=1, source_target_pairs={{0,16},{1,17},{2,18},{3,19},{4,20},{5,21},{6,22},{7,23},{8,24},{9,... | collective-permute-start | bytes 368648 | tf_op jit(solution)/shard_map/ppermute | solution.py:242
  9.8 16.7 %collective-permute-start.5 = (bf16[2,8,3840]{2,1,0:T(8,128)(2,1)S(1)}, bf16[2,8,3840]{2,1,0:T(8,128)(2,1)S(1)}, u32[]{:S(2)}, u32[]{:S(2)}) collective-permute-start(bf16[2,8,3840]{2,1,0:T(8,128)(2,1)S(1)} %get-tuple-element.37), channel_id=1, source_target_pairs={{0,18},{1,19},{2,16},{3,17},{4,22},{5,23},{6,20},{7,21},{8,26},{9,... | collective-permute-start | bytes 368648 | tf_op jit(solution)/shard_map/ppermute | solution.py:242
  13.0 16.4 %collective-permute-start.6 = (bf16[2,8,3840]{2,1,0:T(8,128)(2,1)S(1)}, bf16[2,8,3840]{2,1,0:T(8,128)(2,1)S(1)}, u32[]{:S(2)}, u32[]{:S(2)}) collective-permute-start(bf16[2,8,3840]{2,1,0:T(8,128)(2,1)S(1)} %get-tuple-element.38), channel_id=1, source_target_pairs={{0,1},{1,0},{2,3},{3,2},{4,5},{5,4},{6,7},{7,6},{8,9},{9,8},{10,11... | collective-permute-start | bytes 368648 | tf_op jit(solution)/shard_map/ppermute | solution.py:242
  21.6 8.6 %collective-permute-start.7 = (bf16[2,8,3840]{2,1,0:T(8,128)(2,1)S(1)}, bf16[2,8,3840]{2,1,0:T(8,128)(2,1)S(1)}, u32[]{:S(2)}, u32[]{:S(2)}) collective-permute-start(bf16[2,8,3840]{2,1,0:T(8,128)(2,1)S(1)} %get-tuple-element.39), channel_id=1, source_target_pairs={{0,19},{1,18},{2,17},{3,16},{4,23},{5,22},{6,21},{7,20},{8,27},{9,... | collective-permute-start | bytes 368648 | tf_op jit(solution)/shard_map/ppermute | solution.py:242
  25.0 8.2 %collective-permute-start.8 = (bf16[2,8,3840]{2,1,0:T(8,128)(2,1)S(1)}, bf16[2,8,3840]{2,1,0:T(8,128)(2,1)S(1)}, u32[]{:S(2)}, u32[]{:S(2)}) collective-permute-start(bf16[2,8,3840]{2,1,0:T(8,128)(2,1)S(1)} %get-tuple-element.40), channel_id=1, source_target_pairs={{0,8},{1,9},{2,10},{3,11},{4,12},{5,13},{6,14},{7,15},{8,0},{9,1},... | collective-permute-start | bytes 368648 | tf_op jit(solution)/shard_map/ppermute | solution.py:242
  26.5 8.4 %collective-permute-start.9 = (bf16[2,8,3840]{2,1,0:T(8,128)(2,1)S(1)}, bf16[2,8,3840]{2,1,0:T(8,128)(2,1)S(1)}, u32[]{:S(2)}, u32[]{:S(2)}) collective-permute-start(bf16[2,8,3840]{2,1,0:T(8,128)(2,1)S(1)} %get-tuple-element.41), channel_id=1, source_target_pairs={{0,9},{1,8},{2,11},{3,10},{4,13},{5,12},{6,15},{7,14},{8,1},{9,0},... | collective-permute-start | bytes 368648 | tf_op jit(solution)/shard_map/ppermute | solution.py:242
  26.5 10.2 %collective-permute-start.10 = (bf16[2,8,3840]{2,1,0:T(8,128)(2,1)S(1)}, bf16[2,8,3840]{2,1,0:T(8,128)(2,1)S(1)}, u32[]{:S(2)}, u32[]{:S(2)}) collective-permute-start(bf16[2,8,3840]{2,1,0:T(8,128)(2,1)S(1)} %get-tuple-element.42), channel_id=1, source_target_pairs={{0,26},{1,27},{2,24},{3,25},{4,30},{5,31},{6,28},{7,29},{8,18},{9,... | collective-permute-start | bytes 368648 | tf_op jit(solution)/shard_map/ppermute | solution.py:242
  29.4 9.9 %collective-permute-start.12 = (bf16[2,8,3840]{2,1,0:T(8,128)(2,1)S(1)}, bf16[2,8,3840]{2,1,0:T(8,128)(2,1)S(1)}, u32[]{:S(2)}, u32[]{:S(2)}) collective-permute-start(bf16[2,8,3840]{2,1,0:T(8,128)(2,1)S(1)} %shard_map.40), channel_id=1, source_target_pairs={{0,4},{1,5},{2,6},{3,7},{4,0},{5,1},{6,2},{7,3},{8,12},{9,13},{10,... | collective-permute-start | bytes 368648 | tf_op jit(solution)/shard_map/ppermute | solution.py:242
  30.2 12.8 %collective-permute-start.11 = (bf16[2,8,3840]{2,1,0:T(8,128)(2,1)S(1)}, bf16[2,8,3840]{2,1,0:T(8,128)(2,1)S(1)}, u32[]{:S(2)}, u32[]{:S(2)}) collective-permute-start(bf16[2,8,3840]{2,1,0:T(8,128)(2,1)S(1)} %get-tuple-element.43), channel_id=1, source_target_pairs={{0,24},{1,25},{2,26},{3,27},{4,28},{5,29},{6,30},{7,31},{8,16},{9,... | collective-permute-start | bytes 368648 | tf_op jit(solution)/shard_map/ppermute | solution.py:242
  33.2 9.8 %collective-permute-start.13 = (bf16[2,8,3840]{2,1,0:T(8,128)(2,1)S(1)}, bf16[2,8,3840]{2,1,0:T(8,128)(2,1)S(1)}, u32[]{:S(2)}, u32[]{:S(2)}) collective-permute-start(bf16[2,8,3840]{2,1,0:T(8,128)(2,1)S(1)} %get-tuple-element.46), channel_id=1, source_target_pairs={{0,27},{1,26},{2,25},{3,24},{4,31},{5,30},{6,29},{7,28},{8,19},{9,... | collective-permute-start | bytes 368648 | tf_op jit(solution)/shard_map/ppermute | solution.py:242
  34.9 14.7 %collective-permute-start.14 = (bf16[2,8,3840]{2,1,0:T(8,128)(2,1)S(1)}, bf16[2,8,3840]{2,1,0:T(8,128)(2,1)S(1)}, u32[]{:S(2)}, u32[]{:S(2)}) collective-permute-start(bf16[2,8,3840]{2,1,0:T(8,128)(2,1)S(1)} %get-tuple-element.47), channel_id=1, source_target_pairs={{0,10},{1,11},{2,8},{3,9},{4,14},{5,15},{6,12},{7,13},{8,2},{9,3},... | collective-permute-start | bytes 368648 | tf_op jit(solution)/shard_map/ppermute | solution.py:242
  36.8 12.9 %collective-permute-start.15 = (bf16[2,8,3840]{2,1,0:T(8,128)(2,1)S(1)}, bf16[2,8,3840]{2,1,0:T(8,128)(2,1)S(1)}, u32[]{:S(2)}, u32[]{:S(2)}) collective-permute-start(bf16[2,8,3840]{2,1,0:T(8,128)(2,1)S(1)} %get-tuple-element.48), channel_id=1, source_target_pairs={{0,11},{1,10},{2,9},{3,8},{4,15},{5,14},{6,13},{7,12},{8,3},{9,2},... | collective-permute-start | bytes 368648 | tf_op jit(solution)/shard_map/ppermute | solution.py:242
  39.2 10.4 %collective-permute-start.16 = (bf16[2,8,3840]{2,1,0:T(8,128)(2,1)S(1)}, bf16[2,8,3840]{2,1,0:T(8,128)(2,1)S(1)}, u32[]{:S(2)}, u32[]{:S(2)}) collective-permute-start(bf16[2,8,3840]{2,1,0:T(8,128)(2,1)S(1)} %get-tuple-element.49), channel_id=1, source_target_pairs={{0,25},{1,24},{2,27},{3,26},{4,29},{5,28},{6,31},{7,30},{8,17},{9,... | collective-permute-start | bytes 368648 | tf_op jit(solution)/shard_map/ppermute | solution.py:242
